TPU v7x, 32 devices: a whole 2x2x4 slice. The times are simulated.
32 devices in a mesh: pas: 8 (over z, y), head: 4 (over x, core).
Axes of the slice: x: 2, y: 2, z: 4, core: 2. Of those that a mesh axis runs over, the one named last changes fastest.
Arguments:
- queries: bfloat16 [1024, 4096], P('pas', 'head'), may hold values from -144 to 144
- encoded: bfloat16 [8192, 4096], P('pas'), may hold values from -6 to 6
- key_weight: bfloat16 [4096, 4096], P(None, 'head'), may hold values from -0.09375 to 0.09375
- value_weight: bfloat16 [4096, 4096], P(None, 'head'), may hold values from -0.09375 to 0.09375
- out_weight: bfloat16 [4096, 4096], P('head'), may hold values from -0.75 to 0.75
- out_grad: bfloat16 [1024, 4096], P('pas', 'head'), may hold values from -0.75 to 0.75
- slot_of: int32 [32], replicated, may hold values from 0 to 31, as said below
- passage_lists: int32 [8, 16], replicated, may hold values from 0 to 31, as said below
- list_counts: int32 [8], replicated, may hold values from 12 to 16, as said below
Outputs:
- output: bfloat16 [1024, 4096], P('pas', 'head')
- query_grad: bfloat16 [1024, 4096], P('pas', 'head')
- key_grad: bfloat16 [8192, 4096], P('pas', 'head')
- value_grad: bfloat16 [8192, 4096], P('pas', 'head')
Inputs may be any that keep to these rules, and one draw needn't show every extreme that they name: slot_of is a permutation of the pool: passage p is stored at slot slot_of[p], on index slot_of[p] // 4 of pas. `passage_lists`: the entries of one row are distinct passage ids. Among the first list_counts[q] entries of row q, at most 2 are stored on one index of pas, and some row has exactly 2 on some index. Entries past list_counts[q] are not read. `list_counts`: some question reads all 16 entries.
All inputs are finite; a program needn't handle non-finite values.
Results may differ from a plain program's by a relative error of at most 0.0055.
The roundings to bfloat16 on the way count: a program that leaves them out, or rounds other values in their place, can miss the bound.
Values may be sent and summed in bfloat16 or wider, within the bound.
No kernel may reach another device: no remote copies, remote signals or barrier semaphores. Data moves between devices by JAX's collectives and lax.ppermute only.
A program may use at most 192 MiB of HBM per device.

v0:
```python
import jax
import jax.numpy as jnp
from jax import lax
from jax.sharding import PartitionSpec as P

HEAD_DIM = 64
PLEN = 256
CAP = 2


NEG_LARGE = -1e30


def head_attention(query_head, kv_head, grad_head, key_valid):
    score_scale = HEAD_DIM ** (-0.5)
    key_head = kv_head[:, :HEAD_DIM]
    value_head = kv_head[:, HEAD_DIM:]
    scores = (
        lax.dot_general(
            query_head, key_head, (((1,), (1,)), ((), ())), preferred_element_type=jnp.float32
        )
        * score_scale
    )
    scores = jnp.where(key_valid[None, :], scores, NEG_LARGE)
    row_top = jnp.max(scores, axis=1, keepdims=True)
    weights = jnp.where(key_valid[None, :], jnp.exp(scores - row_top), 0.0)
    row_total = jnp.sum(weights, axis=1, keepdims=True)
    context = (
        jnp.dot(weights.astype(jnp.bfloat16), value_head, preferred_element_type=jnp.float32)
        / row_total
    ).astype(jnp.bfloat16)
    grad_dot = jnp.sum(
        grad_head.astype(jnp.float32) * context.astype(jnp.float32), axis=1, keepdims=True
    )
    softmax_rows = weights / row_total
    value_term = lax.dot_general(
        softmax_rows.astype(jnp.bfloat16),
        grad_head,
        (((0,), (0,)), ((), ())),
        preferred_element_type=jnp.float32,
    ).astype(jnp.bfloat16)
    dprob = lax.dot_general(
        grad_head, value_head, (((1,), (1,)), ((), ())), preferred_element_type=jnp.float32
    )
    dscore = (softmax_rows * (dprob - grad_dot)).astype(jnp.bfloat16)
    query_term = (
        jnp.dot(dscore, key_head, preferred_element_type=jnp.float32) * score_scale
    ).astype(jnp.bfloat16)
    key_term = (
        lax.dot_general(
            dscore, query_head, (((0,), (0,)), ((), ())), preferred_element_type=jnp.float32
        )
        * score_scale
    ).astype(jnp.bfloat16)
    return (context, query_term, jnp.concatenate([key_term, value_term], axis=1))


def body(
    queries,
    encoded,
    key_weight,
    value_weight,
    out_weight,
    out_grad,
    slot_of,
    passage_lists,
    list_counts,
):
    head_width = key_weight.shape[1]
    heads_dev = head_width // HEAD_DIM
    tok_count = queries.shape[0]
    pas_dev = encoded.shape[0] // PLEN
    n_pas = lax.axis_size("pas")
    my_index = lax.axis_index("pas")
    pool_size = slot_of.shape[0]
    list_len = passage_lists.shape[1]
    n_questions = passage_lists.shape[0]
    key_part = jnp.dot(encoded, key_weight, preferred_element_type=jnp.float32).astype(jnp.bfloat16)
    value_part = jnp.dot(encoded, value_weight, preferred_element_type=jnp.float32).astype(
        jnp.bfloat16
    )
    kv_local = jnp.concatenate(
        [
            key_part.reshape(pas_dev, PLEN, heads_dev, HEAD_DIM),
            value_part.reshape(pas_dev, PLEN, heads_dev, HEAD_DIM),
        ],
        axis=3,
    )
    context_grad = lax.dot_general(
        lax.all_gather(out_grad, "head", axis=1, tiled=True),
        out_weight,
        (((1,), (1,)), ((), ())),
        preferred_element_type=jnp.float32,
    ).astype(jnp.bfloat16)
    grad_tok = context_grad.reshape(tok_count, heads_dev, HEAD_DIM)
    query_tok = queries.reshape(tok_count, heads_dev, HEAD_DIM)
    matches = passage_lists[:, :, None] == jnp.arange(pool_size, dtype=jnp.int32)[None, None, :]
    global_slot = jnp.sum(jnp.where(matches, slot_of[None, None, :], 0), axis=2)
    is_live = jnp.arange(list_len, dtype=jnp.int32)[None, :] < list_counts[:, None]
    owner_of = global_slot // pas_dev
    local_of = global_slot % pas_dev
    list_range = jnp.arange(list_len, dtype=jnp.int32)
    earlier = list_range[None, :, None] > list_range[None, None, :]
    same_owner = (owner_of[:, :, None] == owner_of[:, None, :]) & is_live[:, None, :] & earlier
    rank_of = jnp.sum(same_owner.astype(jnp.int32), axis=2)
    cap_range = jnp.arange(CAP, dtype=jnp.int32)
    at_mine = is_live & (owner_of == my_index)
    selector = (
        at_mine[:, :, None, None]
        & (rank_of[:, :, None, None] == cap_range[None, None, :, None])
        & (local_of[:, :, None, None] == jnp.arange(pas_dev, dtype=jnp.int32)[None, None, None, :])
    )
    selector = jnp.sum(selector.astype(jnp.float32), axis=1).astype(jnp.bfloat16)
    block_size = PLEN * heads_dev * 2 * HEAD_DIM
    outgoing = jnp.einsum(
        "rcl,lx->rcx",
        selector,
        kv_local.reshape(pas_dev, block_size),
        preferred_element_type=jnp.float32,
    ).astype(jnp.bfloat16)
    outgoing = outgoing.reshape(n_questions, CAP * PLEN, heads_dev, 2 * HEAD_DIM)
    incoming = lax.all_to_all(outgoing, "pas", split_axis=0, concat_axis=0, tiled=True)
    slot_live = (
        is_live[:, :, None, None]
        & (owner_of[:, :, None, None] == jnp.arange(n_pas, dtype=jnp.int32)[None, None, :, None])
        & (rank_of[:, :, None, None] == cap_range[None, None, None, :])
    )
    slot_live = jnp.any(slot_live, axis=1)
    my_slots = lax.dynamic_index_in_dim(slot_live, my_index, 0, keepdims=False)
    key_valid = jnp.repeat(my_slots.reshape(n_pas * CAP), PLEN)
    key_count = n_pas * CAP * PLEN
    kv_flat = incoming.reshape(key_count, heads_dev, 2 * HEAD_DIM)

    def reader_head(head_index, loop_state):
        context_all, query_all, kv_grad_all = loop_state
        query_head = lax.dynamic_index_in_dim(query_tok, head_index, 1, keepdims=False)
        kv_head = lax.dynamic_index_in_dim(kv_flat, head_index, 1, keepdims=False)
        grad_head = lax.dynamic_index_in_dim(grad_tok, head_index, 1, keepdims=False)
        context_head, query_head_grad, kv_head_grad = head_attention(
            query_head, kv_head, grad_head, key_valid
        )
        context_all = lax.dynamic_update_index_in_dim(context_all, context_head, head_index, 1)
        query_all = lax.dynamic_update_index_in_dim(query_all, query_head_grad, head_index, 1)
        kv_grad_all = lax.dynamic_update_index_in_dim(kv_grad_all, kv_head_grad, head_index, 1)
        return (context_all, query_all, kv_grad_all)

    start_state = (
        jnp.zeros((tok_count, heads_dev, HEAD_DIM), jnp.bfloat16),
        jnp.zeros((tok_count, heads_dev, HEAD_DIM), jnp.bfloat16),
        jnp.zeros((key_count, heads_dev, 2 * HEAD_DIM), jnp.bfloat16),
    )
    context, query_done, kv_grad_all = lax.fori_loop(0, heads_dev, reader_head, start_state)
    query_grad = query_done.reshape(tok_count, head_width)
    returned = lax.all_to_all(
        kv_grad_all.reshape(n_pas, CAP * PLEN, heads_dev, 2 * HEAD_DIM),
        "pas",
        split_axis=0,
        concat_axis=0,
        tiled=True,
    )
    own_grad = jnp.einsum(
        "rcl,rcx->lx",
        selector,
        returned.reshape(n_pas, CAP, block_size),
        preferred_element_type=jnp.float32,
    ).astype(jnp.bfloat16)
    own_grad = own_grad.reshape(pas_dev * PLEN, heads_dev, 2 * HEAD_DIM)
    key_grad = own_grad[:, :, :HEAD_DIM].reshape(pas_dev * PLEN, head_width)
    value_grad = own_grad[:, :, HEAD_DIM:].reshape(pas_dev * PLEN, head_width)
    projected = jnp.dot(
        context.reshape(tok_count, head_width), out_weight, preferred_element_type=jnp.float32
    )
    output = lax.psum_scatter(projected, "head", scatter_dimension=1, tiled=True).astype(
        jnp.bfloat16
    )
    return (output, query_grad, key_grad, value_grad)


def solution(mesh):
    in_specs = (
        P("pas", "head"),
        P("pas", None),
        P(None, "head"),
        P(None, "head"),
        P("head", None),
        P("pas", "head"),
        P(),
        P(),
        P(),
    )
    out_specs = (P("pas", "head"), P("pas", "head"), P("pas", "head"), P("pas", "head"))
    return jax.shard_map(body, mesh=mesh, in_specs=in_specs, out_specs=out_specs, check_vma=False)
```

profile of v0, /device:TPU:0, one launch (start us, length us, event | category | flops | bytes accessed | tf_op | source)
XLA Modules:
  0.0 1109.5 jit_solution(1194739259539999836)
XLA Ops:
  9.3 14.6 %convolution_convert_fusion.3 = bf16[1024,1024]{1,0:T(8,128)(2,1)} fusion(bf16[1024,4096]{1,0:T(8,128)(2,1)} %param.12, bf16[4096,1024]{1,0:T(8,128)(2,1)} %param.13), kind=kOutput, calls=%fused_computation.51 | convolution fusion | flops 8590983168 | bytes 18874368 | tf_op jit(solution)/shard_map/dot_general | solution.py:78
  23.9 2.9 copy.31
  26.8 2.8 reshape.235
  29.5 14.6 %convolution_convert_fusion.2 = bf16[1024,1024]{1,0:T(8,128)(2,1)} fusion(bf16[1024,4096]{1,0:T(8,128)(2,1)} %param.12, bf16[4096,1024]{1,0:T(8,128)(2,1)} %param.14), kind=kOutput, calls=%fused_computation.50 | convolution fusion | flops 8590983168 | bytes 18874368 | tf_op jit(solution)/shard_map/dot_general | solution.py:79
  44.1 2.9 copy.32
  47.0 2.8 reshape.236
  49.8 6.9 pad_maximum_fusion
  56.7 6.1 copy.33
  62.8 5.7 reshape.248
  68.6 6.8 convolution_convert_fusion.1
  75.4 53.6 %copy.34 = bf16[8,2,524288]{2,1,0:T(2,128)(2,1)} copy(bf16[8,2,524288]{2,0,1:T(8,128)(2,1)S(1)} %convolution_convert_fusion.1) | data formatting | bytes 33554432 | tf_op jit(solution)/shard_map/convert_element_type | solution.py:120
  129.0 18.2 %reshape.238 = bf16[8,512,16,128]{3,2,1,0:T(8,128)(2,1)} reshape(bf16[8,2,524288]{2,1,0:T(2,128)(2,1)} %copy.34) | data formatting | bytes 33554432 | tf_op jit(solution)/shard_map/reshape | solution.py:121
  147.2 7.4 all-to-all-start
  156.1 19.0 %all-gather.2.cloned.1.call-done = bf16[128,4096]{1,0:T(8,128)(2,1)} async-done(((bf16[128,1024]{1,0:T(8,128)(2,1)}), bf16[128,4096]{1,0:T(8,128)(2,1)}) %all-gather.2.cloned.1.call-update) | async-done | bytes 1048592 | tf_op jit(solution)/shard_map/all_gather | solution.py:90
  175.1 6.6 convolution_convert_fusion.4
  181.9 335.7 %all-to-all-done = bf16[8,512,16,128]{3,2,1,0:T(8,128)(2,1)} async-done(((bf16[8,512,16,128]{3,2,1,0:T(8,128)(2,1)}), bf16[8,512,16,128]{3,2,1,0:T(8,128)(2,1)}, u32[]{:S(2)}, u32[]{:S(2)}) %all-to-all-start) | async-done | bytes 16777248 | tf_op jit(solution)/shard_map/all_to_all | solution.py:122
  517.6 15.1 %copy.37 = bf16[4096,16,128]{2,0,1:T(8,128)(2,1)} copy(bf16[4096,16,128]{2,1,0:T(8,128)(2,1)} %bitcast.1) | data formatting | bytes 33554432
  532.7 116.4 %while.18 = (s32[]{:T(128)}, bf16[128,16,64]{0,2,1:T(8,128)(2,1)S(1)}, bf16[128,16,64]{0,2,1:T(8,128)(2,1)S(1)}, bf16[4096,16,128]{0,2,1:T(8,128)(2,1)}, bf16[12...) while((s32[]{:T(128)}, ...), condition=%wide.region_8.9_spmd.clone, body=%wide.region_4.8_spmd.clone.sunk | while | flops 415563392 | bytes 23254680 | solution.py:152
  532.8 1.3 dynamic-slice_bitcast_fusion.2
  540.0 1.3 dynamic-slice_bitcast_fusion.2
  547.3 1.3 dynamic-slice_bitcast_fusion.2
  554.6 1.3 dynamic-slice_bitcast_fusion.2
  561.9 1.3 dynamic-slice_bitcast_fusion.2
  569.1 1.3 dynamic-slice_bitcast_fusion.2
  576.4 1.3 dynamic-slice_bitcast_fusion.2
  583.7 1.3 dynamic-slice_bitcast_fusion.2
  590.9 1.3 dynamic-slice_bitcast_fusion.2
  598.2 1.3 dynamic-slice_bitcast_fusion.2
  605.5 1.3 dynamic-slice_bitcast_fusion.2
  612.8 1.3 dynamic-slice_bitcast_fusion.2
  620.0 1.3 dynamic-slice_bitcast_fusion.2
  627.3 1.3 dynamic-slice_bitcast_fusion.2
  634.6 1.3 dynamic-slice_bitcast_fusion.2
  641.9 1.3 dynamic-slice_bitcast_fusion.2
  649.0 22.3 %copy.45 = bf16[4096,16,128]{2,1,0:T(8,128)(2,1)} copy(bf16[4096,16,128]{0,2,1:T(8,128)(2,1)} %get-tuple-element.147) | data formatting | bytes 33554432 | tf_op jit(solution)/shard_map/reshape | solution.py:155
  671.3 5.8 all-to-all-start.1
  677.1 6.0 fusion.46
  684.0 32.0 %reduce-scatter.2.cloned.1.call-done = f32[128,1024]{1,0:T(8,128)} async-done(((f32[128,4096]{1,0:T(8,128)}), f32[128,1024]{1,0:T(8,128)}) %reduce-scatter.2.cloned.1.call-update) | async-done | bytes 524304 | tf_op jit(solution)/shard_map/reduce_scatter | solution.py:173
  716.0 1.8 convert_element_type.97
  717.8 321.3 %all-to-all-done.1 = bf16[8,512,16,128]{3,2,1,0:T(8,128)(2,1)} async-done(((bf16[8,512,16,128]{3,2,1,0:T(8,128)(2,1)}), bf16[8,512,16,128]{3,2,1,0:T(8,128)(2,1)}, u32[]{:S(2)}, u32[]{:S(2)}) %all-to-all-start.1) | async-done | bytes 16777248 | tf_op jit(solution)/shard_map/all_to_all | solution.py:154
  1039.1 15.2 %reshape.244 = bf16[8,2,524288]{2,1,0:T(2,128)(2,1)} reshape(bf16[8,512,16,128]{3,2,1,0:T(8,128)(2,1)} %all-to-all-done.1) | data formatting | bytes 33554432 | tf_op jit(solution)/shard_map/reshape | solution.py:164
  1054.3 18.0 %fusion.37 = bf16[4,524288]{1,0:T(4,128)(2,1)} fusion(bf16[8,2,524288]{2,1,0:T(2,128)(2,1)} %reshape.244, bf16[8,2,4]{0,2,1:T(4,128)(2,1)S(1)} %convert_reduce_fusion.1), kind=kOutput, calls=%fused_computation.47 | convolution fusion | flops 69206016 | bytes 20971648 | tf_op jit(solution)/shard_map/rcl,rcx->lx/dot_general | solution.py:161
  1072.2 8.3 reshape.245
  1080.5 7.8 fusion.45
  1088.3 4.5 copy.47
  1092.8 2.6 copy.44
  1095.4 4.5 copy.46
  1099.8 2.6 copy.43
  (202 shorter events, 99.6 us)
Async XLA Ops:
  147.2 8.8 copy-start
  147.2 370.4 %all-to-all-start = ((bf16[8,512,16,128]{3,2,1,0:T(8,128)(2,1)}), bf16[8,512,16,128]{3,2,1,0:T(8,128)(2,1)}, u32[]{:S(2)}, u32[]{:S(2)}) async-start(bf16[8,512,16,128]{3,2,1,0:T(8,128)(2,1)} %reshape.238), calls=%async_computation | async-start | bytes 33554432 | tf_op jit(solution)/shard_map/all_to_all | solution.py:122
  154.6 20.5 %all-gather.2.cloned.1.call-start = ((), (), s32[]{:S(2)}) async-start(), calls=%async_computation.3 | async-start | bytes 1310720 | tf_op jit(solution)/shard_map/all_gather | solution.py:90
  671.3 367.8 %all-to-all-start.1 = ((bf16[8,512,16,128]{3,2,1,0:T(8,128)(2,1)}), bf16[8,512,16,128]{3,2,1,0:T(8,128)(2,1)}, u32[]{:S(2)}, u32[]{:S(2)}) async-start(bf16[8,512,16,128]{3,2,1,0:T(8,128)(2,1)} %bitcast.80), calls=%async_computation.2 | async-start | bytes 33554432 | tf_op jit(solution)/shard_map/all_to_all | solution.py:154
  677.1 38.9 %reduce-scatter.2.cloned.1.call-start = ((), (), s32[]{:S(2)}) async-start(), calls=%async_computation.4 | async-start | bytes 2621440 | tf_op jit(solution)/shard_map/reduce_scatter | solution.py:173
Sparse Core Ops, SparseCore 0:
  157.0 18.0 all-gather.1
  683.3 32.6 reduce-scatter.1
where the time goes:
time: 1120 us; the launch traced here: 1110 us
  waiting for transfers between devices  709 us (63%)
  local copies, waits for them, and re-layouts  201 us (18%)
  matrix products  134 us (12%)
  other arithmetic  37.4 us (3%)
  between operations  14.4 us (1%)
  starting transfers between devices  13.3 us (1%)
    all_to_all x1, waiting for transfers between devices, body(): lax.all_to_all(outgoing, 'pas', split_axis=0, concat_axis=0, tiled=True)  336 us
    all_to_all x1, waiting for transfers between devices, body(): lax.all_to_all(kv_grad_all.reshape(n_pas, CAP * PLEN, heads_dev, 2 * HEAD...  321 us
    convert_element_type x1, local copies, waits for them, and re-layouts, body(): outgoing = jnp.einsum('rcl,lx->rcx', selector, kv_local.reshape(pas_dev,...  53.6 us
    reduce_scatter x1, waiting for transfers between devices, body(): lax.psum_scatter(projected, 'head', scatter_dimension=1, tiled=True)  32 us
    unnamed x9, local copies, waits for them, and re-layouts  30.2 us
  transfers between devices with their start and end apart: 4, of which 4 were waited for; matrix products, arithmetic and copies ran while one was open for 1% of the time, Pallas kernels for 0%

commit v1 on v0

v1 whole, which is shorter than its diff:
```python
import functools

import jax
import jax.numpy as jnp
from jax import lax
from jax.experimental import pallas as pl
from jax.experimental.pallas import tpu as pltpu
from jax.sharding import PartitionSpec as P

HEAD_DIM = 64
PLEN = 256
INNER = 4
LANES = 128
NEG_LARGE = -1e30
SCALE = HEAD_DIM ** (-0.5)

BF16 = jnp.bfloat16
F32 = jnp.float32

VMEM_LIMIT = 56 * 1024 * 1024


def params(semantics=None):
    return pltpu.CompilerParams(vmem_limit_bytes=VMEM_LIMIT, dimension_semantics=semantics)


def dot_nt(a, b):
    return lax.dot_general(a, b, (((1,), (1,)), ((), ())), preferred_element_type=F32)


def dot_nn(a, b):
    return lax.dot_general(a, b, (((1,), (0,)), ((), ())), preferred_element_type=F32)


def dot_tn(a, b):
    return lax.dot_general(a, b, (((0,), (0,)), ((), ())), preferred_element_type=F32)


def project_kernel(inner, x_ref, w_ref, o_ref, acc):
    step = pl.program_id(0)
    part = dot_nn(x_ref[...], w_ref[...])

    @pl.when(step == 0)
    def _():
        acc[...] = part

    @pl.when(step > 0)
    def _():
        acc[...] += part

    @pl.when(step == pl.num_programs(0) - 1)
    def _():
        width = o_ref.shape[2]
        for block in range(inner):
            o_ref[block] = acc[:, block * width : (block + 1) * width].astype(BF16)


def project(x, w, inner):
    rows, depth = x.shape
    cols = w.shape[1]
    tile = 512
    return pl.pallas_call(
        functools.partial(project_kernel, inner),
        grid=(depth // tile,),
        in_specs=[
            pl.BlockSpec((rows, tile), lambda k: (0, k)),
            pl.BlockSpec((tile, cols), lambda k: (k, 0)),
        ],
        out_specs=pl.BlockSpec((inner, rows, cols // inner), lambda k: (0, 0, 0)),
        out_shape=jax.ShapeDtypeStruct((inner, rows, cols // inner), BF16),
        scratch_shapes=[pltpu.VMEM((rows, cols), F32)],
        compiler_params=params(("arbitrary",)),
        cost_estimate=pl.CostEstimate(
            flops=2 * rows * depth * cols,
            bytes_accessed=2 * (rows * depth + depth * cols + rows * cols),
            transcendentals=0,
        ),
        name="project",
    )(x, w)


def two_heads(block):
    lane = lax.broadcasted_iota(jnp.int32, block.shape, 1)
    zero = jnp.zeros_like(block)
    return jnp.concatenate(
        [jnp.where(lane < HEAD_DIM, block, zero), jnp.where(lane >= HEAD_DIM, block, zero)], axis=0
    )


def own_blocks(full):
    rows = full.shape[1] // 2
    return jnp.concatenate([full[:HEAD_DIM, :rows], full[HEAD_DIM:, rows:]], axis=0)


def each_question(n_outer, inner, n_local, refs, begin, entry, end):
    outer_ref, slot_ref, list_ref, count_ref = refs
    my_outer = outer_ref[0]
    first_slot = my_outer * n_local
    list_len = list_ref.shape[1]

    def question(rel, carry):
        outer = lax.rem(my_outer + lax.div(rel, inner), n_outer)
        ident = outer * inner + lax.rem(rel, inner)
        begin(rel)

        def one(e, inner_carry):
            slot = slot_ref[list_ref[ident, e]] - first_slot

            @pl.when((slot >= 0) & (slot < n_local))
            def _():
                entry(rel, slot)

            return inner_carry

        lax.fori_loop(0, jnp.minimum(count_ref[ident], list_len), one, 0)
        end(rel)
        return carry

    lax.fori_loop(0, n_outer * inner, question, 0)


def pair_lanes(pair):
    return slice(pair * LANES, (pair + 1) * LANES)


def stats_kernel(n_outer, inner, outer_ref, slot_ref, list_ref, count_ref, k_ref, q_ref, o_ref, qbd):
    n_pair = q_ref.shape[2] // LANES
    n_local = k_ref.shape[0]

    def begin(rel):
        for pair in range(n_pair):
            qbd[pair] = two_heads(q_ref[rel, :, pair_lanes(pair)])
        o_ref[0, rel] = jnp.full(o_ref.shape[2:], NEG_LARGE, F32)
        o_ref[1, rel] = jnp.zeros(o_ref.shape[2:], F32)

    def entry(rel, slot):
        for pair in range(n_pair):
            scores = dot_nt(k_ref[slot, :, pair_lanes(pair)], qbd[pair])
            row = slice(pair, pair + 1)
            old = o_ref[0, rel, row, :]
            new = jnp.maximum(old, jnp.max(scores, axis=0, keepdims=True))
            add = jnp.sum(jnp.exp(scores - new), axis=0, keepdims=True)
            o_ref[0, rel, row, :] = new
            o_ref[1, rel, row, :] = o_ref[1, rel, row, :] * jnp.exp(old - new) + add

    each_question(
        n_outer, inner, n_local, (outer_ref, slot_ref, list_ref, count_ref), begin, entry, lambda rel: None
    )


def value_grad_kernel(
    n_outer, inner, outer_ref, slot_ref, list_ref, count_ref, k_ref, q_ref, g_ref, st_ref, o_ref, qbd, gbd, acc
):
    n_pair = q_ref.shape[2] // LANES
    n_local = k_ref.shape[0]
    acc[...] = jnp.zeros_like(acc)

    def begin(rel):
        for pair in range(n_pair):
            qbd[pair] = two_heads(q_ref[rel, :, pair_lanes(pair)])
            gbd[pair] = two_heads(g_ref[rel, :, pair_lanes(pair)])

    def entry(rel, slot):
        for pair in range(n_pair):
            row = slice(pair, pair + 1)
            scores = dot_nt(k_ref[slot, :, pair_lanes(pair)], qbd[pair])
            probs = jnp.exp(scores - st_ref[0, rel, row, :]) * st_ref[1, rel, row, :]
            term = dot_nn(probs.astype(BF16), gbd[pair]).astype(BF16)
            acc[slot, :, pair_lanes(pair)] += term.astype(F32)

    each_question(
        n_outer, inner, n_local, (outer_ref, slot_ref, list_ref, count_ref), begin, entry, lambda rel: None
    )

    def finish(slot, carry):
        o_ref[slot] = acc[slot].astype(BF16)
        return carry

    lax.fori_loop(0, n_local, finish, 0)


def context_kernel(
    n_outer, inner, outer_ref, slot_ref, list_ref, count_ref, k_ref, v_ref, q_ref, st_ref, o_ref, qbd, acc
):
    n_pair = q_ref.shape[2] // LANES
    n_local = k_ref.shape[0]

    def begin(rel):
        for pair in range(n_pair):
            qbd[pair] = two_heads(q_ref[rel, :, pair_lanes(pair)])
        acc[...] = jnp.zeros_like(acc)

    def entry(rel, slot):
        for pair in range(n_pair):
            row = slice(pair, pair + 1)
            scores = dot_nt(k_ref[slot, :, pair_lanes(pair)], qbd[pair])
            weights = jnp.exp(scores - st_ref[0, rel, row, :]).astype(BF16)
            acc[pair] += dot_tn(v_ref[slot, :, pair_lanes(pair)], weights)

    def end(rel):
        for pair in range(n_pair):
            o_ref[rel, pair_lanes(pair), :] = own_blocks(acc[pair])

    each_question(
        n_outer, inner, n_local, (outer_ref, slot_ref, list_ref, count_ref), begin, entry, end
    )


def score_grad_kernel(
    n_outer,
    inner,
    outer_ref,
    slot_ref,
    list_ref,
    count_ref,
    k_ref,
    v_ref,
    q_ref,
    g_ref,
    st_ref,
    dot_ref,
    dk_ref,
    dq_ref,
    qbd,
    gbd,
    acc_k,
    acc_q,
):
    n_pair = q_ref.shape[2] // LANES
    n_local = k_ref.shape[0]
    acc_k[...] = jnp.zeros_like(acc_k)

    def begin(rel):
        for pair in range(n_pair):
            qbd[pair] = two_heads(q_ref[rel, :, pair_lanes(pair)])
            gbd[pair] = two_heads(g_ref[rel, :, pair_lanes(pair)])
        acc_q[...] = jnp.zeros_like(acc_q)

    def entry(rel, slot):
        for pair in range(n_pair):
            row = slice(pair, pair + 1)
            keys = k_ref[slot, :, pair_lanes(pair)]
            scores = dot_nt(keys, qbd[pair])
            probs = jnp.exp(scores - st_ref[0, rel, row, :]) * st_ref[1, rel, row, :]
            dprob = dot_nt(v_ref[slot, :, pair_lanes(pair)], gbd[pair])
            dscore = (probs * (dprob - dot_ref[rel, row, :])).astype(BF16)
            term = dot_nn(dscore, qbd[pair]).astype(BF16)
            acc_k[slot, :, pair_lanes(pair)] += term.astype(F32)
            acc_q[pair] += dot_tn(keys, dscore)

    def end(rel):
        for pair in range(n_pair):
            dq_ref[rel, pair_lanes(pair), :] = own_blocks(acc_q[pair])

    each_question(
        n_outer, inner, n_local, (outer_ref, slot_ref, list_ref, count_ref), begin, entry, end
    )

    def finish(slot, carry):
        dk_ref[slot] = acc_k[slot].astype(BF16)
        return carry

    lax.fori_loop(0, n_local, finish, 0)


def combine_context_kernel(n_parts, *refs):
    parts, (total_ref, g_ref, o_ref, dot_ref) = refs[:n_parts], refs[n_parts:]
    width = g_ref.shape[2]
    for q in range(g_ref.shape[0]):
        mix = parts[0][q]
        for part in parts[1:]:
            mix = mix + part[q]
        grad = jnp.transpose(g_ref[q].astype(F32))
        rows = mix.shape[1]
        pieces = []
        for head in range(width // HEAD_DIM):
            feats = slice(head * HEAD_DIM, (head + 1) * HEAD_DIM)
            pair, lanes = head // 2, slice((head % 2) * rows, (head % 2 + 1) * rows)
            ctx = (mix[feats] / total_ref[q, pair : pair + 1, lanes]).astype(BF16).astype(F32)
            dot_ref[q, pair : pair + 1, lanes] = jnp.sum(grad[feats] * ctx, axis=0, keepdims=True)
            pieces.append(ctx)
        o_ref[q] = jnp.transpose(jnp.concatenate(pieces, axis=0)).astype(BF16)


def combine_query_kernel(n_parts, *refs):
    parts, o_ref = refs[:n_parts], refs[n_parts]
    for q in range(o_ref.shape[0]):
        mix = parts[0][q]
        for part in parts[1:]:
            mix = mix + part[q]
        o_ref[q] = jnp.transpose(mix * SCALE).astype(BF16)


def vmem_call(kernel, scalars, arrays, out_shape, scratch, flops, name, transcendentals=0):
    smem = pl.BlockSpec(memory_space=pltpu.SMEM)
    vmem = pl.BlockSpec(memory_space=pltpu.VMEM)
    size = sum(a.size * a.dtype.itemsize for a in arrays)
    outs = jax.tree.leaves(out_shape)
    size += sum(o.size * o.dtype.itemsize for o in outs)
    return pl.pallas_call(
        kernel,
        in_specs=[smem] * len(scalars) + [vmem] * len(arrays),
        out_specs=jax.tree.map(lambda _: vmem, out_shape),
        out_shape=out_shape,
        scratch_shapes=scratch,
        compiler_params=params(),
        cost_estimate=pl.CostEstimate(
            flops=int(flops), bytes_accessed=int(size), transcendentals=int(transcendentals)
        ),
        name=name,
    )(*scalars, *arrays)


def body(
    queries,
    encoded,
    key_weight,
    value_weight,
    out_weight,
    out_grad,
    slot_of,
    passage_lists,
    list_counts,
):
    head_width = key_weight.shape[1]
    rows = queries.shape[0]
    tok_local = encoded.shape[0]
    pas_dev = tok_local // PLEN
    n_pas = lax.axis_size("pas")
    inner = INNER
    n_outer = n_pas // inner
    width = head_width // inner
    n_pair = width // LANES
    n_local = inner * pas_dev
    n_q = n_pas
    my_outer = (lax.axis_index("pas") // inner).astype(jnp.int32).reshape(1)
    groups = [[o * inner + i for i in range(inner)] for o in range(n_outer)]

    def swap(x):
        return lax.all_to_all(
            x, "pas", split_axis=0, concat_axis=0, tiled=True, axis_index_groups=groups
        )

    def from_outer(x, r):
        return lax.ppermute(
            x,
            "pas",
            [(((o + r) % n_outer) * inner + i, o * inner + i) for o in range(n_outer) for i in range(inner)],
        )

    def to_outer(x, r):
        return lax.ppermute(
            x,
            "pas",
            [(o * inner + i, ((o + r) % n_outer) * inner + i) for o in range(n_outer) for i in range(inner)],
        )

    def by_block(x):
        return jnp.transpose(x.reshape(x.shape[0], inner, width), (1, 0, 2))

    def from_block(x):
        return jnp.transpose(x, (1, 0, 2)).reshape(x.shape[1], head_width)

    def gather_outer(x):
        return jnp.concatenate([x] + [from_outer(x, r) for r in range(1, n_outer)], axis=0)

    scalars = (my_outer, slot_of, passage_lists, list_counts)
    dims = (n_outer, inner)
    unit = 2.0 * n_q * inner * 2 * PLEN * 2 * rows * LANES * n_pair
    exps = n_q * inner * 2 * PLEN * 2 * rows * n_pair

    q_all = gather_outer(swap(by_block(queries * jnp.asarray(SCALE, BF16))))
    key_part = project(encoded, key_weight, inner)
    keys = swap(key_part).reshape(n_local, PLEN, width)
    value_part = project(encoded, value_weight, inner)
    values = swap(value_part).reshape(n_local, PLEN, width)
    context_grad = lax.dot_general(
        lax.all_gather(out_grad, "head", axis=1, tiled=True),
        out_weight,
        (((1,), (1,)), ((), ())),
        preferred_element_type=F32,
    ).astype(BF16)
    g_own = swap(by_block(context_grad))
    g_all = gather_outer(g_own)

    pair_scratch = pltpu.VMEM((n_pair, 2 * rows, LANES), BF16)
    stat_shape = (n_q, n_pair, 2 * rows)
    stats = vmem_call(
        functools.partial(stats_kernel, *dims),
        scalars,
        (keys, q_all),
        jax.ShapeDtypeStruct((2,) + stat_shape, F32),
        [pair_scratch],
        unit,
        "stats",
        exps,
    )
    tops, sums = [stats[0]], [stats[1]]
    for r in range(1, n_outer):
        other = jnp.roll(from_outer(stats, r), r * inner, axis=1)
        tops.append(other[0])
        sums.append(other[1])
    row_top = functools.reduce(jnp.maximum, tops)
    row_total = sum(s * jnp.exp(t - row_top) for s, t in zip(sums, tops))
    norm = jnp.stack([row_top, 1.0 / row_total])

    acc_scratch = pltpu.VMEM((n_local, PLEN, width), F32)
    value_done = vmem_call(
        functools.partial(value_grad_kernel, *dims),
        scalars,
        (keys, q_all, g_all, norm),
        jax.ShapeDtypeStruct((n_local, PLEN, width), BF16),
        [pair_scratch, pair_scratch, acc_scratch],
        2 * unit,
        "value_grad",
        exps,
    )
    value_grad = from_block(swap(value_done.reshape(inner, tok_local, width)))

    mix_scratch = pltpu.VMEM((n_pair, LANES, 2 * rows), F32)
    mix_shape = jax.ShapeDtypeStruct((n_q, width, rows), F32)
    mixes = vmem_call(
        functools.partial(context_kernel, *dims),
        scalars,
        (keys, values, q_all, norm),
        mix_shape,
        [pair_scratch, mix_scratch],
        2 * unit,
        "context",
        exps,
    )

    def parts_of(x):
        return [x[:inner]] + [
            to_outer(x[r * inner : (r + 1) * inner], r) for r in range(1, n_outer)
        ]

    context, grad_dot = vmem_call(
        functools.partial(combine_context_kernel, n_outer),
        (),
        tuple(parts_of(mixes)) + (row_total[:inner], g_own),
        (
            jax.ShapeDtypeStruct((inner, rows, width), BF16),
            jax.ShapeDtypeStruct((inner, n_pair, 2 * rows), F32),
        ),
        [],
        1e6,
        "combine_context",
    )
    dots = gather_outer(grad_dot)
    key_done, query_mix = vmem_call(
        functools.partial(score_grad_kernel, *dims),
        scalars,
        (keys, values, q_all, g_all, norm, dots),
        (jax.ShapeDtypeStruct((n_local, PLEN, width), BF16), mix_shape),
        [pair_scratch, pair_scratch, acc_scratch, mix_scratch],
        4 * unit,
        "score_grad",
        exps,
    )
    query_done = vmem_call(
        functools.partial(combine_query_kernel, n_outer),
        (),
        tuple(parts_of(query_mix)),
        jax.ShapeDtypeStruct((inner, rows, width), BF16),
        [],
        1e6,
        "combine_query",
    )
    query_grad = from_block(swap(query_done))
    key_grad = from_block(swap(key_done.reshape(inner, tok_local, width)))

    context_rows = from_block(swap(context))
    projected = jnp.dot(context_rows, out_weight, preferred_element_type=F32)
    output = lax.psum_scatter(projected, "head", scatter_dimension=1, tiled=True).astype(BF16)
    return (output, query_grad, key_grad, value_grad)


def solution(mesh):
    in_specs = (
        P("pas", "head"),
        P("pas", None),
        P(None, "head"),
        P(None, "head"),
        P("head", None),
        P("pas", "head"),
        P(),
        P(),
        P(),
    )
    out_specs = (P("pas", "head"), P("pas", "head"), P("pas", "head"), P("pas", "head"))
    return jax.shard_map(body, mesh=mesh, in_specs=in_specs, out_specs=out_specs, check_vma=False)
```

time: 1120 us -> 390 us (0.35)
  waiting for transfers between devices: 709 us -> 124 us
  local copies, waits for them, and re-layouts: 201 us -> 16.9 us
  Pallas kernels: 0 us -> 172 us
  matrix products: 134 us -> 12.6 us
  other arithmetic: 37.4 us -> 4.41 us
  starting transfers between devices: 13.3 us -> 42.1 us
    all_to_all x2 -> x8, waiting for transfers between devices: 657 us -> 48.1 us  [swap(): lax.all_to_all(x, 'pas', split_axis=0, concat_axis=0, tiled=True, axis_in...]
    pallas_call x0 -> x8, Pallas kernels: none -> 172 us  [the longest x6 139 us: vmem_call(): pl.pallas_call(kernel, in_specs=[smem] * len(scalars) + [vmem] * len(arra...]
    dot_general x101 -> x1, matrix products: 127 us -> 5.99 us  [body(): projected = jnp.dot(context_rows, out_weight, preferred_element_type=F32)]
    ppermute x0 -> x6, waiting for transfers between devices: none -> 75.4 us  [the longest x2 46.3 us: to_outer(): lax.ppermute(x, 'pas', [(o * inner + i, (o + r) % n_outer * inner + i) fo...]
    reshape x8 -> x4, local copies, waits for them, and re-layouts: 75.3 us -> 6.52 us  [the longest x2 4.81 us: from_block(): return jnp.transpose(x, (1, 0, 2)).reshape(x.shape[1], head_width)]
    convert_element_type x3 -> x0, local copies, waits for them, and re-layouts: 59.3 us -> none  [the longest x1 53.6 us: body(): outgoing = jnp.einsum('rcl,lx->rcx', selector, kv_local.reshape(pas_dev,...]
    reduce_scatter x1, waiting for transfers between devices: 32 us -> 0.01 us  [body(): lax.psum_scatter(projected, 'head', scatter_dimension=1, tiled=True)]
    unnamed x9 -> x18, local copies, waits for them, and re-layouts: 30.2 us -> 5.72 us
  transfers between devices with their start and end apart: 4 -> 16, of which waited for: 4 -> 8; matrix products, arithmetic and copies ran while one was open for 1% -> 6% of each run, Pallas kernels for 0% -> 34%
where the time goes in v1:
time: 390 us; the launch traced here: 386 us
  Pallas kernels  172 us (44%)
  waiting for transfers between devices  124 us (32%)
  starting transfers between devices  42.1 us (11%)
  local copies, waits for them, and re-layouts  16.9 us (4%)
  between operations  14.2 us (4%)
  matrix products  12.6 us (3%)
  other arithmetic  4.41 us (1%)
    pallas_call x6, Pallas kernels, vmem_call(): pl.pallas_call(kernel, in_specs=[smem] * len(scalars) + [vmem] * len(arra...  139 us
    all_to_all x8, waiting for transfers between devices, swap(): lax.all_to_all(x, 'pas', split_axis=0, concat_axis=0, tiled=True, axis_in...  48.1 us
    ppermute x2, waiting for transfers between devices, to_outer(): lax.ppermute(x, 'pas', [(o * inner + i, (o + r) % n_outer * inner + i) fo...  46.3 us
    all_to_all x8, starting transfers between devices, swap(): lax.all_to_all(x, 'pas', split_axis=0, concat_axis=0, tiled=True, axis_in...  33.4 us
    pallas_call x2, Pallas kernels, project(): pl.pallas_call(functools.partial(project_kernel, inner), grid=(depth // t...  32.6 us
    ppermute x4, waiting for transfers between devices, from_outer(): lax.ppermute(x, 'pas', [((o + r) % n_outer * inner + i, o * inner + i) fo...  29 us
  transfers between devices with their start and end apart: 16, of which 8 were waited for; matrix products, arithmetic and copies ran while one was open for 6% of the time, Pallas kernels for 34%

profile of v1, /device:TPU:0, one launch (start us, length us, event | category | flops | bytes accessed | tf_op | source)
XLA Modules:
  0.0 386.2 jit_solution(10673450021849742012)
XLA Ops:
  7.2 1.1 copy.24
  8.3 0.9 copy.25
  9.2 5.2 %all-to-all-start.2 = ((bf16[4,128,256]{2,1,0:T(8,128)(2,1)}), bf16[4,128,256]{2,1,0:T(8,128)(2,1)S(1)}, u32[]{:S(2)}, u32[]{:S(2)}) async-start(bf16[4,128,256]{2,1,0:T(8,128)(2,1)} %bitcast.4), calls=%async_computation.2 | async-start | bytes 524288 | tf_op jit(solution)/shard_map/all_to_all | solution.py:340
  14.4 16.3 %project.2 = bf16[4,1024,256]{2,1,0:T(8,128)(2,1)} custom-call(bf16[1024,4096]{1,0:T(8,128)(2,1)} %x_ref.3, bf16[4096,1024]{1,0:T(8,128)(2,1)} %w_ref.2), custom_call_target="tpu_custom_call" | custom-call | flops 8589934592 | bytes 18874368 | tf_op jit(solution)/shard_map/project/pallas_call | solution.py:62
  30.7 4.2 %all-to-all-start = ((bf16[4,1024,256]{2,1,0:T(8,128)(2,1)}), bf16[4,1024,256]{2,1,0:T(8,128)(2,1)S(1)}, u32[]{:S(2)}, u32[]{:S(2)}) async-start(bf16[4,1024,256]{2,1,0:T(8,128)(2,1)} %project.2), calls=%async_computation | async-start | bytes 4194304 | tf_op jit(solution)/shard_map/all_to_all | solution.py:340
  34.9 16.3 %project.3 = bf16[4,1024,256]{2,1,0:T(8,128)(2,1)} custom-call(bf16[1024,4096]{1,0:T(8,128)(2,1)} %x_ref.3, bf16[4096,1024]{1,0:T(8,128)(2,1)} %w_ref.3), custom_call_target="tpu_custom_call" | custom-call | flops 8589934592 | bytes 18874368 | tf_op jit(solution)/shard_map/project/pallas_call | solution.py:62
  51.2 8.0 %all-to-all-done = bf16[4,1024,256]{2,1,0:T(8,128)(2,1)S(1)} async-done(((bf16[4,1024,256]{2,1,0:T(8,128)(2,1)}), bf16[4,1024,256]{2,1,0:T(8,128)(2,1)S(1)}, u32[]{:S(2)}, u32[]{:S(2)}) %all-to-all-start) | async-done | bytes 2097184 | tf_op jit(solution)/shard_map/all_to_all | solution.py:340
  59.2 1.3 copy-done.1
  60.5 4.4 %all-to-all-start.1 = ((bf16[4,1024,256]{2,1,0:T(8,128)(2,1)}), bf16[4,1024,256]{2,1,0:T(8,128)(2,1)}, u32[]{:S(2)}, u32[]{:S(2)}) async-start(bf16[4,1024,256]{2,1,0:T(8,128)(2,1)} %project.3), calls=%async_computation.1 | async-start | bytes 4194304 | tf_op jit(solution)/shard_map/all_to_all | solution.py:340
  65.0 0.7 all-gather.2.cloned.1.call-update
  65.7 2.7 collective-permute-start
  68.4 24.3 %collective-permute-done = bf16[4,128,256]{2,1,0:T(8,128)(2,1)S(1)} collective-permute-done((bf16[4,128,256]{2,1,0:T(8,128)(2,1)S(1)}, bf16[4,128,256]{2,1,0:T(8,128)(2,1)S(1)}, u32[]{:S(2)}, u32[]{:S(2)}) %collective-permute-start) | collective-permute-done | bytes 262176 | tf_op jit(solution)/shard_map/ppermute | solution.py:345
  92.7 0.8 copy-done.5
  93.5 21.8 %stats.1 = f32[2,8,2,256]{3,2,1,0:T(2,128)} custom-call(s32[1]{0:T(128)} %bitcast.outer_ref, s32[32]{0:T(128)} %slot_ref.7, s32[8,16]{1,0:T(8,128)} %list_ref.7, s32[8]{0:T(128)} %count_ref.7, bf16[16,256,256]{2,1,0:T(8,128)(2,1)} %bitcast.31, bf16[8,128,256]{2,1,0:T(8,128)(2,1)} %copy-done.5), custom_call_target="tpu_custom_call" | custom-call | flops 2147483648 | bytes 2654208 | tf_op jit(solution)/shard_map/stats/pallas_call | solution.py:300
  115.3 3.1 collective-permute-start.1
  118.4 6.6 %convolution_convert_fusion = bf16[128,1024]{1,0:T(8,128)(2,1)S(1)} fusion(bf16[128,4096]{1,0:T(8,128)(2,1)} %all-gather.2.cloned.1.call-done, bf16[1024,4096]{1,0:T(8,128)(2,1)} %param.13), kind=kOutput, calls=%fused_computation | convolution fusion | flops 1073872896 | bytes 9699328 | tf_op jit(solution)/shard_map/dot_general | solution.py:377
  125.2 0.9 copy.27
  126.2 0.6 pad_maximum_fusion.st_ref
  126.8 3.9 %all-to-all-start.3 = ((bf16[4,128,256]{2,1,0:T(8,128)(2,1)}), bf16[4,128,256]{2,1,0:T(8,128)(2,1)S(1)}, u32[]{:S(2)}, u32[]{:S(2)}) async-start(bf16[4,128,256]{2,1,0:T(8,128)(2,1)} %bitcast.10), calls=%async_computation.3 | async-start | bytes 524288 | tf_op jit(solution)/shard_map/all_to_all | solution.py:340
  130.7 37.8 %context.1 = f32[8,256,128]{2,1,0:T(8,128)} custom-call(s32[1]{0:T(128)} %bitcast.outer_ref, s32[32]{0:T(128)} %slot_ref.7, s32[8,16]{1,0:T(8,128)} %list_ref.7, s32[8]{0:T(128)} %count_ref.7, bf16[16,256,256]{2,1,0:T(8,128)(2,1)} %bitcast.32, bf16[16,256,256]{2,1,0:T(8,128)(2,1)} %bitcast.2.v_ref, bf16[8,128,256]{2,1,0:T(8,128)(2,1)} %copy-done.5, ...), custom_call_target="tpu_custom_call" | custom-call | flops 4294967296 | bytes 5799936 | tf_op jit(solution)/shard_map/context/pallas_call | solution.py:300
  168.4 2.1 fusion.9
  170.5 2.3 collective-permute-start.2
  172.8 0.6 collective-permute-start.3
  173.5 0.6 fusion.3.refs_2_
  174.1 28.4 %collective-permute-done.2.refs_1_ = f32[4,256,128]{2,1,0:T(8,128)S(1)} collective-permute-done((f32[4,256,128]{2,1,0:T(8,128)S(1)}, f32[4,256,128]{2,1,0:T(8,128)S(1)}, u32[]{:S(2)}, u32[]{:S(2)}) %collective-permute-start.2) | collective-permute-done | bytes 524320 | tf_op jit(solution)/shard_map/ppermute | solution.py:352
  202.5 0.8 copy-done.2
  203.3 2.2 combine_context.1
  205.5 0.7 collective-permute-done.3
  206.2 4.1 %collective-permute-done.4 = f32[4,2,256]{2,1,0:T(2,128)S(1)} collective-permute-done((f32[4,2,256]{2,1,0:T(2,128)}, f32[4,2,256]{2,1,0:T(2,128)S(1)}, u32[]{:S(2)}, u32[]{:S(2)}) %collective-permute-start.4) | collective-permute-done | bytes 8224 | tf_op jit(solution)/shard_map/ppermute | solution.py:345
  210.3 1.3 pad_maximum_fusion.2.dot_ref
  211.6 40.5 %score_grad.1 = (bf16[16,256,256]{2,1,0:T(8,128)(2,1)}, f32[8,256,128]{2,1,0:T(8,128)}) custom-call(s32[1]{0:T(128)} %bitcast.outer_ref, s32[32]{0:T(128)} %slot_ref.7, s32[8,16]{1,0:T(8,128)} %list_ref.7, s32[8]{0:T(128)} %count_ref.7, bf16[16,256,256]{2,1,0:T(8,128)(2,1)} %bitcast.33, bf16[16,256,256]{2,1,0:T(8,128)(2,1)} %bitcast.2.v_ref, ...), custom_call_target="tpu_custom_call" | custom-call | flops 8589934592 | bytes 8437760 | tf_op jit(solution)/shard_map/score_grad/pallas_call | solution.py:300
  252.1 2.1 fusion.8
  254.1 3.4 all-to-all-start.4
  257.5 17.9 %collective-permute-done.5.refs_1_ = f32[4,256,128]{2,1,0:T(8,128)S(1)} collective-permute-done((f32[4,256,128]{2,1,0:T(8,128)S(1)}, f32[4,256,128]{2,1,0:T(8,128)S(1)}, u32[]{:S(2)}, u32[]{:S(2)}) %collective-permute-start.5) | collective-permute-done | bytes 524320 | tf_op jit(solution)/shard_map/ppermute | solution.py:352
  275.5 0.8 copy-done.3
  276.3 2.0 combine_query.1
  278.3 3.6 all-to-all-start.5
  281.9 34.9 %value_grad.1 = bf16[16,256,256]{2,1,0:T(8,128)(2,1)} custom-call(s32[1]{0:T(128)} %bitcast.outer_ref, s32[32]{0:T(128)} %slot_ref.7, s32[8,16]{1,0:T(8,128)} %list_ref.7, s32[8]{0:T(128)} %count_ref.7, bf16[16,256,256]{2,1,0:T(8,128)(2,1)} %bitcast.34, bf16[8,128,256]{2,1,0:T(8,128)(2,1)} %copy-done.5, bf16[8,128,256]{2,1,0:T(8,128)(2,1)} %copy-done.4, ...), custom_call_target="tpu_custom_call" | custom-call | flops 4294967296 | bytes 5275648 | tf_op jit(solution)/shard_map/value_grad/pallas_call | solution.py:300
  316.9 4.2 %all-to-all-start.7 = ((bf16[4,1024,256]{2,1,0:T(8,128)(2,1)}), bf16[4,1024,256]{2,1,0:T(8,128)(2,1)S(1)}, u32[]{:S(2)}, u32[]{:S(2)}) async-start(bf16[4,1024,256]{2,1,0:T(8,128)(2,1)} %bitcast.36), calls=%async_computation.8 | async-start | bytes 4194304 | tf_op jit(solution)/shard_map/all_to_all | solution.py:340
  321.2 6.0 %fusion.11 = f32[128,4096]{1,0:T(8,128)} fusion(bf16[128,1024]{0,1:T(8,128)(2,1)S(1)} %bitcast.39, bf16[1024,4096]{1,0:T(8,128)(2,1)} %param.13), kind=kOutput, calls=%fused_computation.27 | convolution fusion | flops 1073741824 | bytes 10747904 | tf_op jit(solution)/shard_map/dot_general | solution.py:474
  327.2 17.6 %all-to-all-done.7 = bf16[4,1024,256]{2,1,0:T(8,128)(2,1)S(1)} async-done(((bf16[4,1024,256]{2,1,0:T(8,128)(2,1)}), bf16[4,1024,256]{2,1,0:T(8,128)(2,1)S(1)}, u32[]{:S(2)}, u32[]{:S(2)}) %all-to-all-start.7) | async-done | bytes 2097184 | tf_op jit(solution)/shard_map/all_to_all | solution.py:340
  344.9 4.4 %all-to-all-start.6 = ((bf16[4,1024,256]{2,1,0:T(8,128)(2,1)}), bf16[4,1024,256]{2,1,0:T(8,128)(2,1)}, u32[]{:S(2)}, u32[]{:S(2)}) async-start(bf16[4,1024,256]{2,1,0:T(8,128)(2,1)} %bitcast.35), calls=%async_computation.7 | async-start | bytes 4194304 | tf_op jit(solution)/shard_map/all_to_all | solution.py:340
  349.4 0.2 copy.29
  349.5 0.9 copy.32
  350.4 1.6 copy.34
  352.0 22.4 %all-to-all-done.6 = bf16[4,1024,256]{2,1,0:T(8,128)(2,1)} async-done(((bf16[4,1024,256]{2,1,0:T(8,128)(2,1)}), bf16[4,1024,256]{2,1,0:T(8,128)(2,1)}, u32[]{:S(2)}, u32[]{:S(2)}) %all-to-all-start.6) | async-done | bytes 2097184 | tf_op jit(solution)/shard_map/all_to_all | solution.py:340
  374.4 3.2 copy.33
  377.6 1.8 convert_element_type.7
  (33 shorter events, 0.6 us)
Async XLA Ops:
  9.2 21.5 %all-to-all-start.2 = ((bf16[4,128,256]{2,1,0:T(8,128)(2,1)}), bf16[4,128,256]{2,1,0:T(8,128)(2,1)S(1)}, u32[]{:S(2)}, u32[]{:S(2)}) async-start(bf16[4,128,256]{2,1,0:T(8,128)(2,1)} %bitcast.4), calls=%async_computation.2 | async-start | bytes 524288 | tf_op jit(solution)/shard_map/all_to_all | solution.py:340
  30.7 28.5 %all-to-all-start = ((bf16[4,1024,256]{2,1,0:T(8,128)(2,1)}), bf16[4,1024,256]{2,1,0:T(8,128)(2,1)S(1)}, u32[]{:S(2)}, u32[]{:S(2)}) async-start(bf16[4,1024,256]{2,1,0:T(8,128)(2,1)} %project.2), calls=%async_computation | async-start | bytes 4194304 | tf_op jit(solution)/shard_map/all_to_all | solution.py:340
  59.2 1.3 copy-start.1
  60.5 66.3 %all-to-all-start.1 = ((bf16[4,1024,256]{2,1,0:T(8,128)(2,1)}), bf16[4,1024,256]{2,1,0:T(8,128)(2,1)}, u32[]{:S(2)}, u32[]{:S(2)}) async-start(bf16[4,1024,256]{2,1,0:T(8,128)(2,1)} %project.3), calls=%async_computation.1 | async-start | bytes 4194304 | tf_op jit(solution)/shard_map/all_to_all | solution.py:340
  65.0 53.4 %all-gather.2.cloned.1.call-start = ((), (), s32[]{:S(2)}) async-start(), calls=%async_computation.9 | async-start | bytes 1310720 | tf_op jit(solution)/shard_map/all_gather | solution.py:378
  65.7 27.0 %collective-permute-start = (bf16[4,128,256]{2,1,0:T(8,128)(2,1)S(1)}, bf16[4,128,256]{2,1,0:T(8,128)(2,1)S(1)}, u32[]{:S(2)}, u32[]{:S(2)}) collective-permute-start(bf16[4,128,256]{2,1,0:T(8,128)(2,1)S(1)} %all-to-all-done.2), channel_id=1, source_target_pairs={{16,0},{20,4},{24,8},{28,12},{0,16},{4,20},{8,24},{12,28},{17,1},{... | collective-permute-start | bytes 786440 | tf_op jit(solution)/shard_map/ppermute | solution.py:345
  92.7 0.8 copy-start.5
  115.3 10.8 %copy-start.6 = (f32[2,8,2,256]{3,2,1,0:T(2,128)S(1)}, f32[2,8,2,256]{3,2,1,0:T(2,128)}, u32[]{:S(2)}) copy-start(f32[2,8,2,256]{3,2,1,0:T(2,128)} %stats.1) | copy-start | bytes 98308
  115.3 10.8 %collective-permute-start.1 = (f32[2,8,2,256]{3,2,1,0:T(2,128)}, f32[2,8,2,256]{3,2,1,0:T(2,128)S(1)}, u32[]{:S(2)}, u32[]{:S(2)}) collective-permute-start(f32[2,8,2,256]{3,2,1,0:T(2,128)} %stats.1), channel_id=1, source_target_pairs={{16,0},{20,4},{24,8},{28,12},{0,16},{4,20},{8,24},{12,28},{17,1},{... | collective-permute-start | bytes 98312 | tf_op jit(solution)/shard_map/ppermute | solution.py:345
  126.8 46.0 %all-to-all-start.3 = ((bf16[4,128,256]{2,1,0:T(8,128)(2,1)}), bf16[4,128,256]{2,1,0:T(8,128)(2,1)S(1)}, u32[]{:S(2)}, u32[]{:S(2)}) async-start(bf16[4,128,256]{2,1,0:T(8,128)(2,1)} %bitcast.10), calls=%async_computation.3 | async-start | bytes 524288 | tf_op jit(solution)/shard_map/all_to_all | solution.py:340
  170.5 32.0 %collective-permute-start.2 = (f32[4,256,128]{2,1,0:T(8,128)S(1)}, f32[4,256,128]{2,1,0:T(8,128)S(1)}, u32[]{:S(2)}, u32[]{:S(2)}) collective-permute-start(f32[4,256,128]{2,1,0:T(8,128)S(1)} %get-tuple-element.24), channel_id=1, source_target_pairs={{0,16},{4,20},{8,24},{12,28},{16,0},{20,4},{24,8},{28,12},{1,17},{... | collective-permute-start | bytes 1572872 | tf_op jit(solution)/shard_map/ppermute | solution.py:352
  172.8 29.7 %copy-start = (bf16[4,128,256]{2,1,0:T(8,128)(2,1)}, bf16[4,128,256]{2,1,0:T(8,128)(2,1)S(1)}, u32[]{:S(2)}) copy-start(bf16[4,128,256]{2,1,0:T(8,128)(2,1)S(1)} %all-to-all-done.3.refs_3_) | copy-start | bytes 786436
  172.8 33.4 %collective-permute-start.3 = (bf16[4,128,256]{2,1,0:T(8,128)(2,1)S(1)}, bf16[4,128,256]{2,1,0:T(8,128)(2,1)S(1)}, u32[]{:S(2)}, u32[]{:S(2)}) collective-permute-start(bf16[4,128,256]{2,1,0:T(8,128)(2,1)S(1)} %all-to-all-done.3.refs_3_), channel_id=1, source_target_pairs={{16,0},{20,4},{24,8},{28,12},{0,16},{4,20},{8,24},{12,28},{17,1},{... | collective-permute-start | bytes 786440 | tf_op jit(solution)/shard_map/ppermute | solution.py:345
  202.5 0.8 copy-start.2
  205.5 4.8 %collective-permute-start.4 = (f32[4,2,256]{2,1,0:T(2,128)}, f32[4,2,256]{2,1,0:T(2,128)S(1)}, u32[]{:S(2)}, u32[]{:S(2)}) collective-permute-start(f32[4,2,256]{2,1,0:T(2,128)} %get-tuple-element.9), channel_id=1, source_target_pairs={{16,0},{20,4},{24,8},{28,12},{0,16},{4,20},{8,24},{12,28},{17,1},{... | collective-permute-start | bytes 24584 | tf_op jit(solution)/shard_map/ppermute | solution.py:345
  206.2 5.4 %copy-start.4 = (bf16[8,128,256]{2,1,0:T(8,128)(2,1)}, bf16[8,128,256]{2,1,0:T(8,128)(2,1)S(1)}, u32[]{:S(2)}) copy-start(bf16[8,128,256]{2,1,0:T(8,128)(2,1)S(1)} %constant_dynamic-update-slice_fusion.2.g_ref) | copy-start | bytes 1572868
  254.1 21.3 %collective-permute-start.5 = (f32[4,256,128]{2,1,0:T(8,128)S(1)}, f32[4,256,128]{2,1,0:T(8,128)S(1)}, u32[]{:S(2)}, u32[]{:S(2)}) collective-permute-start(f32[4,256,128]{2,1,0:T(8,128)S(1)} %get-tuple-element.22), channel_id=1, source_target_pairs={{0,16},{4,20},{8,24},{12,28},{16,0},{20,4},{24,8},{28,12},{1,17},{... | collective-permute-start | bytes 1572872 | tf_op jit(solution)/shard_map/ppermute | solution.py:352
  254.1 24.2 %all-to-all-start.4 = ((bf16[4,128,256]{2,1,0:T(8,128)(2,1)}), bf16[4,128,256]{2,1,0:T(8,128)(2,1)S(1)}, u32[]{:S(2)}, u32[]{:S(2)}) async-start(bf16[4,128,256]{2,1,0:T(8,128)(2,1)} %get-tuple-element.8), calls=%async_computation.4 | async-start | bytes 524288 | tf_op jit(solution)/shard_map/all_to_all | solution.py:340
  275.5 0.8 copy-start.3
  278.3 38.5 %all-to-all-start.5 = ((bf16[4,128,256]{2,1,0:T(8,128)(2,1)}), bf16[4,128,256]{2,1,0:T(8,128)(2,1)S(1)}, u32[]{:S(2)}, u32[]{:S(2)}) async-start(bf16[4,128,256]{2,1,0:T(8,128)(2,1)} %combine_query.1), calls=%async_computation.6 | async-start | bytes 524288 | tf_op jit(solution)/shard_map/all_to_all | solution.py:340
  316.9 28.0 %all-to-all-start.7 = ((bf16[4,1024,256]{2,1,0:T(8,128)(2,1)}), bf16[4,1024,256]{2,1,0:T(8,128)(2,1)S(1)}, u32[]{:S(2)}, u32[]{:S(2)}) async-start(bf16[4,1024,256]{2,1,0:T(8,128)(2,1)} %bitcast.36), calls=%async_computation.8 | async-start | bytes 4194304 | tf_op jit(solution)/shard_map/all_to_all | solution.py:340
  321.1 56.6 %reduce-scatter.2.cloned.1.call-start = ((), (), s32[]{:S(2)}) async-start(), calls=%async_computation.10 | async-start | bytes 2621440 | tf_op jit(solution)/shard_map/reduce_scatter | solution.py:475
  344.9 29.5 %all-to-all-start.6 = ((bf16[4,1024,256]{2,1,0:T(8,128)(2,1)}), bf16[4,1024,256]{2,1,0:T(8,128)(2,1)}, u32[]{:S(2)}, u32[]{:S(2)}) async-start(bf16[4,1024,256]{2,1,0:T(8,128)(2,1)} %bitcast.35), calls=%async_computation.7 | async-start | bytes 4194304 | tf_op jit(solution)/shard_map/all_to_all | solution.py:340
Sparse Core Ops, SparseCore 0:
  67.4 18.2 all-gather.1
  327.4 31.1 reduce-scatter.1

commit v2 on v1

v2 whole, which is shorter than its diff:
```python
import functools

import jax
import jax.numpy as jnp
from jax import lax
from jax.experimental import pallas as pl
from jax.experimental.pallas import tpu as pltpu
from jax.sharding import PartitionSpec as P

HEAD_DIM = 64
PLEN = 256
INNER = 4
GROUP = 4
LANES = 128
NEG_LARGE = -1e30
SCALE = HEAD_DIM ** (-0.5)

BF16 = jnp.bfloat16
F32 = jnp.float32

VMEM_LIMIT = 56 * 1024 * 1024


def params(semantics=None):
    return pltpu.CompilerParams(vmem_limit_bytes=VMEM_LIMIT, dimension_semantics=semantics)


def dot_nt(a, b):
    return lax.dot_general(a, b, (((1,), (1,)), ((), ())), preferred_element_type=F32)


def dot_nn(a, b):
    return lax.dot_general(a, b, (((1,), (0,)), ((), ())), preferred_element_type=F32)


def dot_tn(a, b):
    return lax.dot_general(a, b, (((0,), (0,)), ((), ())), preferred_element_type=F32)


def cost_us(time):
    return pl.CostEstimate(flops=int(time * 1e9), bytes_accessed=0, transcendentals=0)


def project_kernel(x_ref, w_ref, o_ref):
    width = o_ref.shape[2]
    for block in range(INNER):
        cols = slice(block * width, (block + 1) * width)
        o_ref[block] = dot_nn(x_ref[...], w_ref[:, cols]).astype(BF16)


def project(x, w):
    rows, depth = x.shape
    cols = w.shape[1]
    tile = 256
    return pl.pallas_call(
        project_kernel,
        grid=(rows // tile,),
        in_specs=[
            pl.BlockSpec((tile, depth), lambda m: (m, 0)),
            pl.BlockSpec((depth, cols), lambda m: (0, 0)),
        ],
        out_specs=pl.BlockSpec((INNER, tile, cols // INNER), lambda m: (0, m, 0)),
        out_shape=jax.ShapeDtypeStruct((INNER, rows, cols // INNER), BF16),
        compiler_params=params(("arbitrary",)),
        cost_estimate=cost_us(14),
        name="project",
    )(x, w)


def two_heads(block):
    lane = lax.broadcasted_iota(jnp.int32, block.shape, 1)
    zero = jnp.zeros_like(block)
    return jnp.concatenate(
        [jnp.where(lane < HEAD_DIM, block, zero), jnp.where(lane >= HEAD_DIM, block, zero)], axis=0
    )


def own_blocks(full):
    rows = full.shape[1] // 2
    return jnp.concatenate([full[:HEAD_DIM, :rows], full[HEAD_DIM:, rows:]], axis=0)


def route_kernel(n_local, outer_ref, slot_ref, list_ref, count_ref, pick_ref, live_ref):
    n_q, list_len = list_ref.shape
    first_slot = outer_ref[0] * n_local

    def question(ident, carry):
        found = jnp.int32(0)
        for e in range(list_len):
            slot = slot_ref[list_ref[ident, e]] - first_slot
            here = (slot >= 0) & (slot < n_local) & (e < count_ref[ident])
            pick_ref[ident, found] = jnp.where(here, slot, 0)
            found = found + here.astype(jnp.int32)
        for e in range(GROUP):
            pick_ref[ident, found + e] = 0
        live_ref[ident] = found
        return carry

    lax.fori_loop(0, n_q, question, 0)


def each_group(pick_ref, live_ref, ident, entries):
    live = live_ref[ident]

    def group(step, carry):
        first = step * GROUP
        entries([(pick_ref[ident, first + j], first + j < live) for j in range(GROUP)])
        return carry

    lax.fori_loop(0, lax.div(live + (GROUP - 1), GROUP), group, 0)


def pair_lanes(pair):
    return slice(pair * LANES, (pair + 1) * LANES)


def stats_kernel(pick_ref, live_ref, k_ref, q_ref, o_ref, qbd):
    n_q = q_ref.shape[0]
    n_pair = q_ref.shape[2] // LANES

    def question(ident, carry):
        for pair in range(n_pair):
            qbd[pair] = two_heads(q_ref[ident, :, pair_lanes(pair)])
        o_ref[0, ident] = jnp.full(o_ref.shape[2:], NEG_LARGE, F32)
        o_ref[1, ident] = jnp.zeros(o_ref.shape[2:], F32)

        def entries(items):
            for pair in range(n_pair):
                row = slice(pair, pair + 1)
                scores = [dot_nt(k_ref[slot, :, pair_lanes(pair)], qbd[pair]) for slot, _ in items]
                old = o_ref[0, ident, row, :]
                new = old
                for (_, live), part in zip(items, scores):
                    top = jnp.max(part, axis=0, keepdims=True)
                    new = jnp.maximum(new, jnp.where(live, top, NEG_LARGE))
                add = o_ref[1, ident, row, :] * jnp.exp(old - new)
                for (_, live), part in zip(items, scores):
                    shift = jnp.where(live, new, -NEG_LARGE)
                    add = add + jnp.sum(jnp.exp(part - shift), axis=0, keepdims=True)
                o_ref[0, ident, row, :] = new
                o_ref[1, ident, row, :] = add

        each_group(pick_ref, live_ref, ident, entries)
        return carry

    lax.fori_loop(0, n_q, question, 0)


def value_grad_kernel(pick_ref, live_ref, k_ref, q_ref, g_ref, st_ref, o_ref, qbd, gbd, acc):
    n_q = q_ref.shape[0]
    n_pair = q_ref.shape[2] // LANES
    acc[...] = jnp.zeros_like(acc)

    def question(ident, carry):
        for pair in range(n_pair):
            qbd[pair] = two_heads(q_ref[ident, :, pair_lanes(pair)])
            gbd[pair] = two_heads(g_ref[ident, :, pair_lanes(pair)])

        def entries(items):
            for pair in range(n_pair):
                row = slice(pair, pair + 1)
                for slot, live in items:
                    shift = jnp.where(live, st_ref[0, ident, row, :], -NEG_LARGE)
                    scores = dot_nt(k_ref[slot, :, pair_lanes(pair)], qbd[pair])
                    probs = jnp.exp(scores - shift) * st_ref[1, ident, row, :]
                    term = dot_nn(probs.astype(BF16), gbd[pair]).astype(BF16)
                    acc[slot, :, pair_lanes(pair)] += term.astype(F32)

        each_group(pick_ref, live_ref, ident, entries)
        return carry

    lax.fori_loop(0, n_q, question, 0)

    def finish(slot, carry):
        o_ref[slot] = acc[slot].astype(BF16)
        return carry

    lax.fori_loop(0, k_ref.shape[0], finish, 0)


def turn(src_ref, dst_ref):
    def one(slot, carry):
        dst_ref[slot] = jnp.transpose(src_ref[slot])
        return carry

    lax.fori_loop(0, src_ref.shape[0], one, 0)


def context_kernel(n_outer, pick_ref, live_ref, outer_ref, k_ref, v_ref, q_ref, st_ref, *rest):
    o_refs, (qbd, vt) = rest[:n_outer], rest[n_outer:]
    n_q = q_ref.shape[0]
    inner = n_q // n_outer
    n_pair = q_ref.shape[2] // LANES
    turn(v_ref, vt)

    def question(o_ref, outer, index, carry):
        ident = outer * inner + index
        for pair in range(n_pair):
            qbd[pair] = two_heads(q_ref[ident, :, pair_lanes(pair)])
        zero = jnp.zeros((LANES, 2 * q_ref.shape[1]), F32)

        def group(step, sums):
            out = []
            for pair in range(n_pair):
                total = sums[pair]
                row = slice(pair, pair + 1)
                for j in range(GROUP):
                    at = step * GROUP + j
                    slot = pick_ref[ident, at]
                    shift = jnp.where(at < live_ref[ident], st_ref[0, ident, row, :], -NEG_LARGE)
                    scores = dot_nt(k_ref[slot, :, pair_lanes(pair)], qbd[pair])
                    weights = jnp.exp(scores - shift).astype(BF16)
                    total = total + dot_nn(vt[slot, pair_lanes(pair), :], weights)
                out.append(total)
            return tuple(out)

        steps = lax.div(live_ref[ident] + (GROUP - 1), GROUP)
        sums = lax.fori_loop(0, steps, group, (zero,) * n_pair)
        for pair in range(n_pair):
            o_ref[index, pair_lanes(pair), :] = own_blocks(sums[pair])
        return carry

    for r in reversed(range(n_outer)):
        outer = lax.rem(outer_ref[0] + r, n_outer)
        lax.fori_loop(0, inner, functools.partial(question, o_refs[r], outer), 0)


def score_grad_kernel(n_outer, pick_ref, live_ref, outer_ref, k_ref, v_ref, q_ref, g_ref, st_ref, *rest):
    dot_refs, rest = rest[:n_outer], rest[n_outer:]
    dk_ref, rest = rest[0], rest[1:]
    dq_refs, (qbd, gbd, kt, acc_k) = rest[:n_outer], rest[n_outer:]
    n_q = q_ref.shape[0]
    inner = n_q // n_outer
    n_pair = q_ref.shape[2] // LANES
    turn(k_ref, kt)
    acc_k[...] = jnp.zeros_like(acc_k)

    def question(dot_ref, dq_ref, outer, index, carry):
        ident = outer * inner + index
        for pair in range(n_pair):
            qbd[pair] = two_heads(q_ref[ident, :, pair_lanes(pair)])
            gbd[pair] = two_heads(g_ref[ident, :, pair_lanes(pair)])
        zero = jnp.zeros((LANES, 2 * q_ref.shape[1]), F32)

        def group(step, sums):
            out = []
            for pair in range(n_pair):
                total = sums[pair]
                row = slice(pair, pair + 1)
                for j in range(GROUP):
                    at = step * GROUP + j
                    slot = pick_ref[ident, at]
                    shift = jnp.where(at < live_ref[ident], st_ref[0, ident, row, :], -NEG_LARGE)
                    scores = dot_nt(k_ref[slot, :, pair_lanes(pair)], qbd[pair])
                    probs = jnp.exp(scores - shift) * st_ref[1, ident, row, :]
                    dprob = dot_nt(v_ref[slot, :, pair_lanes(pair)], gbd[pair])
                    dscore = (probs * (dprob - dot_ref[index, row, :])).astype(BF16)
                    term = dot_nn(dscore, qbd[pair]).astype(BF16)
                    acc_k[slot, :, pair_lanes(pair)] += term.astype(F32)
                    total = total + dot_nn(kt[slot, pair_lanes(pair), :], dscore)
                out.append(total)
            return tuple(out)

        steps = lax.div(live_ref[ident] + (GROUP - 1), GROUP)
        sums = lax.fori_loop(0, steps, group, (zero,) * n_pair)
        for pair in range(n_pair):
            dq_ref[index, pair_lanes(pair), :] = own_blocks(sums[pair])
        return carry

    for r in reversed(range(n_outer)):
        outer = lax.rem(outer_ref[0] + r, n_outer)
        lax.fori_loop(0, inner, functools.partial(question, dot_refs[r], dq_refs[r], outer), 0)

    def finish(slot, carry):
        dk_ref[slot] = acc_k[slot].astype(BF16)
        return carry

    lax.fori_loop(0, k_ref.shape[0], finish, 0)


def merge_kernel(n_outer, *refs):
    parts, o_ref = refs[:n_outer], refs[n_outer]
    top = parts[0][0]
    for part in parts[1:]:
        top = jnp.maximum(top, part[0])
    total = parts[0][1] * jnp.exp(parts[0][0] - top)
    for part in parts[1:]:
        total = total + part[1] * jnp.exp(part[0] - top)
    o_ref[0] = top
    o_ref[1] = 1.0 / total
    o_ref[2] = total


def combine_context_kernel(n_parts, outer_ref, *refs):
    parts, (st_ref, g_ref, o_ref, dot_ref) = refs[:n_parts], refs[n_parts:]
    width = g_ref.shape[2]
    inner = o_ref.shape[0]
    first = outer_ref[0] * inner
    for q in range(inner):
        mix = parts[0][q]
        for part in parts[1:]:
            mix = mix + part[q]
        grad = jnp.transpose(g_ref[first + q].astype(F32))
        rows = mix.shape[1]
        pieces = []
        for head in range(width // HEAD_DIM):
            feats = slice(head * HEAD_DIM, (head + 1) * HEAD_DIM)
            pair, lanes = head // 2, slice((head % 2) * rows, (head % 2 + 1) * rows)
            total = st_ref[2, first + q, pair : pair + 1, lanes]
            ctx = (mix[feats] / total).astype(BF16).astype(F32)
            dot_ref[q, pair : pair + 1, lanes] = jnp.sum(grad[feats] * ctx, axis=0, keepdims=True)
            pieces.append(ctx)
        o_ref[q] = jnp.transpose(jnp.concatenate(pieces, axis=0)).astype(BF16)


def combine_query_kernel(n_parts, *refs):
    parts, o_ref = refs[:n_parts], refs[n_parts]
    for q in range(o_ref.shape[0]):
        mix = parts[0][q]
        for part in parts[1:]:
            mix = mix + part[q]
        o_ref[q] = jnp.transpose(mix * SCALE).astype(BF16)


def spread_kernel(x_ref, o_ref):
    width = o_ref.shape[2]
    for block in range(INNER):
        part = x_ref[:, block * width : (block + 1) * width] * jnp.asarray(SCALE, BF16)
        for outer in range(o_ref.shape[0] // INNER):
            o_ref[outer * INNER + block] = part


def context_grad_kernel(x_ref, w_ref, o_ref):
    part = dot_nt(x_ref[...], w_ref[...]).astype(BF16)
    for outer in range(o_ref.shape[0]):
        o_ref[outer, 0] = part


def context_grad_blocks(x, w, n_outer, width):
    rows, depth = x.shape
    return pl.pallas_call(
        context_grad_kernel,
        grid=(INNER,),
        in_specs=[
            pl.BlockSpec((rows, depth), lambda j: (0, 0)),
            pl.BlockSpec((width, depth), lambda j: (j, 0)),
        ],
        out_specs=pl.BlockSpec((n_outer, 1, rows, width), lambda j: (0, j, 0, 0)),
        out_shape=jax.ShapeDtypeStruct((n_outer, INNER, rows, width), BF16),
        compiler_params=params(("arbitrary",)),
        cost_estimate=cost_us(5),
        name="context_grad",
    )(x, w)


def out_project_kernel(x_ref, w_ref, o_ref):
    step = pl.program_id(0)
    part = dot_nn(x_ref[0], w_ref[...])

    @pl.when(step == 0)
    def _():
        o_ref[...] = part

    @pl.when(step > 0)
    def _():
        o_ref[...] += part


def out_project(x, w):
    blocks, rows, width = x.shape
    cols = w.shape[1]
    return pl.pallas_call(
        out_project_kernel,
        grid=(blocks,),
        in_specs=[
            pl.BlockSpec((1, rows, width), lambda j: (j, 0, 0)),
            pl.BlockSpec((width, cols), lambda j: (j, 0)),
        ],
        out_specs=pl.BlockSpec((rows, cols), lambda j: (0, 0)),
        out_shape=jax.ShapeDtypeStruct((rows, cols), F32),
        compiler_params=params(("arbitrary",)),
        cost_estimate=cost_us(5),
        name="out_project",
    )(x, w)


def vmem_call(kernel, scalars, arrays, out_shape, scratch, time, name):
    smem = pl.BlockSpec(memory_space=pltpu.SMEM)
    vmem = pl.BlockSpec(memory_space=pltpu.VMEM)
    return pl.pallas_call(
        kernel,
        in_specs=[smem] * len(scalars) + [vmem] * len(arrays),
        out_specs=jax.tree.map(lambda _: vmem, out_shape),
        out_shape=out_shape,
        scratch_shapes=scratch,
        compiler_params=params(),
        cost_estimate=cost_us(time),
        name=name,
    )(*scalars, *arrays)


def route(outer, slot_of, passage_lists, list_counts, n_local):
    smem = pl.BlockSpec(memory_space=pltpu.SMEM)
    n_q, list_len = passage_lists.shape
    return pl.pallas_call(
        functools.partial(route_kernel, n_local),
        in_specs=[smem] * 4,
        out_specs=(smem, smem),
        out_shape=(
            jax.ShapeDtypeStruct((n_q, list_len + GROUP), jnp.int32),
            jax.ShapeDtypeStruct((n_q,), jnp.int32),
        ),
        cost_estimate=cost_us(3),
        name="route",
    )(outer, slot_of, passage_lists, list_counts)


def after(value, *others):
    return lax.optimization_barrier((value,) + others)[0]


def body(
    queries,
    encoded,
    key_weight,
    value_weight,
    out_weight,
    out_grad,
    slot_of,
    passage_lists,
    list_counts,
):
    head_width = key_weight.shape[1]
    rows = queries.shape[0]
    tok_local = encoded.shape[0]
    n_pas = lax.axis_size("pas")
    inner = INNER
    n_outer = n_pas // inner
    width = head_width // inner
    n_pair = width // LANES
    n_local = inner * (tok_local // PLEN)
    n_q = n_pas
    outer = (lax.axis_index("pas") // inner).astype(jnp.int32).reshape(1)
    groups = [[o * inner + i for i in range(inner)] for o in range(n_outer)]
    sds = jax.ShapeDtypeStruct

    def swap(x):
        return lax.all_to_all(
            x, "pas", split_axis=0, concat_axis=0, tiled=True, axis_index_groups=groups
        )

    def swap_all(x):
        return lax.all_to_all(x, "pas", split_axis=0, concat_axis=0, tiled=True)

    def to_outer(x, r):
        return lax.ppermute(
            x,
            "pas",
            [(o * inner + i, ((o + r) % n_outer) * inner + i) for o in range(n_outer) for i in range(inner)],
        )

    def from_block(x):
        return jnp.transpose(x, (1, 0, 2)).reshape(x.shape[1], head_width)

    def partials(parts):
        return [parts[0]] + [to_outer(parts[r], r) for r in range(1, n_outer)]

    q_spread = vmem_call(spread_kernel, (), (queries,), sds((n_q, rows, width), BF16), [], 1.5, "spread")
    q_all = swap_all(q_spread)
    grad_rows = lax.all_gather(out_grad, "head", axis=1, tiled=True)

    key_part = project(after(encoded, q_spread), key_weight)
    keys = swap(key_part).reshape(n_local, PLEN, width)
    value_part = project(after(encoded, key_part), value_weight)
    values = swap(value_part).reshape(n_local, PLEN, width)
    g_spread = context_grad_blocks(after(grad_rows, value_part), out_weight, n_outer, width)
    g_spread = g_spread.reshape(n_q, rows, width)
    g_all = swap_all(g_spread)

    pick, live = route(outer, slot_of, passage_lists, list_counts, n_local)
    pair_scratch = pltpu.VMEM((n_pair, 2 * rows, LANES), BF16)
    acc_scratch = pltpu.VMEM((n_local, PLEN, width), F32)
    turned = pltpu.VMEM((n_local, width, PLEN), BF16)
    stat_shape = (n_q, n_pair, 2 * rows)
    mix_shape = (sds((inner, width, rows), F32),) * n_outer

    stats = vmem_call(
        stats_kernel,
        (pick, live),
        (keys, after(q_all, g_spread)),
        sds((2,) + stat_shape, F32),
        [pair_scratch],
        14,
        "stats",
    )
    norm = vmem_call(
        functools.partial(merge_kernel, n_outer),
        (),
        [stats] + [to_outer(stats, r) for r in range(1, n_outer)],
        sds((3,) + stat_shape, F32),
        [],
        1,
        "merge",
    )
    mixes = vmem_call(
        functools.partial(context_kernel, n_outer),
        (pick, live, outer),
        (keys, values, q_all, norm),
        mix_shape,
        [pair_scratch, turned],
        22,
        "context",
    )
    value_done = vmem_call(
        value_grad_kernel,
        (pick, live),
        (keys, q_all, g_all, after(norm, mixes[0])),
        sds((n_local, PLEN, width), BF16),
        [pair_scratch, pair_scratch, acc_scratch],
        20,
        "value_grad",
    )
    context, grad_dot = vmem_call(
        functools.partial(combine_context_kernel, n_outer),
        (outer,),
        partials(mixes) + [after(norm, value_done), g_all],
        (sds((inner, rows, width), BF16), sds((inner, n_pair, 2 * rows), F32)),
        [],
        2,
        "combine_context",
    )
    dots = [grad_dot] + [to_outer(grad_dot, n_outer - r) for r in range(1, n_outer)]
    projected = out_project(swap(context), out_weight)
    value_back = swap(value_done.reshape(inner, tok_local, width))
    output = lax.psum_scatter(projected, "head", scatter_dimension=1, tiled=True).astype(BF16)
    done = vmem_call(
        functools.partial(score_grad_kernel, n_outer),
        (pick, live, outer),
        [keys, values, q_all, g_all, after(norm, projected)] + dots,
        (sds((n_local, PLEN, width), BF16),) + mix_shape,
        [pair_scratch, pair_scratch, turned, acc_scratch],
        36,
        "score_grad",
    )
    key_back = swap(after(done[0], value_back).reshape(inner, tok_local, width))
    query_done = vmem_call(
        functools.partial(combine_query_kernel, n_outer),
        (),
        [after(done[1], output)] + partials(done[1:])[1:],
        sds((inner, rows, width), BF16),
        [],
        2,
        "combine_query",
    )
    query_grad = from_block(swap(after(query_done, key_back)))
    key_grad, value_grad = from_block(key_back), from_block(value_back)
    return (output, query_grad, key_grad, value_grad)


def solution(mesh):
    in_specs = (
        P("pas", "head"),
        P("pas", None),
        P(None, "head"),
        P(None, "head"),
        P("head", None),
        P("pas", "head"),
        P(),
        P(),
        P(),
    )
    out_specs = (P("pas", "head"), P("pas", "head"), P("pas", "head"), P("pas", "head"))
    return jax.shard_map(body, mesh=mesh, in_specs=in_specs, out_specs=out_specs, check_vma=False)
```

time: 390 us -> 268 us (0.69)
  waiting for transfers between devices: 124 us -> 44.2 us
  Pallas kernels: 172 us -> 141 us
  matrix products: 12.6 us -> 0 us
  starting transfers between devices: 42.1 us -> 53.1 us
  local copies, waits for them, and re-layouts: 16.9 us -> 12.2 us
    pallas_call x6 -> x8, Pallas kernels: 139 us -> 96.9 us  [vmem_call(): pl.pallas_call(kernel, in_specs=[smem] * len(scalars) + [vmem] * len(arra...]
    all_to_all x8 -> x6, waiting for transfers between devices: 48.1 us -> 12.5 us  [swap(): lax.all_to_all(x, 'pas', split_axis=0, concat_axis=0, tiled=True, axis_in...]
    ppermute x4 -> x0, waiting for transfers between devices: 29 us -> none  [from_outer(): lax.ppermute(x, 'pas', [((o + r) % n_outer * inner + i, o * inner + i) fo...]
    ppermute x2 -> x4, waiting for transfers between devices: 46.3 us -> 30.6 us  [to_outer(): lax.ppermute(x, 'pas', [(o * inner + i, (o + r) % n_outer * inner + i) fo...]
    all_to_all x0 -> x2, starting transfers between devices: none -> 13.6 us  [swap_all(): return lax.all_to_all(x, 'pas', split_axis=0, concat_axis=0, tiled=True)]
    dot_general x2 -> x0, matrix products: 12.6 us -> none  [the longest x1 6.62 us: body(): lax.dot_general(lax.all_gather(out_grad, 'head', axis=1, tiled=True), out...]
    pallas_call x2 -> x5, Pallas kernels: 32.6 us -> 44.1 us  [the longest x2 28.4 us: project(): pl.pallas_call(project_kernel, grid=(rows // tile,), in_specs=[pl.BlockSp...]
    ppermute x2 -> x4, starting transfers between devices: 2.29 us -> 11.5 us  [to_outer(): lax.ppermute(x, 'pas', [(o * inner + i, (o + r) % n_outer * inner + i) fo...]
  transfers between devices with their start and end apart: 16 -> 14, of which waited for: 8 -> 7; matrix products, arithmetic and copies ran while one was open for 6% -> 2% of each run, Pallas kernels for 34% -> 51%
where the time goes in v2:
time: 268 us; the launch traced here: 266 us
  Pallas kernels  141 us (53%)
  starting transfers between devices  53.1 us (20%)
  waiting for transfers between devices  44.2 us (16%)
  between operations  14.2 us (5%)
  local copies, waits for them, and re-layouts  12.2 us (5%)
    pallas_call x8, Pallas kernels, vmem_call(): pl.pallas_call(kernel, in_specs=[smem] * len(scalars) + [vmem] * len(arra...  96.9 us
    ppermute x4, waiting for transfers between devices, to_outer(): lax.ppermute(x, 'pas', [(o * inner + i, (o + r) % n_outer * inner + i) fo...  30.6 us
    pallas_call x2, Pallas kernels, project(): pl.pallas_call(project_kernel, grid=(rows // tile,), in_specs=[pl.BlockSp...  28.4 us
    all_to_all x6, starting transfers between devices, swap(): lax.all_to_all(x, 'pas', split_axis=0, concat_axis=0, tiled=True, axis_in...  27.8 us
    all_to_all x2, starting transfers between devices, swap_all(): return lax.all_to_all(x, 'pas', split_axis=0, concat_axis=0, tiled=True)  13.6 us
    all_to_all x6, waiting for transfers between devices, swap(): lax.all_to_all(x, 'pas', split_axis=0, concat_axis=0, tiled=True, axis_in...  12.5 us
    ppermute x4, starting transfers between devices, to_outer(): lax.ppermute(x, 'pas', [(o * inner + i, (o + r) % n_outer * inner + i) fo...  11.5 us
    unnamed x19, local copies, waits for them, and re-layouts  7.27 us
  transfers between devices with their start and end apart: 14, of which 7 were waited for; matrix products, arithmetic and copies ran while one was open for 2% of the time, Pallas kernels for 51%

profile of v2, /device:TPU:0, one launch (start us, length us, event | category | flops | bytes accessed | tf_op | source)
XLA Modules:
  0.0 266.5 jit_solution(13664651362285965814)
XLA Ops:
  7.2 1.8 spread.1
  8.9 7.3 %all-to-all-start.2 = ((bf16[8,128,256]{2,1,0:T(8,128)(2,1)}), bf16[8,128,256]{2,1,0:T(8,128)(2,1)S(1)}, u32[]{:S(2)}, u32[]{:S(2)}) async-start(bf16[8,128,256]{2,1,0:T(8,128)(2,1)} %spread.1), calls=%async_computation.2 | async-start | bytes 1048576 | tf_op jit(solution)/shard_map/all_to_all | solution.py:453
  16.2 14.2 %project.2 = bf16[4,1024,256]{2,1,0:T(8,128)(2,1)} custom-call(bf16[1024,4096]{1,0:T(8,128)(2,1)} %x_ref.3, bf16[4096,1024]{1,0:T(8,128)(2,1)} %w_ref.4), custom_call_target="tpu_custom_call" | custom-call | flops 14000000000 | tf_op jit(solution)/shard_map/project/pallas_call | solution.py:55
  30.4 0.3 all-to-all-done.2.q_ref
  30.7 0.8 copy-done.1
  31.5 3.9 %all-to-all-start = ((bf16[4,1024,256]{2,1,0:T(8,128)(2,1)}), bf16[4,1024,256]{2,1,0:T(8,128)(2,1)S(1)}, u32[]{:S(2)}, u32[]{:S(2)}) async-start(bf16[4,1024,256]{2,1,0:T(8,128)(2,1)} %project.2), calls=%async_computation | async-start | bytes 4194304 | tf_op jit(solution)/shard_map/all_to_all | solution.py:448
  35.4 0.7 all-gather.2.cloned.1.call-update
  36.1 14.2 %project.3 = bf16[4,1024,256]{2,1,0:T(8,128)(2,1)} custom-call(bf16[1024,4096]{1,0:T(8,128)(2,1)} %x_ref.3, bf16[4096,1024]{1,0:T(8,128)(2,1)} %w_ref.5), custom_call_target="tpu_custom_call" | custom-call | flops 14000000000 | tf_op jit(solution)/shard_map/project/pallas_call | solution.py:55
  50.3 9.4 %all-to-all-done = bf16[4,1024,256]{2,1,0:T(8,128)(2,1)S(1)} async-done(((bf16[4,1024,256]{2,1,0:T(8,128)(2,1)}), bf16[4,1024,256]{2,1,0:T(8,128)(2,1)S(1)}, u32[]{:S(2)}, u32[]{:S(2)}) %all-to-all-start) | async-done | bytes 2097184 | tf_op jit(solution)/shard_map/all_to_all | solution.py:448
  59.7 1.3 copy-done
  61.0 4.5 %all-to-all-start.1 = ((bf16[4,1024,256]{2,1,0:T(8,128)(2,1)}), bf16[4,1024,256]{2,1,0:T(8,128)(2,1)}, u32[]{:S(2)}, u32[]{:S(2)}) async-start(bf16[4,1024,256]{2,1,0:T(8,128)(2,1)} %project.3), calls=%async_computation.1 | async-start | bytes 4194304 | tf_op jit(solution)/shard_map/all_to_all | solution.py:448
  65.5 2.2 route.1
  67.7 0.0 all-gather.2.cloned.1.call-done.x_ref
  67.8 6.8 %context_grad.1 = bf16[2,4,128,256]{3,2,1,0:T(8,128)(2,1)} custom-call(bf16[128,4096]{1,0:T(8,128)(2,1)} %all-gather.2.cloned.1.call-done.x_ref, bf16[1024,4096]{1,0:T(8,128)(2,1)} %w_ref.7), custom_call_target="tpu_custom_call" | custom-call | flops 5000000000 | tf_op jit(solution)/shard_map/context_grad/pallas_call | solution.py:341
  74.6 14.3 %stats.1.refs_0_ = f32[2,8,2,256]{3,2,1,0:T(2,128)} custom-call(s32[8,20]{1,0:T(8,128)} %get-tuple-element.23.pick_ref, s32[8]{0:T(128)} %get-tuple-element.24.live_ref, bf16[16,256,256]{2,1,0:T(8,128)(2,1)} %bitcast.15, bf16[8,128,256]{2,1,0:T(8,128)(2,1)} %copy-done.1), custom_call_target="tpu_custom_call" | custom-call | flops 14000000000 | tf_op jit(solution)/shard_map/stats/pallas_call | solution.py:390
  88.8 2.6 collective-permute-start
  91.4 2.6 collective-permute-done.refs_1_
  94.1 0.6 copy-done.7
  94.7 1.4 merge.1.st_ref.refs_2_
  96.1 6.3 %all-to-all-start.3 = ((bf16[8,128,256]{2,1,0:T(8,128)(2,1)}), bf16[8,128,256]{2,1,0:T(8,128)(2,1)S(1)}, u32[]{:S(2)}, u32[]{:S(2)}) async-start(bf16[8,128,256]{2,1,0:T(8,128)(2,1)} %bitcast.3), calls=%async_computation.3 | async-start | bytes 1048576 | tf_op jit(solution)/shard_map/all_to_all | solution.py:453
  102.4 21.2 %context.1 = (f32[4,256,128]{2,1,0:T(8,128)}, f32[4,256,128]{2,1,0:T(8,128)}) custom-call(s32[8,20]{1,0:T(8,128)} %get-tuple-element.23.pick_ref, s32[8]{0:T(128)} %get-tuple-element.24.live_ref, s32[1]{0:T(128)} %bitcast.outer_ref, bf16[16,256,256]{2,1,0:T(8,128)(2,1)} %bitcast.16, bf16[16,256,256]{2,1,0:T(8,128)(2,1)} %bitcast.2.v_ref, ...), custom_call_target="tpu_custom_call" | custom-call | flops 22000001024 | tf_op jit(solution)/shard_map/context/pallas_call | solution.py:390
  123.6 2.9 %collective-permute-start.1 = (f32[4,256,128]{2,1,0:T(8,128)}, f32[4,256,128]{2,1,0:T(8,128)S(1)}, u32[]{:S(2)}, u32[]{:S(2)}) collective-permute-start(f32[4,256,128]{2,1,0:T(8,128)} %get-tuple-element.30), channel_id=1, source_target_pairs={{0,16},{4,20},{8,24},{12,28},{16,0},{20,4},{24,8},{28,12},{1,17},{... | collective-permute-start | bytes 1572872 | tf_op jit(solution)/shard_map/ppermute | solution.py:456
  126.5 0.8 copy-done.2
  127.3 19.3 %value_grad.1 = bf16[16,256,256]{2,1,0:T(8,128)(2,1)} custom-call(s32[8,20]{1,0:T(8,128)} %get-tuple-element.23.pick_ref, s32[8]{0:T(128)} %get-tuple-element.24.live_ref, bf16[16,256,256]{2,1,0:T(8,128)(2,1)} %bitcast.17, bf16[8,128,256]{2,1,0:T(8,128)(2,1)} %copy-done.1, bf16[8,128,256]{2,1,0:T(8,128)(2,1)} %copy-done.2, f32[3,8,2,256]{3,2,1,0:T(2,128)} %merge.1.st_ref.refs_2_), custom_call_target="tpu_custom_call" | custom-call | flops 20000000000 | tf_op jit(solution)/shard_map/value_grad/pallas_call | solution.py:390
  146.6 0.5 collective-permute-done.1.refs_1_
  147.1 0.8 copy-done.5
  147.9 2.3 combine_context.1
  150.2 3.4 %all-to-all-start.4 = ((bf16[4,128,256]{2,1,0:T(8,128)(2,1)}), bf16[4,128,256]{2,1,0:T(8,128)(2,1)S(1)}, u32[]{:S(2)}, u32[]{:S(2)}) async-start(bf16[4,128,256]{2,1,0:T(8,128)(2,1)} %get-tuple-element.33), calls=%async_computation.4 | async-start | bytes 524288 | tf_op jit(solution)/shard_map/all_to_all | solution.py:448
  153.6 2.9 %collective-permute-start.2 = (f32[4,2,256]{2,1,0:T(2,128)}, f32[4,2,256]{2,1,0:T(2,128)S(1)}, u32[]{:S(2)}, u32[]{:S(2)}) collective-permute-start(f32[4,2,256]{2,1,0:T(2,128)} %get-tuple-element.35.rest_0_), channel_id=1, source_target_pairs={{0,16},{4,20},{8,24},{12,28},{16,0},{20,4},{24,8},{28,12},{1,17},{... | collective-permute-start | bytes 24584 | tf_op jit(solution)/shard_map/ppermute | solution.py:456
  156.5 2.6 all-to-all-done.4.x_ref
  159.0 0.7 copy-done.3
  159.7 3.6 %all-to-all-start.5 = ((bf16[4,1024,256]{2,1,0:T(8,128)(2,1)}), bf16[4,1024,256]{2,1,0:T(8,128)(2,1)S(1)}, u32[]{:S(2)}, u32[]{:S(2)}) async-start(bf16[4,1024,256]{2,1,0:T(8,128)(2,1)} %bitcast.19), calls=%async_computation.6 | async-start | bytes 4194304 | tf_op jit(solution)/shard_map/all_to_all | solution.py:448
  163.3 0.2 reduce-scatter.2.cloned.1.call-start
  163.6 6.7 %out_project.1 = f32[128,4096]{1,0:T(8,128)} custom-call(bf16[4,128,256]{2,1,0:T(8,128)(2,1)} %copy-done.3, bf16[1024,4096]{1,0:T(8,128)(2,1)} %w_ref.7), custom_call_target="tpu_custom_call" | custom-call | flops 5000000000 | tf_op jit(solution)/shard_map/out_project/pallas_call | solution.py:372
  170.3 0.6 copy-done.8
  170.9 34.6 %score_grad.1 = (bf16[16,256,256]{2,1,0:T(8,128)(2,1)}, f32[4,256,128]{2,1,0:T(8,128)}, f32[4,256,128]{2,1,0:T(8,128)}) custom-call(s32[8,20]{1,0:T(8,128)} %get-tuple-element.23.pick_ref, s32[8]{0:T(128)} %get-tuple-element.24.live_ref, s32[1]{0:T(128)} %bitcast.outer_ref, bf16[16,256,256]{2,1,0:T(8,128)(2,1)} %bitcast.18, ...), custom_call_target="tpu_custom_call" | custom-call | flops 35999997952 | tf_op jit(solution)/shard_map/score_grad/pallas_call | solution.py:390
  205.5 4.6 %all-to-all-start.6 = ((bf16[4,1024,256]{2,1,0:T(8,128)(2,1)}), bf16[4,1024,256]{2,1,0:T(8,128)(2,1)}, u32[]{:S(2)}, u32[]{:S(2)}) async-start(bf16[4,1024,256]{2,1,0:T(8,128)(2,1)} %bitcast.20), calls=%async_computation.7 | async-start | bytes 4194304 | tf_op jit(solution)/shard_map/all_to_all | solution.py:448
  210.1 3.1 %collective-permute-start.3 = (f32[4,256,128]{2,1,0:T(8,128)S(1)}, f32[4,256,128]{2,1,0:T(8,128)S(1)}, u32[]{:S(2)}, u32[]{:S(2)}) collective-permute-start(f32[4,256,128]{2,1,0:T(8,128)S(1)} %copy-done.4), channel_id=1, source_target_pairs={{0,16},{4,20},{8,24},{12,28},{16,0},{20,4},{24,8},{28,12},{1,17},{... | collective-permute-start | bytes 1572872 | tf_op jit(solution)/shard_map/ppermute | solution.py:456
  213.2 1.8 convert_element_type.3
  215.0 27.5 %collective-permute-done.3.refs_1_ = f32[4,256,128]{2,1,0:T(8,128)S(1)} collective-permute-done((f32[4,256,128]{2,1,0:T(8,128)S(1)}, f32[4,256,128]{2,1,0:T(8,128)S(1)}, u32[]{:S(2)}, u32[]{:S(2)}) %collective-permute-start.3) | collective-permute-done | bytes 524320 | tf_op jit(solution)/shard_map/ppermute | solution.py:456
  242.6 0.8 copy-done.6
  243.3 2.0 combine_query.1
  245.4 7.9 %all-to-all-start.7 = ((bf16[4,128,256]{2,1,0:T(8,128)(2,1)}), bf16[4,128,256]{2,1,0:T(8,128)(2,1)S(1)}, u32[]{:S(2)}, u32[]{:S(2)}) async-start(bf16[4,128,256]{2,1,0:T(8,128)(2,1)} %combine_query.1), calls=%async_computation.8 | async-start | bytes 524288 | tf_op jit(solution)/shard_map/all_to_all | solution.py:448
  253.3 1.6 copy.20
  254.9 3.2 %copy.19 = bf16[4,128,8,256]{3,2,0,1:T(8,128)(2,1)} copy(bf16[4,128,8,256]{3,2,1,0:T(8,128)(2,1)} %bitcast.10) | data formatting | bytes 4194304 | tf_op jit(solution)/shard_map/reshape | solution.py:463
  258.1 0.6 all-to-all-done.7
  258.6 0.2 copy.15
  258.8 0.9 copy.18
  (18 shorter events, 0.1 us)
Async XLA Ops:
  8.9 21.8 %all-to-all-start.2 = ((bf16[8,128,256]{2,1,0:T(8,128)(2,1)}), bf16[8,128,256]{2,1,0:T(8,128)(2,1)S(1)}, u32[]{:S(2)}, u32[]{:S(2)}) async-start(bf16[8,128,256]{2,1,0:T(8,128)(2,1)} %spread.1), calls=%async_computation.2 | async-start | bytes 1048576 | tf_op jit(solution)/shard_map/all_to_all | solution.py:453
  30.7 0.8 copy-start.1
  31.5 28.2 %all-to-all-start = ((bf16[4,1024,256]{2,1,0:T(8,128)(2,1)}), bf16[4,1024,256]{2,1,0:T(8,128)(2,1)S(1)}, u32[]{:S(2)}, u32[]{:S(2)}) async-start(bf16[4,1024,256]{2,1,0:T(8,128)(2,1)} %project.2), calls=%async_computation | async-start | bytes 4194304 | tf_op jit(solution)/shard_map/all_to_all | solution.py:448
  35.4 32.3 %all-gather.2.cloned.1.call-start = ((), (), s32[]{:S(2)}) async-start(), calls=%async_computation.9 | async-start | bytes 1310720 | tf_op jit(solution)/shard_map/all_gather | solution.py:470
  59.7 1.3 copy-start
  61.0 35.1 %all-to-all-start.1 = ((bf16[4,1024,256]{2,1,0:T(8,128)(2,1)}), bf16[4,1024,256]{2,1,0:T(8,128)(2,1)}, u32[]{:S(2)}, u32[]{:S(2)}) async-start(bf16[4,1024,256]{2,1,0:T(8,128)(2,1)} %project.3), calls=%async_computation.1 | async-start | bytes 4194304 | tf_op jit(solution)/shard_map/all_to_all | solution.py:448
  88.8 5.2 %collective-permute-start = (f32[2,8,2,256]{3,2,1,0:T(2,128)}, f32[2,8,2,256]{3,2,1,0:T(2,128)S(1)}, u32[]{:S(2)}, u32[]{:S(2)}) collective-permute-start(f32[2,8,2,256]{3,2,1,0:T(2,128)} %stats.1.refs_0_), channel_id=1, source_target_pairs={{0,16},{4,20},{8,24},{12,28},{16,0},{20,4},{24,8},{28,12},{1,17},{... | collective-permute-start | bytes 98312 | tf_op jit(solution)/shard_map/ppermute | solution.py:456
  94.1 0.6 copy-start.7
  96.1 30.4 %all-to-all-start.3 = ((bf16[8,128,256]{2,1,0:T(8,128)(2,1)}), bf16[8,128,256]{2,1,0:T(8,128)(2,1)S(1)}, u32[]{:S(2)}, u32[]{:S(2)}) async-start(bf16[8,128,256]{2,1,0:T(8,128)(2,1)} %bitcast.3), calls=%async_computation.3 | async-start | bytes 1048576 | tf_op jit(solution)/shard_map/all_to_all | solution.py:453
  123.6 23.5 %collective-permute-start.1 = (f32[4,256,128]{2,1,0:T(8,128)}, f32[4,256,128]{2,1,0:T(8,128)S(1)}, u32[]{:S(2)}, u32[]{:S(2)}) collective-permute-start(f32[4,256,128]{2,1,0:T(8,128)} %get-tuple-element.30), channel_id=1, source_target_pairs={{0,16},{4,20},{8,24},{12,28},{16,0},{20,4},{24,8},{28,12},{1,17},{... | collective-permute-start | bytes 1572872 | tf_op jit(solution)/shard_map/ppermute | solution.py:456
  126.5 0.8 copy-start.2
  147.1 0.8 copy-start.5
  150.2 8.8 %all-to-all-start.4 = ((bf16[4,128,256]{2,1,0:T(8,128)(2,1)}), bf16[4,128,256]{2,1,0:T(8,128)(2,1)S(1)}, u32[]{:S(2)}, u32[]{:S(2)}) async-start(bf16[4,128,256]{2,1,0:T(8,128)(2,1)} %get-tuple-element.33), calls=%async_computation.4 | async-start | bytes 524288 | tf_op jit(solution)/shard_map/all_to_all | solution.py:448
  153.6 16.7 %collective-permute-start.2 = (f32[4,2,256]{2,1,0:T(2,128)}, f32[4,2,256]{2,1,0:T(2,128)S(1)}, u32[]{:S(2)}, u32[]{:S(2)}) collective-permute-start(f32[4,2,256]{2,1,0:T(2,128)} %get-tuple-element.35.rest_0_), channel_id=1, source_target_pairs={{0,16},{4,20},{8,24},{12,28},{16,0},{20,4},{24,8},{28,12},{1,17},{... | collective-permute-start | bytes 24584 | tf_op jit(solution)/shard_map/ppermute | solution.py:456
  159.0 0.7 copy-start.3
  159.7 45.8 %all-to-all-start.5 = ((bf16[4,1024,256]{2,1,0:T(8,128)(2,1)}), bf16[4,1024,256]{2,1,0:T(8,128)(2,1)S(1)}, u32[]{:S(2)}, u32[]{:S(2)}) async-start(bf16[4,1024,256]{2,1,0:T(8,128)(2,1)} %bitcast.19), calls=%async_computation.6 | async-start | bytes 4194304 | tf_op jit(solution)/shard_map/all_to_all | solution.py:448
  163.3 49.9 %reduce-scatter.2.cloned.1.call-start = ((), (), s32[]{:S(2)}) async-start(), calls=%async_computation.10 | async-start | bytes 2621440 | tf_op jit(solution)/shard_map/reduce_scatter | solution.py:535
  170.3 0.6 copy-start.8
  205.5 4.6 %copy-start.4 = (f32[4,256,128]{2,1,0:T(8,128)S(1)}, f32[4,256,128]{2,1,0:T(8,128)}, u32[]{:S(2)}) copy-start(f32[4,256,128]{2,1,0:T(8,128)} %get-tuple-element.38) | copy-start | bytes 1572868
  205.5 39.9 %all-to-all-start.6 = ((bf16[4,1024,256]{2,1,0:T(8,128)(2,1)}), bf16[4,1024,256]{2,1,0:T(8,128)(2,1)}, u32[]{:S(2)}, u32[]{:S(2)}) async-start(bf16[4,1024,256]{2,1,0:T(8,128)(2,1)} %bitcast.20), calls=%async_computation.7 | async-start | bytes 4194304 | tf_op jit(solution)/shard_map/all_to_all | solution.py:448
  210.1 32.4 %collective-permute-start.3 = (f32[4,256,128]{2,1,0:T(8,128)S(1)}, f32[4,256,128]{2,1,0:T(8,128)S(1)}, u32[]{:S(2)}, u32[]{:S(2)}) collective-permute-start(f32[4,256,128]{2,1,0:T(8,128)S(1)} %copy-done.4), channel_id=1, source_target_pairs={{0,16},{4,20},{8,24},{12,28},{16,0},{20,4},{24,8},{28,12},{1,17},{... | collective-permute-start | bytes 1572872 | tf_op jit(solution)/shard_map/ppermute | solution.py:456
  242.6 0.8 copy-start.6
  245.4 13.2 %all-to-all-start.7 = ((bf16[4,128,256]{2,1,0:T(8,128)(2,1)}), bf16[4,128,256]{2,1,0:T(8,128)(2,1)S(1)}, u32[]{:S(2)}, u32[]{:S(2)}) async-start(bf16[4,128,256]{2,1,0:T(8,128)(2,1)} %combine_query.1), calls=%async_computation.8 | async-start | bytes 524288 | tf_op jit(solution)/shard_map/all_to_all | solution.py:448
Sparse Core Ops, SparseCore 0:
  37.8 18.1 all-gather.1
  170.4 33.2 reduce-scatter.1

commit v3 on v2

--- a/solution.py
+++ b/solution.py
@@ -10,7 +10,7 @@
 HEAD_DIM = 64
 PLEN = 256
 INNER = 4
-GROUP = 4
+GROUP = 8
 LANES = 128
 NEG_LARGE = -1e30
 SCALE = HEAD_DIM ** (-0.5)
@@ -75,6 +75,15 @@
     )
 
 
+def two_heads_turned(block):
+    turned = jnp.transpose(block)
+    feat = lax.broadcasted_iota(jnp.int32, turned.shape, 0)
+    zero = jnp.zeros_like(turned)
+    return jnp.concatenate(
+        [jnp.where(feat < HEAD_DIM, turned, zero), jnp.where(feat >= HEAD_DIM, turned, zero)], axis=1
+    )
+
+
 def own_blocks(full):
     rows = full.shape[1] // 2
     return jnp.concatenate([full[:HEAD_DIM, :rows], full[HEAD_DIM:, rows:]], axis=0)
@@ -99,74 +108,95 @@
     lax.fori_loop(0, n_q, question, 0)
 
 
-def each_group(pick_ref, live_ref, ident, entries):
+def each_group(pick_ref, live_ref, ident, entries, start):
     live = live_ref[ident]
 
     def group(step, carry):
         first = step * GROUP
-        entries([(pick_ref[ident, first + j], first + j < live) for j in range(GROUP)])
-        return carry
-
-    lax.fori_loop(0, lax.div(live + (GROUP - 1), GROUP), group, 0)
+        slots = [pick_ref[ident, first + j] for j in range(GROUP)]
+        return entries(carry, slots, [first + j < live for j in range(GROUP)])
+
+    return lax.fori_loop(0, lax.div(live + (GROUP - 1), GROUP), group, start)
 
 
 def pair_lanes(pair):
     return slice(pair * LANES, (pair + 1) * LANES)
 
 
-def stats_kernel(pick_ref, live_ref, k_ref, q_ref, o_ref, qbd):
+def stacked(ref, slots, pair):
+    return jnp.concatenate([ref[slot, :, pair_lanes(pair)] for slot in slots], axis=0)
+
+
+def beside(ref, slots, pair):
+    return jnp.concatenate([ref[slot, pair_lanes(pair), :] for slot in slots], axis=1)
+
+
+def shifted(scores, lives, top):
+    keys = scores.shape[0] // GROUP
+    return [
+        jnp.exp(scores[j * keys : (j + 1) * keys] - jnp.where(live, top, -NEG_LARGE))
+        for j, live in enumerate(lives)
+    ]
+
+
+def stats_kernel(pick_ref, live_ref, k_ref, q_ref, o_ref, qt):
     n_q = q_ref.shape[0]
     n_pair = q_ref.shape[2] // LANES
 
     def question(ident, carry):
         for pair in range(n_pair):
-            qbd[pair] = two_heads(q_ref[ident, :, pair_lanes(pair)])
+            qt[pair] = two_heads_turned(q_ref[ident, :, pair_lanes(pair)])
         o_ref[0, ident] = jnp.full(o_ref.shape[2:], NEG_LARGE, F32)
         o_ref[1, ident] = jnp.zeros(o_ref.shape[2:], F32)
 
-        def entries(items):
+        def entries(state, slots, lives):
             for pair in range(n_pair):
                 row = slice(pair, pair + 1)
-                scores = [dot_nt(k_ref[slot, :, pair_lanes(pair)], qbd[pair]) for slot, _ in items]
+                scores = [dot_nn(k_ref[slot, :, pair_lanes(pair)], qt[pair]) for slot in slots]
                 old = o_ref[0, ident, row, :]
                 new = old
-                for (_, live), part in zip(items, scores):
-                    top = jnp.max(part, axis=0, keepdims=True)
+                for j, live in enumerate(lives):
+                    top = jnp.max(scores[j], axis=0, keepdims=True)
                     new = jnp.maximum(new, jnp.where(live, top, NEG_LARGE))
                 add = o_ref[1, ident, row, :] * jnp.exp(old - new)
-                for (_, live), part in zip(items, scores):
-                    shift = jnp.where(live, new, -NEG_LARGE)
-                    add = add + jnp.sum(jnp.exp(part - shift), axis=0, keepdims=True)
+                for part, live in zip(scores, lives):
+                    part = jnp.exp(part - jnp.where(live, new, -NEG_LARGE))
+                    add = add + jnp.sum(part, axis=0, keepdims=True)
                 o_ref[0, ident, row, :] = new
                 o_ref[1, ident, row, :] = add
-
-        each_group(pick_ref, live_ref, ident, entries)
+            return state
+
+        each_group(pick_ref, live_ref, ident, entries, 0)
         return carry
 
     lax.fori_loop(0, n_q, question, 0)
 
 
-def value_grad_kernel(pick_ref, live_ref, k_ref, q_ref, g_ref, st_ref, o_ref, qbd, gbd, acc):
+def value_grad_kernel(pick_ref, live_ref, k_ref, q_ref, g_ref, st_ref, o_ref, qt, gbd, acc):
     n_q = q_ref.shape[0]
     n_pair = q_ref.shape[2] // LANES
     acc[...] = jnp.zeros_like(acc)
 
     def question(ident, carry):
         for pair in range(n_pair):
-            qbd[pair] = two_heads(q_ref[ident, :, pair_lanes(pair)])
+            qt[pair] = two_heads_turned(q_ref[ident, :, pair_lanes(pair)])
             gbd[pair] = two_heads(g_ref[ident, :, pair_lanes(pair)])
 
-        def entries(items):
+        def entries(state, slots, lives):
             for pair in range(n_pair):
                 row = slice(pair, pair + 1)
-                for slot, live in items:
-                    shift = jnp.where(live, st_ref[0, ident, row, :], -NEG_LARGE)
-                    scores = dot_nt(k_ref[slot, :, pair_lanes(pair)], qbd[pair])
-                    probs = jnp.exp(scores - shift) * st_ref[1, ident, row, :]
-                    term = dot_nn(probs.astype(BF16), gbd[pair]).astype(BF16)
-                    acc[slot, :, pair_lanes(pair)] += term.astype(F32)
-
-        each_group(pick_ref, live_ref, ident, entries)
+                scores = dot_nn(stacked(k_ref, slots, pair), qt[pair])
+                norm = st_ref[1, ident, row, :]
+                probs = [
+                    (part * norm).astype(BF16)
+                    for part in shifted(scores, lives, st_ref[0, ident, row, :])
+                ]
+                term = dot_nn(jnp.concatenate(probs, axis=0), gbd[pair]).astype(BF16)
+                for j, slot in enumerate(slots):
+                    acc[slot, :, pair_lanes(pair)] += term[j * PLEN : (j + 1) * PLEN].astype(F32)
+            return state
+
+        each_group(pick_ref, live_ref, ident, entries, 0)
         return carry
 
     lax.fori_loop(0, n_q, question, 0)
@@ -187,7 +217,7 @@
 
 
 def context_kernel(n_outer, pick_ref, live_ref, outer_ref, k_ref, v_ref, q_ref, st_ref, *rest):
-    o_refs, (qbd, vt) = rest[:n_outer], rest[n_outer:]
+    o_refs, (qt, vt) = rest[:n_outer], rest[n_outer:]
     n_q = q_ref.shape[0]
     inner = n_q // n_outer
     n_pair = q_ref.shape[2] // LANES
@@ -196,26 +226,22 @@
     def question(o_ref, outer, index, carry):
         ident = outer * inner + index
         for pair in range(n_pair):
-            qbd[pair] = two_heads(q_ref[ident, :, pair_lanes(pair)])
+            qt[pair] = two_heads_turned(q_ref[ident, :, pair_lanes(pair)])
         zero = jnp.zeros((LANES, 2 * q_ref.shape[1]), F32)
 
-        def group(step, sums):
+        def entries(sums, slots, lives):
             out = []
             for pair in range(n_pair):
-                total = sums[pair]
-                row = slice(pair, pair + 1)
-                for j in range(GROUP):
-                    at = step * GROUP + j
-                    slot = pick_ref[ident, at]
-                    shift = jnp.where(at < live_ref[ident], st_ref[0, ident, row, :], -NEG_LARGE)
-                    scores = dot_nt(k_ref[slot, :, pair_lanes(pair)], qbd[pair])
-                    weights = jnp.exp(scores - shift).astype(BF16)
-                    total = total + dot_nn(vt[slot, pair_lanes(pair), :], weights)
-                out.append(total)
+                scores = dot_nn(stacked(k_ref, slots, pair), qt[pair])
+                weights = [
+                    part.astype(BF16)
+                    for part in shifted(scores, lives, st_ref[0, ident, slice(pair, pair + 1), :])
+                ]
+                mix = dot_nn(beside(vt, slots, pair), jnp.concatenate(weights, axis=0))
+                out.append(sums[pair] + mix)
             return tuple(out)
 
-        steps = lax.div(live_ref[ident] + (GROUP - 1), GROUP)
-        sums = lax.fori_loop(0, steps, group, (zero,) * n_pair)
+        sums = each_group(pick_ref, live_ref, ident, entries, (zero,) * n_pair)
         for pair in range(n_pair):
             o_ref[index, pair_lanes(pair), :] = own_blocks(sums[pair])
         return carry
@@ -228,7 +254,7 @@
 def score_grad_kernel(n_outer, pick_ref, live_ref, outer_ref, k_ref, v_ref, q_ref, g_ref, st_ref, *rest):
     dot_refs, rest = rest[:n_outer], rest[n_outer:]
     dk_ref, rest = rest[0], rest[1:]
-    dq_refs, (qbd, gbd, kt, acc_k) = rest[:n_outer], rest[n_outer:]
+    dq_refs, (qt, qbd, gt, kt, acc_k) = rest[:n_outer], rest[n_outer:]
     n_q = q_ref.shape[0]
     inner = n_q // n_outer
     n_pair = q_ref.shape[2] // LANES
@@ -239,30 +265,30 @@
         ident = outer * inner + index
         for pair in range(n_pair):
             qbd[pair] = two_heads(q_ref[ident, :, pair_lanes(pair)])
-            gbd[pair] = two_heads(g_ref[ident, :, pair_lanes(pair)])
+            qt[pair] = two_heads_turned(q_ref[ident, :, pair_lanes(pair)])
+            gt[pair] = two_heads_turned(g_ref[ident, :, pair_lanes(pair)])
         zero = jnp.zeros((LANES, 2 * q_ref.shape[1]), F32)
 
-        def group(step, sums):
+        def entries(sums, slots, lives):
             out = []
             for pair in range(n_pair):
-                total = sums[pair]
                 row = slice(pair, pair + 1)
-                for j in range(GROUP):
-                    at = step * GROUP + j
-                    slot = pick_ref[ident, at]
-                    shift = jnp.where(at < live_ref[ident], st_ref[0, ident, row, :], -NEG_LARGE)
-                    scores = dot_nt(k_ref[slot, :, pair_lanes(pair)], qbd[pair])
-                    probs = jnp.exp(scores - shift) * st_ref[1, ident, row, :]
-                    dprob = dot_nt(v_ref[slot, :, pair_lanes(pair)], gbd[pair])
-                    dscore = (probs * (dprob - dot_ref[index, row, :])).astype(BF16)
-                    term = dot_nn(dscore, qbd[pair]).astype(BF16)
-                    acc_k[slot, :, pair_lanes(pair)] += term.astype(F32)
-                    total = total + dot_nn(kt[slot, pair_lanes(pair), :], dscore)
-                out.append(total)
+                scores = dot_nn(stacked(k_ref, slots, pair), qt[pair])
+                dprob = dot_nn(stacked(v_ref, slots, pair), gt[pair])
+                norm = st_ref[1, ident, row, :]
+                dots = dot_ref[index, row, :]
+                dscore = [
+                    (part * norm * (dprob[j * PLEN : (j + 1) * PLEN] - dots)).astype(BF16)
+                    for j, part in enumerate(shifted(scores, lives, st_ref[0, ident, row, :]))
+                ]
+                dscore = jnp.concatenate(dscore, axis=0)
+                term = dot_nn(dscore, qbd[pair]).astype(BF16)
+                for j, slot in enumerate(slots):
+                    acc_k[slot, :, pair_lanes(pair)] += term[j * PLEN : (j + 1) * PLEN].astype(F32)
+                out.append(sums[pair] + dot_nn(beside(kt, slots, pair), dscore))
             return tuple(out)
 
-        steps = lax.div(live_ref[ident] + (GROUP - 1), GROUP)
-        sums = lax.fori_loop(0, steps, group, (zero,) * n_pair)
+        sums = each_group(pick_ref, live_ref, ident, entries, (zero,) * n_pair)
         for pair in range(n_pair):
             dq_ref[index, pair_lanes(pair), :] = own_blocks(sums[pair])
         return carry
@@ -471,14 +497,14 @@
 
     key_part = project(after(encoded, q_spread), key_weight)
     keys = swap(key_part).reshape(n_local, PLEN, width)
-    value_part = project(after(encoded, key_part), value_weight)
-    values = swap(value_part).reshape(n_local, PLEN, width)
+    value_part = project(after(encoded, key_part, grad_rows), value_weight)
     g_spread = context_grad_blocks(after(grad_rows, value_part), out_weight, n_outer, width)
     g_spread = g_spread.reshape(n_q, rows, width)
-    g_all = swap_all(g_spread)
-
-    pick, live = route(outer, slot_of, passage_lists, list_counts, n_local)
+    pick, live = route(after(outer, value_part), slot_of, passage_lists, list_counts, n_local)
+    values = swap(after(value_part, g_spread, pick)).reshape(n_local, PLEN, width)
+
     pair_scratch = pltpu.VMEM((n_pair, 2 * rows, LANES), BF16)
+    turned_pair = pltpu.VMEM((n_pair, LANES, 2 * rows), BF16)
     acc_scratch = pltpu.VMEM((n_local, PLEN, width), F32)
     turned = pltpu.VMEM((n_local, width, PLEN), BF16)
     stat_shape = (n_q, n_pair, 2 * rows)
@@ -487,10 +513,10 @@
     stats = vmem_call(
         stats_kernel,
         (pick, live),
-        (keys, after(q_all, g_spread)),
+        (keys, q_all),
         sds((2,) + stat_shape, F32),
-        [pair_scratch],
-        14,
+        [turned_pair],
+        13,
         "stats",
     )
     norm = vmem_call(
@@ -507,17 +533,18 @@
         (pick, live, outer),
         (keys, values, q_all, norm),
         mix_shape,
-        [pair_scratch, turned],
-        22,
+        [turned_pair, turned],
+        19,
         "context",
     )
+    g_all = swap_all(after(g_spread, mixes[0]))
     value_done = vmem_call(
         value_grad_kernel,
         (pick, live),
         (keys, q_all, g_all, after(norm, mixes[0])),
         sds((n_local, PLEN, width), BF16),
-        [pair_scratch, pair_scratch, acc_scratch],
-        20,
+        [turned_pair, pair_scratch, acc_scratch],
+        15,
         "value_grad",
     )
     context, grad_dot = vmem_call(
@@ -538,8 +565,8 @@
         (pick, live, outer),
         [keys, values, q_all, g_all, after(norm, projected)] + dots,
         (sds((n_local, PLEN, width), BF16),) + mix_shape,
-        [pair_scratch, pair_scratch, turned, acc_scratch],
-        36,
+        [turned_pair, pair_scratch, turned_pair, turned, acc_scratch],
+        25,
         "score_grad",
     )
     key_back = swap(after(done[0], value_back).reshape(inner, tok_local, width))

time: 268 us -> 276 us (1.030)
  waiting for transfers between devices: 44.2 us -> 70.7 us
  Pallas kernels: 141 us -> 122 us
  blocking collectives: 0 us -> 9.82 us
  starting transfers between devices: 53.1 us -> 44.2 us
    all_to_all x2, waiting for transfers between devices: 0.3 us -> 23.6 us  [swap_all(): return lax.all_to_all(x, 'pas', split_axis=0, concat_axis=0, tiled=True)]
    pallas_call x8, Pallas kernels: 96.9 us -> 78 us  [vmem_call(): pl.pallas_call(kernel, in_specs=[smem] * len(scalars) + [vmem] * len(arra...]
    ppermute x4, waiting for transfers between devices: 30.6 us -> 43.8 us  [to_outer(): lax.ppermute(x, 'pas', [(o * inner + i, (o + r) % n_outer * inner + i) fo...]
    all_to_all x6 -> x5, waiting for transfers between devices: 12.5 us -> 2.55 us  [swap(): lax.all_to_all(x, 'pas', split_axis=0, concat_axis=0, tiled=True, axis_in...]
    all_to_all x0 -> x1, blocking collectives: none -> 9.82 us  [swap(): lax.all_to_all(x, 'pas', split_axis=0, concat_axis=0, tiled=True, axis_in...]
    ppermute x4, starting transfers between devices: 11.5 us -> 6.49 us  [to_outer(): lax.ppermute(x, 'pas', [(o * inner + i, (o + r) % n_outer * inner + i) fo...]
    all_to_all x6 -> x5, starting transfers between devices: 27.8 us -> 24.2 us  [swap(): lax.all_to_all(x, 'pas', split_axis=0, concat_axis=0, tiled=True, axis_in...]
  transfers between devices with their start and end apart: 14 -> 13, of which waited for: 7 -> 8; matrix products, arithmetic and copies ran while one was open for 2% -> 2% of each run, Pallas kernels for 51% -> 37%
where the time goes in v3:
time: 276 us; the launch traced here: 275 us
  Pallas kernels  122 us (44%)
  waiting for transfers between devices  70.7 us (26%)
  starting transfers between devices  44.2 us (16%)
  between operations  14.1 us (5%)
  local copies, waits for them, and re-layouts  11.6 us (4%)
  blocking collectives  9.82 us (4%)
    pallas_call x8, Pallas kernels, vmem_call(): pl.pallas_call(kernel, in_specs=[smem] * len(scalars) + [vmem] * len(arra...  78 us
    ppermute x4, waiting for transfers between devices, to_outer(): lax.ppermute(x, 'pas', [(o * inner + i, (o + r) % n_outer * inner + i) fo...  43.8 us
    pallas_call x2, Pallas kernels, project(): pl.pallas_call(project_kernel, grid=(rows // tile,), in_specs=[pl.BlockSp...  28.7 us
    all_to_all x5, starting transfers between devices, swap(): lax.all_to_all(x, 'pas', split_axis=0, concat_axis=0, tiled=True, axis_in...  24.2 us
    all_to_all x2, waiting for transfers between devices, swap_all(): return lax.all_to_all(x, 'pas', split_axis=0, concat_axis=0, tiled=True)  23.6 us
    all_to_all x2, starting transfers between devices, swap_all(): return lax.all_to_all(x, 'pas', split_axis=0, concat_axis=0, tiled=True)  13.3 us
    all_to_all x1, blocking collectives, swap(): lax.all_to_all(x, 'pas', split_axis=0, concat_axis=0, tiled=True, axis_in...  9.82 us
    pallas_call x1, Pallas kernels, context_grad_blocks(): pl.pallas_call(context_grad_kernel, grid=(INNER,), in_specs=[pl.BlockSpec...  6.83 us
  transfers between devices with their start and end apart: 13, of which 8 were waited for; matrix products, arithmetic and copies ran while one was open for 2% of the time, Pallas kernels for 37%

profile of v3, /device:TPU:0, one launch (start us, length us, event | category | flops | bytes accessed | tf_op | source)
XLA Modules:
  0.0 274.6 jit_solution(17120077497933532451)
XLA Ops:
  7.2 0.0 all-gather.2.cloned.1.call-start
  7.2 0.7 all-gather.2.cloned.1.call-update
  7.9 1.8 spread.1
  9.7 7.3 %all-to-all-start.2 = ((bf16[8,128,256]{2,1,0:T(8,128)(2,1)}), bf16[8,128,256]{2,1,0:T(8,128)(2,1)S(1)}, u32[]{:S(2)}, u32[]{:S(2)}) async-start(bf16[8,128,256]{2,1,0:T(8,128)(2,1)} %spread.1), calls=%async_computation.2 | async-start | bytes 1048576 | tf_op jit(solution)/shard_map/all_to_all | solution.py:479
  17.0 14.6 %project.2 = bf16[4,1024,256]{2,1,0:T(8,128)(2,1)} custom-call(bf16[1024,4096]{1,0:T(8,128)(2,1)} %x_ref.3, bf16[4096,1024]{1,0:T(8,128)(2,1)} %w_ref.4), custom_call_target="tpu_custom_call" | custom-call | flops 14000000000 | tf_op jit(solution)/shard_map/project/pallas_call | solution.py:55
  31.5 0.8 copy-done.1
  32.3 4.2 %all-to-all-start = ((bf16[4,1024,256]{2,1,0:T(8,128)(2,1)}), bf16[4,1024,256]{2,1,0:T(8,128)(2,1)S(1)}, u32[]{:S(2)}, u32[]{:S(2)}) async-start(bf16[4,1024,256]{2,1,0:T(8,128)(2,1)} %project.2), calls=%async_computation | async-start | bytes 4194304 | tf_op jit(solution)/shard_map/all_to_all | solution.py:474
  36.5 14.2 %project.3 = bf16[4,1024,256]{2,1,0:T(8,128)(2,1)} custom-call(bf16[1024,4096]{1,0:T(8,128)(2,1)} %x_ref.3, bf16[4096,1024]{1,0:T(8,128)(2,1)} %w_ref.5), custom_call_target="tpu_custom_call" | custom-call | flops 14000000000 | tf_op jit(solution)/shard_map/project/pallas_call | solution.py:55
  50.7 2.3 route.1
  53.0 6.8 %context_grad.1 = bf16[2,4,128,256]{3,2,1,0:T(8,128)(2,1)} custom-call(bf16[128,4096]{1,0:T(8,128)(2,1)} %all-gather.2.cloned.1.call-done.x_ref, bf16[1024,4096]{1,0:T(8,128)(2,1)} %w_ref.7), custom_call_target="tpu_custom_call" | custom-call | flops 5000000000 | tf_op jit(solution)/shard_map/context_grad/pallas_call | solution.py:367
  59.8 1.0 all-to-all-done
  60.8 1.3 copy-done
  62.1 4.4 %all-to-all-start.1 = ((bf16[4,1024,256]{2,1,0:T(8,128)(2,1)}), bf16[4,1024,256]{2,1,0:T(8,128)(2,1)}, u32[]{:S(2)}, u32[]{:S(2)}) async-start(bf16[4,1024,256]{2,1,0:T(8,128)(2,1)} %project.3), calls=%async_computation.1 | async-start | bytes 4194304 | tf_op jit(solution)/shard_map/all_to_all | solution.py:474
  66.6 13.6 %stats.1.refs_0_ = f32[2,8,2,256]{3,2,1,0:T(2,128)} custom-call(s32[8,24]{1,0:T(8,128)} %get-tuple-element.28.pick_ref, s32[8]{0:T(128)} %get-tuple-element.29.live_ref, bf16[16,256,256]{2,1,0:T(8,128)(2,1)} %bitcast.15, bf16[8,128,256]{2,1,0:T(8,128)(2,1)} %copy-done.1), custom_call_target="tpu_custom_call" | custom-call | flops 12999999488 | tf_op jit(solution)/shard_map/stats/pallas_call | solution.py:416
  80.2 2.6 collective-permute-start
  82.8 6.7 %collective-permute-done.refs_1_ = f32[2,8,2,256]{3,2,1,0:T(2,128)S(1)} collective-permute-done((f32[2,8,2,256]{3,2,1,0:T(2,128)}, f32[2,8,2,256]{3,2,1,0:T(2,128)S(1)}, u32[]{:S(2)}, u32[]{:S(2)}) %collective-permute-start) | collective-permute-done | bytes 32800 | tf_op jit(solution)/shard_map/ppermute | solution.py:482
  89.5 0.6 copy-done.6
  90.1 1.4 merge.1.st_ref.refs_2_
  91.5 0.8 all-to-all-done.1
  92.4 18.0 %context.1 = (f32[4,256,128]{2,1,0:T(8,128)}, f32[4,256,128]{2,1,0:T(8,128)}) custom-call(s32[8,24]{1,0:T(8,128)} %get-tuple-element.28.pick_ref, s32[8]{0:T(128)} %get-tuple-element.29.live_ref, s32[1]{0:T(128)} %bitcast.outer_ref, bf16[16,256,256]{2,1,0:T(8,128)(2,1)} %bitcast.16, bf16[16,256,256]{2,1,0:T(8,128)(2,1)} %bitcast.3.v_ref, ...), custom_call_target="tpu_custom_call" | custom-call | flops 19000000512 | tf_op jit(solution)/shard_map/context/pallas_call | solution.py:416
  110.4 6.0 %all-to-all-start.3 = ((bf16[8,128,256]{2,1,0:T(8,128)(2,1)}), bf16[8,128,256]{2,1,0:T(8,128)(2,1)S(1)}, u32[]{:S(2)}, u32[]{:S(2)}) async-start(bf16[8,128,256]{2,1,0:T(8,128)(2,1)} %bitcast.2), calls=%async_computation.3 | async-start | bytes 1048576 | tf_op jit(solution)/shard_map/all_to_all | solution.py:479
  116.4 2.9 %collective-permute-start.1 = (f32[4,256,128]{2,1,0:T(8,128)}, f32[4,256,128]{2,1,0:T(8,128)S(1)}, u32[]{:S(2)}, u32[]{:S(2)}) collective-permute-start(f32[4,256,128]{2,1,0:T(8,128)} %get-tuple-element.33), channel_id=1, source_target_pairs={{0,16},{4,20},{8,24},{12,28},{16,0},{20,4},{24,8},{28,12},{1,17},{... | collective-permute-start | bytes 1572872 | tf_op jit(solution)/shard_map/ppermute | solution.py:482
  119.3 23.6 %all-to-all-done.3.g_ref.refs_3_ = bf16[8,128,256]{2,1,0:T(8,128)(2,1)S(1)} async-done(((bf16[8,128,256]{2,1,0:T(8,128)(2,1)}), bf16[8,128,256]{2,1,0:T(8,128)(2,1)S(1)}, u32[]{:S(2)}, u32[]{:S(2)}) %all-to-all-start.3) | async-done | bytes 524320 | tf_op jit(solution)/shard_map/all_to_all | solution.py:479
  142.9 0.8 copy-done.2
  143.7 15.2 %value_grad.1 = bf16[16,256,256]{2,1,0:T(8,128)(2,1)} custom-call(s32[8,24]{1,0:T(8,128)} %get-tuple-element.28.pick_ref, s32[8]{0:T(128)} %get-tuple-element.29.live_ref, bf16[16,256,256]{2,1,0:T(8,128)(2,1)} %bitcast.17, bf16[8,128,256]{2,1,0:T(8,128)(2,1)} %copy-done.1, bf16[8,128,256]{2,1,0:T(8,128)(2,1)} %copy-done.2, f32[3,8,2,256]{3,2,1,0:T(2,128)} %merge.1.st_ref.refs_2_), custom_call_target="tpu_custom_call" | custom-call | flops 15000000512 | tf_op jit(solution)/shard_map/value_grad/pallas_call | solution.py:416
  158.9 0.8 copy-done.4
  159.7 2.3 combine_context.1
  162.0 9.8 %all_to_all.40.x_ref = bf16[4,128,256]{2,1,0:T(8,128)(2,1)} all-to-all(bf16[4,128,256]{2,1,0:T(8,128)(2,1)} %get-tuple-element.37), channel_id=1, replica_groups={{0,4,8,12},{16,20,24,28},{1,5,9,13},{17,21,25,29},{2,6,10,14},{18,22,26..., dimensions={0} | all-to-all | bytes 524288 | tf_op jit(solution)/shard_map/all_to_all | solution.py:474
  171.8 3.7 %all-to-all-start.5 = ((bf16[4,1024,256]{2,1,0:T(8,128)(2,1)}), bf16[4,1024,256]{2,1,0:T(8,128)(2,1)S(1)}, u32[]{:S(2)}, u32[]{:S(2)}) async-start(bf16[4,1024,256]{2,1,0:T(8,128)(2,1)} %bitcast.19), calls=%async_computation.6 | async-start | bytes 4194304 | tf_op jit(solution)/shard_map/all_to_all | solution.py:474
  175.6 0.2 reduce-scatter.2.cloned.1.call-start
  175.8 0.1 collective-permute-start.2
  175.9 6.7 %out_project.1 = f32[128,4096]{1,0:T(8,128)} custom-call(bf16[4,128,256]{2,1,0:T(8,128)(2,1)} %all_to_all.40.x_ref, bf16[1024,4096]{1,0:T(8,128)(2,1)} %w_ref.7), custom_call_target="tpu_custom_call" | custom-call | flops 5000000000 | tf_op jit(solution)/shard_map/out_project/pallas_call | solution.py:398
  182.6 9.8 %collective-permute-done.2.rest_1_ = f32[4,2,256]{2,1,0:T(2,128)S(1)} collective-permute-done((f32[4,2,256]{2,1,0:T(2,128)S(1)}, f32[4,2,256]{2,1,0:T(2,128)S(1)}, u32[]{:S(2)}, u32[]{:S(2)}) %collective-permute-start.2) | collective-permute-done | bytes 8224 | tf_op jit(solution)/shard_map/ppermute | solution.py:482
  192.5 0.6 copy-done.8
  193.1 23.6 %score_grad.1 = (bf16[16,256,256]{2,1,0:T(8,128)(2,1)}, f32[4,256,128]{2,1,0:T(8,128)}, f32[4,256,128]{2,1,0:T(8,128)}) custom-call(s32[8,24]{1,0:T(8,128)} %get-tuple-element.28.pick_ref, s32[8]{0:T(128)} %get-tuple-element.29.live_ref, s32[1]{0:T(128)} %bitcast.outer_ref, bf16[16,256,256]{2,1,0:T(8,128)(2,1)} %bitcast.18, ...), custom_call_target="tpu_custom_call" | custom-call | flops 24999999488 | tf_op jit(solution)/shard_map/score_grad/pallas_call | solution.py:416
  216.6 7.0 %all-to-all-start.6 = ((bf16[4,1024,256]{2,1,0:T(8,128)(2,1)}), bf16[4,1024,256]{2,1,0:T(8,128)(2,1)}, u32[]{:S(2)}, u32[]{:S(2)}) async-start(bf16[4,1024,256]{2,1,0:T(8,128)(2,1)} %bitcast.20), calls=%async_computation.7 | async-start | bytes 4194304 | tf_op jit(solution)/shard_map/all_to_all | solution.py:474
  223.7 0.9 collective-permute-start.3
  224.6 1.8 convert_element_type.3
  226.4 27.3 %collective-permute-done.3.refs_1_ = f32[4,256,128]{2,1,0:T(8,128)S(1)} collective-permute-done((f32[4,256,128]{2,1,0:T(8,128)S(1)}, f32[4,256,128]{2,1,0:T(8,128)S(1)}, u32[]{:S(2)}, u32[]{:S(2)}) %collective-permute-start.3) | collective-permute-done | bytes 524320 | tf_op jit(solution)/shard_map/ppermute | solution.py:482
  253.6 0.8 copy-done.5
  254.4 2.0 combine_query.1
  256.5 0.1 all-to-all-done.6
  256.6 4.8 %all-to-all-start.7 = ((bf16[4,128,256]{2,1,0:T(8,128)(2,1)}), bf16[4,128,256]{2,1,0:T(8,128)(2,1)S(1)}, u32[]{:S(2)}, u32[]{:S(2)}) async-start(bf16[4,128,256]{2,1,0:T(8,128)(2,1)} %combine_query.1), calls=%async_computation.8 | async-start | bytes 524288 | tf_op jit(solution)/shard_map/all_to_all | solution.py:474
  261.4 1.6 copy.20
  263.0 3.2 %copy.19 = bf16[4,128,8,256]{3,2,0,1:T(8,128)(2,1)} copy(bf16[4,128,8,256]{3,2,1,0:T(8,128)(2,1)} %bitcast.10) | data formatting | bytes 4194304 | tf_op jit(solution)/shard_map/reshape | solution.py:489
  266.2 0.6 all-to-all-done.7
  266.8 0.2 copy.15
  266.9 0.9 copy.18
  (17 shorter events, 0.0 us)
Async XLA Ops:
  7.2 29.3 %all-gather.2.cloned.1.call-start = ((), (), s32[]{:S(2)}) async-start(), calls=%async_computation.9 | async-start | bytes 1310720 | tf_op jit(solution)/shard_map/all_gather | solution.py:496
  9.7 21.8 %all-to-all-start.2 = ((bf16[8,128,256]{2,1,0:T(8,128)(2,1)}), bf16[8,128,256]{2,1,0:T(8,128)(2,1)S(1)}, u32[]{:S(2)}, u32[]{:S(2)}) async-start(bf16[8,128,256]{2,1,0:T(8,128)(2,1)} %spread.1), calls=%async_computation.2 | async-start | bytes 1048576 | tf_op jit(solution)/shard_map/all_to_all | solution.py:479
  31.5 0.8 copy-start.1
  32.3 28.5 %all-to-all-start = ((bf16[4,1024,256]{2,1,0:T(8,128)(2,1)}), bf16[4,1024,256]{2,1,0:T(8,128)(2,1)S(1)}, u32[]{:S(2)}, u32[]{:S(2)}) async-start(bf16[4,1024,256]{2,1,0:T(8,128)(2,1)} %project.2), calls=%async_computation | async-start | bytes 4194304 | tf_op jit(solution)/shard_map/all_to_all | solution.py:474
  60.8 1.3 copy-start
  62.1 30.2 %all-to-all-start.1 = ((bf16[4,1024,256]{2,1,0:T(8,128)(2,1)}), bf16[4,1024,256]{2,1,0:T(8,128)(2,1)}, u32[]{:S(2)}, u32[]{:S(2)}) async-start(bf16[4,1024,256]{2,1,0:T(8,128)(2,1)} %project.3), calls=%async_computation.1 | async-start | bytes 4194304 | tf_op jit(solution)/shard_map/all_to_all | solution.py:474
  80.2 9.3 %collective-permute-start = (f32[2,8,2,256]{3,2,1,0:T(2,128)}, f32[2,8,2,256]{3,2,1,0:T(2,128)S(1)}, u32[]{:S(2)}, u32[]{:S(2)}) collective-permute-start(f32[2,8,2,256]{3,2,1,0:T(2,128)} %stats.1.refs_0_), channel_id=1, source_target_pairs={{0,16},{4,20},{8,24},{12,28},{16,0},{20,4},{24,8},{28,12},{1,17},{... | collective-permute-start | bytes 98312 | tf_op jit(solution)/shard_map/ppermute | solution.py:482
  89.5 0.6 copy-start.6
  110.4 32.5 %all-to-all-start.3 = ((bf16[8,128,256]{2,1,0:T(8,128)(2,1)}), bf16[8,128,256]{2,1,0:T(8,128)(2,1)S(1)}, u32[]{:S(2)}, u32[]{:S(2)}) async-start(bf16[8,128,256]{2,1,0:T(8,128)(2,1)} %bitcast.2), calls=%async_computation.3 | async-start | bytes 1048576 | tf_op jit(solution)/shard_map/all_to_all | solution.py:479
  116.4 42.5 %collective-permute-start.1 = (f32[4,256,128]{2,1,0:T(8,128)}, f32[4,256,128]{2,1,0:T(8,128)S(1)}, u32[]{:S(2)}, u32[]{:S(2)}) collective-permute-start(f32[4,256,128]{2,1,0:T(8,128)} %get-tuple-element.33), channel_id=1, source_target_pairs={{0,16},{4,20},{8,24},{12,28},{16,0},{20,4},{24,8},{28,12},{1,17},{... | collective-permute-start | bytes 1572872 | tf_op jit(solution)/shard_map/ppermute | solution.py:482
  142.9 0.8 copy-start.2
  158.9 0.8 copy-start.4
  171.8 4.0 %copy-start.7 = (f32[4,2,256]{2,1,0:T(2,128)S(1)}, f32[4,2,256]{2,1,0:T(2,128)}, u32[]{:S(2)}) copy-start(f32[4,2,256]{2,1,0:T(2,128)} %get-tuple-element.39.rest_0_) | copy-start | bytes 24580
  171.8 44.8 %all-to-all-start.5 = ((bf16[4,1024,256]{2,1,0:T(8,128)(2,1)}), bf16[4,1024,256]{2,1,0:T(8,128)(2,1)S(1)}, u32[]{:S(2)}, u32[]{:S(2)}) async-start(bf16[4,1024,256]{2,1,0:T(8,128)(2,1)} %bitcast.19), calls=%async_computation.6 | async-start | bytes 4194304 | tf_op jit(solution)/shard_map/all_to_all | solution.py:474
  175.6 49.0 %reduce-scatter.2.cloned.1.call-start = ((), (), s32[]{:S(2)}) async-start(), calls=%async_computation.10 | async-start | bytes 2621440 | tf_op jit(solution)/shard_map/reduce_scatter | solution.py:562
  175.8 16.6 %collective-permute-start.2 = (f32[4,2,256]{2,1,0:T(2,128)S(1)}, f32[4,2,256]{2,1,0:T(2,128)S(1)}, u32[]{:S(2)}, u32[]{:S(2)}) collective-permute-start(f32[4,2,256]{2,1,0:T(2,128)S(1)} %copy-done.7), channel_id=1, source_target_pairs={{0,16},{4,20},{8,24},{12,28},{16,0},{20,4},{24,8},{28,12},{1,17},{... | collective-permute-start | bytes 24584 | tf_op jit(solution)/shard_map/ppermute | solution.py:482
  192.5 0.6 copy-start.8
  216.6 7.0 %copy-start.3 = (f32[4,256,128]{2,1,0:T(8,128)S(1)}, f32[4,256,128]{2,1,0:T(8,128)}, u32[]{:S(2)}) copy-start(f32[4,256,128]{2,1,0:T(8,128)} %get-tuple-element.42) | copy-start | bytes 1572868
  216.6 40.0 %all-to-all-start.6 = ((bf16[4,1024,256]{2,1,0:T(8,128)(2,1)}), bf16[4,1024,256]{2,1,0:T(8,128)(2,1)}, u32[]{:S(2)}, u32[]{:S(2)}) async-start(bf16[4,1024,256]{2,1,0:T(8,128)(2,1)} %bitcast.20), calls=%async_computation.7 | async-start | bytes 4194304 | tf_op jit(solution)/shard_map/all_to_all | solution.py:474
  223.7 30.0 %collective-permute-start.3 = (f32[4,256,128]{2,1,0:T(8,128)S(1)}, f32[4,256,128]{2,1,0:T(8,128)S(1)}, u32[]{:S(2)}, u32[]{:S(2)}) collective-permute-start(f32[4,256,128]{2,1,0:T(8,128)S(1)} %copy-done.3), channel_id=1, source_target_pairs={{0,16},{4,20},{8,24},{12,28},{16,0},{20,4},{24,8},{28,12},{1,17},{... | collective-permute-start | bytes 1572872 | tf_op jit(solution)/shard_map/ppermute | solution.py:482
  253.6 0.8 copy-start.5
  256.6 10.2 %all-to-all-start.7 = ((bf16[4,128,256]{2,1,0:T(8,128)(2,1)}), bf16[4,128,256]{2,1,0:T(8,128)(2,1)S(1)}, u32[]{:S(2)}, u32[]{:S(2)}) async-start(bf16[4,128,256]{2,1,0:T(8,128)(2,1)} %combine_query.1), calls=%async_computation.8 | async-start | bytes 524288 | tf_op jit(solution)/shard_map/all_to_all | solution.py:474
Sparse Core Ops, SparseCore 0:
  9.6 19.4 all-gather.1
  182.7 33.0 reduce-scatter.1

commit v4 on v3

--- a/solution.py
+++ b/solution.py
@@ -216,15 +216,13 @@
     lax.fori_loop(0, src_ref.shape[0], one, 0)
 
 
-def context_kernel(n_outer, pick_ref, live_ref, outer_ref, k_ref, v_ref, q_ref, st_ref, *rest):
-    o_refs, (qt, vt) = rest[:n_outer], rest[n_outer:]
-    n_q = q_ref.shape[0]
-    inner = n_q // n_outer
+def context_kernel(n_outer, r, pick_ref, live_ref, outer_ref, k_ref, v_ref, q_ref, st_ref, o_ref, qt, vt):
     n_pair = q_ref.shape[2] // LANES
+    first = lax.rem(outer_ref[0] + r, n_outer) * o_ref.shape[0]
     turn(v_ref, vt)
 
-    def question(o_ref, outer, index, carry):
-        ident = outer * inner + index
+    def question(index, carry):
+        ident = first + index
         for pair in range(n_pair):
             qt[pair] = two_heads_turned(q_ref[ident, :, pair_lanes(pair)])
         zero = jnp.zeros((LANES, 2 * q_ref.shape[1]), F32)
@@ -246,9 +244,7 @@
             o_ref[index, pair_lanes(pair), :] = own_blocks(sums[pair])
         return carry
 
-    for r in reversed(range(n_outer)):
-        outer = lax.rem(outer_ref[0] + r, n_outer)
-        lax.fori_loop(0, inner, functools.partial(question, o_refs[r], outer), 0)
+    lax.fori_loop(0, o_ref.shape[0], question, 0)
 
 
 def score_grad_kernel(n_outer, pick_ref, live_ref, outer_ref, k_ref, v_ref, q_ref, g_ref, st_ref, *rest):
@@ -508,7 +504,7 @@
     acc_scratch = pltpu.VMEM((n_local, PLEN, width), F32)
     turned = pltpu.VMEM((n_local, width, PLEN), BF16)
     stat_shape = (n_q, n_pair, 2 * rows)
-    mix_shape = (sds((inner, width, rows), F32),) * n_outer
+    mix_shape = sds((inner, width, rows), F32)
 
     stats = vmem_call(
         stats_kernel,
@@ -528,20 +524,23 @@
         1,
         "merge",
     )
-    mixes = vmem_call(
-        functools.partial(context_kernel, n_outer),
-        (pick, live, outer),
-        (keys, values, q_all, norm),
-        mix_shape,
-        [turned_pair, turned],
-        19,
-        "context",
-    )
-    g_all = swap_all(after(g_spread, mixes[0]))
+    g_all = swap_all(after(g_spread, values))
+    mixes, norm_then = [None] * n_outer, norm
+    for r in reversed(range(n_outer)):
+        mixes[r] = vmem_call(
+            functools.partial(context_kernel, n_outer, r),
+            (pick, live, outer),
+            (keys, values, q_all, norm_then),
+            mix_shape,
+            [turned_pair, turned],
+            10,
+            "context",
+        )
+        norm_then = after(norm, mixes[r], g_all)
     value_done = vmem_call(
         value_grad_kernel,
         (pick, live),
-        (keys, q_all, g_all, after(norm, mixes[0])),
+        (keys, q_all, g_all, norm_then),
         sds((n_local, PLEN, width), BF16),
         [turned_pair, pair_scratch, acc_scratch],
         15,
@@ -550,21 +549,21 @@
     context, grad_dot = vmem_call(
         functools.partial(combine_context_kernel, n_outer),
         (outer,),
-        partials(mixes) + [after(norm, value_done), g_all],
+        partials([after(mix, g_all) for mix in mixes]) + [after(norm, value_done), g_all],
         (sds((inner, rows, width), BF16), sds((inner, n_pair, 2 * rows), F32)),
         [],
         2,
         "combine_context",
     )
     dots = [grad_dot] + [to_outer(grad_dot, n_outer - r) for r in range(1, n_outer)]
-    projected = out_project(swap(context), out_weight)
+    projected = out_project(swap(after(context, *dots[1:])), out_weight)
     value_back = swap(value_done.reshape(inner, tok_local, width))
     output = lax.psum_scatter(projected, "head", scatter_dimension=1, tiled=True).astype(BF16)
     done = vmem_call(
         functools.partial(score_grad_kernel, n_outer),
         (pick, live, outer),
         [keys, values, q_all, g_all, after(norm, projected)] + dots,
-        (sds((n_local, PLEN, width), BF16),) + mix_shape,
+        (sds((n_local, PLEN, width), BF16),) + (mix_shape,) * n_outer,
         [turned_pair, pair_scratch, turned_pair, turned, acc_scratch],
         25,
         "score_grad",

time: 276 us -> 248 us (0.90)
  waiting for transfers between devices: 70.7 us -> 41.3 us
  Pallas kernels: 122 us -> 127 us
    all_to_all x2, waiting for transfers between devices: 23.6 us -> 1.82 us  [swap_all(): return lax.all_to_all(x, 'pas', split_axis=0, concat_axis=0, tiled=True)]
    ppermute x4, waiting for transfers between devices: 43.8 us -> 34.1 us  [to_outer(): lax.ppermute(x, 'pas', [(o * inner + i, (o + r) % n_outer * inner + i) fo...]
    pallas_call x8 -> x9, Pallas kernels: 78 us -> 82.2 us  [vmem_call(): pl.pallas_call(kernel, in_specs=[smem] * len(scalars) + [vmem] * len(arra...]
    unnamed x19 -> x17, local copies, waits for them, and re-layouts: 6.59 us -> 5.21 us
  transfers between devices with their start and end apart: 13 -> 13, of which waited for: 8 -> 8; matrix products, arithmetic and copies ran while one was open for 2% -> 3% of each run, Pallas kernels for 37% -> 50%
where the time goes in v4:
time: 248 us; the launch traced here: 246 us
  Pallas kernels  127 us (51%)
  starting transfers between devices  42.5 us (17%)
  waiting for transfers between devices  41.3 us (17%)
  between operations  14.1 us (6%)
  local copies, waits for them, and re-layouts  10.2 us (4%)
  blocking collectives  9.84 us (4%)
    pallas_call x9, Pallas kernels, vmem_call(): pl.pallas_call(kernel, in_specs=[smem] * len(scalars) + [vmem] * len(arra...  82.2 us
    ppermute x4, waiting for transfers between devices, to_outer(): lax.ppermute(x, 'pas', [(o * inner + i, (o + r) % n_outer * inner + i) fo...  34.1 us
    pallas_call x2, Pallas kernels, project(): pl.pallas_call(project_kernel, grid=(rows // tile,), in_specs=[pl.BlockSp...  28.7 us
    all_to_all x5, starting transfers between devices, swap(): lax.all_to_all(x, 'pas', split_axis=0, concat_axis=0, tiled=True, axis_in...  21.6 us
    all_to_all x2, starting transfers between devices, swap_all(): return lax.all_to_all(x, 'pas', split_axis=0, concat_axis=0, tiled=True)  13.3 us
    all_to_all x1, blocking collectives, swap(): lax.all_to_all(x, 'pas', split_axis=0, concat_axis=0, tiled=True, axis_in...  9.84 us
    ppermute x4, starting transfers between devices, to_outer(): lax.ppermute(x, 'pas', [(o * inner + i, (o + r) % n_outer * inner + i) fo...  7.34 us
    pallas_call x1, Pallas kernels, context_grad_blocks(): pl.pallas_call(context_grad_kernel, grid=(INNER,), in_specs=[pl.BlockSpec...  6.82 us
  transfers between devices with their start and end apart: 13, of which 8 were waited for; matrix products, arithmetic and copies ran while one was open for 3% of the time, Pallas kernels for 50%

profile of v4, /device:TPU:0, one launch (start us, length us, event | category | flops | bytes accessed | tf_op | source)
XLA Modules:
  0.0 246.4 jit_solution(15486247296855217807)
XLA Ops:
  7.2 0.0 all-gather.2.cloned.1.call-start
  7.2 0.7 all-gather.2.cloned.1.call-update
  7.9 1.8 spread.1
  9.7 7.3 %all-to-all-start.2 = ((bf16[8,128,256]{2,1,0:T(8,128)(2,1)}), bf16[8,128,256]{2,1,0:T(8,128)(2,1)S(1)}, u32[]{:S(2)}, u32[]{:S(2)}) async-start(bf16[8,128,256]{2,1,0:T(8,128)(2,1)} %spread.1), calls=%async_computation.2 | async-start | bytes 1048576 | tf_op jit(solution)/shard_map/all_to_all | solution.py:475
  17.0 14.6 %project.2 = bf16[4,1024,256]{2,1,0:T(8,128)(2,1)} custom-call(bf16[1024,4096]{1,0:T(8,128)(2,1)} %x_ref.3, bf16[4096,1024]{1,0:T(8,128)(2,1)} %w_ref.4), custom_call_target="tpu_custom_call" | custom-call | flops 14000000000 | tf_op jit(solution)/shard_map/project/pallas_call | solution.py:55
  31.5 0.8 copy-done.1
  32.3 4.2 %all-to-all-start = ((bf16[4,1024,256]{2,1,0:T(8,128)(2,1)}), bf16[4,1024,256]{2,1,0:T(8,128)(2,1)S(1)}, u32[]{:S(2)}, u32[]{:S(2)}) async-start(bf16[4,1024,256]{2,1,0:T(8,128)(2,1)} %project.2), calls=%async_computation | async-start | bytes 4194304 | tf_op jit(solution)/shard_map/all_to_all | solution.py:470
  36.5 14.2 %project.3 = bf16[4,1024,256]{2,1,0:T(8,128)(2,1)} custom-call(bf16[1024,4096]{1,0:T(8,128)(2,1)} %x_ref.3, bf16[4096,1024]{1,0:T(8,128)(2,1)} %w_ref.5), custom_call_target="tpu_custom_call" | custom-call | flops 14000000000 | tf_op jit(solution)/shard_map/project/pallas_call | solution.py:55
  50.7 2.3 route.1
  53.0 6.8 %context_grad.1 = bf16[2,4,128,256]{3,2,1,0:T(8,128)(2,1)} custom-call(bf16[128,4096]{1,0:T(8,128)(2,1)} %all-gather.2.cloned.1.call-done.x_ref, bf16[1024,4096]{1,0:T(8,128)(2,1)} %w_ref.7), custom_call_target="tpu_custom_call" | custom-call | flops 5000000000 | tf_op jit(solution)/shard_map/context_grad/pallas_call | solution.py:363
  59.8 1.0 all-to-all-done
  60.8 1.3 copy-done
  62.1 4.5 %all-to-all-start.1 = ((bf16[4,1024,256]{2,1,0:T(8,128)(2,1)}), bf16[4,1024,256]{2,1,0:T(8,128)(2,1)}, u32[]{:S(2)}, u32[]{:S(2)}) async-start(bf16[4,1024,256]{2,1,0:T(8,128)(2,1)} %project.3), calls=%async_computation.1 | async-start | bytes 4194304 | tf_op jit(solution)/shard_map/all_to_all | solution.py:470
  66.6 13.6 %stats.1.refs_0_ = f32[2,8,2,256]{3,2,1,0:T(2,128)} custom-call(s32[8,24]{1,0:T(8,128)} %get-tuple-element.30.pick_ref, s32[8]{0:T(128)} %get-tuple-element.31.live_ref, bf16[16,256,256]{2,1,0:T(8,128)(2,1)} %bitcast.15, bf16[8,128,256]{2,1,0:T(8,128)(2,1)} %copy-done.1), custom_call_target="tpu_custom_call" | custom-call | flops 12999999488 | tf_op jit(solution)/shard_map/stats/pallas_call | solution.py:412
  80.2 2.6 %collective-permute-start = (f32[2,8,2,256]{3,2,1,0:T(2,128)}, f32[2,8,2,256]{3,2,1,0:T(2,128)S(1)}, u32[]{:S(2)}, u32[]{:S(2)}) collective-permute-start(f32[2,8,2,256]{3,2,1,0:T(2,128)} %stats.1.refs_0_), channel_id=1, source_target_pairs={{0,16},{4,20},{8,24},{12,28},{16,0},{20,4},{24,8},{28,12},{1,17},{... | collective-permute-start | bytes 98312 | tf_op jit(solution)/shard_map/ppermute | solution.py:478
  82.8 6.7 %collective-permute-done.refs_1_ = f32[2,8,2,256]{3,2,1,0:T(2,128)S(1)} collective-permute-done((f32[2,8,2,256]{3,2,1,0:T(2,128)}, f32[2,8,2,256]{3,2,1,0:T(2,128)S(1)}, u32[]{:S(2)}, u32[]{:S(2)}) %collective-permute-start) | collective-permute-done | bytes 32800 | tf_op jit(solution)/shard_map/ppermute | solution.py:478
  89.5 0.6 copy-done.6
  90.1 1.4 merge.1.st_ref.refs_2_
  91.5 0.8 all-to-all-done.1
  92.4 6.0 %all-to-all-start.3 = ((bf16[8,128,256]{2,1,0:T(8,128)(2,1)}), bf16[8,128,256]{2,1,0:T(8,128)(2,1)S(1)}, u32[]{:S(2)}, u32[]{:S(2)}) async-start(bf16[8,128,256]{2,1,0:T(8,128)(2,1)} %bitcast.2), calls=%async_computation.3 | async-start | bytes 1048576 | tf_op jit(solution)/shard_map/all_to_all | solution.py:475
  98.4 11.2 %context.2 = f32[4,256,128]{2,1,0:T(8,128)} custom-call(s32[8,24]{1,0:T(8,128)} %get-tuple-element.30.pick_ref, s32[8]{0:T(128)} %get-tuple-element.31.live_ref, s32[1]{0:T(128)} %bitcast.outer_ref, bf16[16,256,256]{2,1,0:T(8,128)(2,1)} %bitcast.16, bf16[16,256,256]{2,1,0:T(8,128)(2,1)} %bitcast.3.v_ref, bf16[8,128,256]{2,1,0:T(8,128)(2,1)} %copy-done.1, ...), custom_call_target="tpu_custom_call" | custom-call | flops 10000000000 | tf_op jit(solution)/shard_map/context/pallas_call | solution.py:412
  109.6 1.8 all-to-all-done.3.g_ref.refs_3_
  111.4 1.2 collective-permute-start.1
  112.6 11.2 %context.3.refs_0_ = f32[4,256,128]{2,1,0:T(8,128)} custom-call(s32[8,24]{1,0:T(8,128)} %get-tuple-element.30.pick_ref, s32[8]{0:T(128)} %get-tuple-element.31.live_ref, s32[1]{0:T(128)} %bitcast.outer_ref, bf16[16,256,256]{2,1,0:T(8,128)(2,1)} %bitcast.17, bf16[16,256,256]{2,1,0:T(8,128)(2,1)} %bitcast.3.v_ref, bf16[8,128,256]{2,1,0:T(8,128)(2,1)} %copy-done.1, ...), custom_call_target="tpu_custom_call" | custom-call | flops 10000000000 | tf_op jit(solution)/shard_map/context/pallas_call | solution.py:412
  123.8 15.2 %value_grad.1 = bf16[16,256,256]{2,1,0:T(8,128)(2,1)} custom-call(s32[8,24]{1,0:T(8,128)} %get-tuple-element.30.pick_ref, s32[8]{0:T(128)} %get-tuple-element.31.live_ref, bf16[16,256,256]{2,1,0:T(8,128)(2,1)} %bitcast.18, bf16[8,128,256]{2,1,0:T(8,128)(2,1)} %copy-done.1, bf16[8,128,256]{2,1,0:T(8,128)(2,1)} %copy-done.2, f32[3,8,2,256]{3,2,1,0:T(2,128)} %merge.1.st_ref.refs_2_), custom_call_target="tpu_custom_call" | custom-call | flops 15000000512 | tf_op jit(solution)/shard_map/value_grad/pallas_call | solution.py:412
  139.0 0.8 copy-done.5
  139.8 2.3 combine_context.1
  142.1 1.7 collective-permute-start.2
  143.8 3.0 %collective-permute-done.2.rest_1_ = f32[4,2,256]{2,1,0:T(2,128)S(1)} collective-permute-done((f32[4,2,256]{2,1,0:T(2,128)}, f32[4,2,256]{2,1,0:T(2,128)S(1)}, u32[]{:S(2)}, u32[]{:S(2)}) %collective-permute-start.2) | collective-permute-done | bytes 8224 | tf_op jit(solution)/shard_map/ppermute | solution.py:478
  146.9 9.8 %all_to_all.40.x_ref = bf16[4,128,256]{2,1,0:T(8,128)(2,1)} all-to-all(bf16[4,128,256]{2,1,0:T(8,128)(2,1)} %get-tuple-element.42), channel_id=1, replica_groups={{0,4,8,12},{16,20,24,28},{1,5,9,13},{17,21,25,29},{2,6,10,14},{18,22,26..., dimensions={0} | all-to-all | bytes 524288 | tf_op jit(solution)/shard_map/all_to_all | solution.py:470
  156.7 3.6 %all-to-all-start.5 = ((bf16[4,1024,256]{2,1,0:T(8,128)(2,1)}), bf16[4,1024,256]{2,1,0:T(8,128)(2,1)S(1)}, u32[]{:S(2)}, u32[]{:S(2)}) async-start(bf16[4,1024,256]{2,1,0:T(8,128)(2,1)} %bitcast.20), calls=%async_computation.6 | async-start | bytes 4194304 | tf_op jit(solution)/shard_map/all_to_all | solution.py:470
  160.3 0.2 reduce-scatter.2.cloned.1.call-start
  160.5 6.7 %out_project.1 = f32[128,4096]{1,0:T(8,128)} custom-call(bf16[4,128,256]{2,1,0:T(8,128)(2,1)} %all_to_all.40.x_ref, bf16[1024,4096]{1,0:T(8,128)(2,1)} %w_ref.7), custom_call_target="tpu_custom_call" | custom-call | flops 5000000000 | tf_op jit(solution)/shard_map/out_project/pallas_call | solution.py:394
  167.2 0.0 reduce-scatter.2.cloned.1.call-update
  167.2 23.4 %score_grad.1 = (bf16[16,256,256]{2,1,0:T(8,128)(2,1)}, f32[4,256,128]{2,1,0:T(8,128)}, f32[4,256,128]{2,1,0:T(8,128)}) custom-call(s32[8,24]{1,0:T(8,128)} %get-tuple-element.30.pick_ref, s32[8]{0:T(128)} %get-tuple-element.31.live_ref, s32[1]{0:T(128)} %bitcast.outer_ref, bf16[16,256,256]{2,1,0:T(8,128)(2,1)} %bitcast.19, ...), custom_call_target="tpu_custom_call" | custom-call | flops 24999999488 | tf_op jit(solution)/shard_map/score_grad/pallas_call | solution.py:412
  190.7 4.6 %all-to-all-start.6 = ((bf16[4,1024,256]{2,1,0:T(8,128)(2,1)}), bf16[4,1024,256]{2,1,0:T(8,128)(2,1)}, u32[]{:S(2)}, u32[]{:S(2)}) async-start(bf16[4,1024,256]{2,1,0:T(8,128)(2,1)} %bitcast.21), calls=%async_computation.7 | async-start | bytes 4194304 | tf_op jit(solution)/shard_map/all_to_all | solution.py:470
  195.3 1.8 collective-permute-start.3
  197.2 2.2 reduce-scatter.2.cloned.1.call-done
  199.4 1.8 convert_element_type.3
  201.2 24.4 %collective-permute-done.3.refs_1_ = f32[4,256,128]{2,1,0:T(8,128)S(1)} collective-permute-done((f32[4,256,128]{2,1,0:T(8,128)S(1)}, f32[4,256,128]{2,1,0:T(8,128)S(1)}, u32[]{:S(2)}, u32[]{:S(2)}) %collective-permute-start.3) | collective-permute-done | bytes 524320 | tf_op jit(solution)/shard_map/ppermute | solution.py:478
  225.6 0.8 copy-done.4
  226.4 2.0 combine_query.1
  228.4 4.8 %all-to-all-start.7 = ((bf16[4,128,256]{2,1,0:T(8,128)(2,1)}), bf16[4,128,256]{2,1,0:T(8,128)(2,1)S(1)}, u32[]{:S(2)}, u32[]{:S(2)}) async-start(bf16[4,128,256]{2,1,0:T(8,128)(2,1)} %combine_query.1), calls=%async_computation.8 | async-start | bytes 524288 | tf_op jit(solution)/shard_map/all_to_all | solution.py:470
  233.2 1.6 copy.20
  234.8 3.2 %copy.19 = bf16[4,128,8,256]{3,2,0,1:T(8,128)(2,1)} copy(bf16[4,128,8,256]{3,2,1,0:T(8,128)(2,1)} %bitcast.10) | data formatting | bytes 4194304 | tf_op jit(solution)/shard_map/reshape | solution.py:485
  238.0 0.6 all-to-all-done.7
  238.6 0.2 copy.15
  238.7 0.9 copy.18
  (16 shorter events, 0.0 us)
Async XLA Ops:
  7.2 29.3 %all-gather.2.cloned.1.call-start = ((), (), s32[]{:S(2)}) async-start(), calls=%async_computation.9 | async-start | bytes 1310720 | tf_op jit(solution)/shard_map/all_gather | solution.py:492
  9.7 21.8 %all-to-all-start.2 = ((bf16[8,128,256]{2,1,0:T(8,128)(2,1)}), bf16[8,128,256]{2,1,0:T(8,128)(2,1)S(1)}, u32[]{:S(2)}, u32[]{:S(2)}) async-start(bf16[8,128,256]{2,1,0:T(8,128)(2,1)} %spread.1), calls=%async_computation.2 | async-start | bytes 1048576 | tf_op jit(solution)/shard_map/all_to_all | solution.py:475
  31.5 0.8 copy-start.1
  32.3 28.5 %all-to-all-start = ((bf16[4,1024,256]{2,1,0:T(8,128)(2,1)}), bf16[4,1024,256]{2,1,0:T(8,128)(2,1)S(1)}, u32[]{:S(2)}, u32[]{:S(2)}) async-start(bf16[4,1024,256]{2,1,0:T(8,128)(2,1)} %project.2), calls=%async_computation | async-start | bytes 4194304 | tf_op jit(solution)/shard_map/all_to_all | solution.py:470
  60.8 1.3 copy-start
  62.1 30.2 %all-to-all-start.1 = ((bf16[4,1024,256]{2,1,0:T(8,128)(2,1)}), bf16[4,1024,256]{2,1,0:T(8,128)(2,1)}, u32[]{:S(2)}, u32[]{:S(2)}) async-start(bf16[4,1024,256]{2,1,0:T(8,128)(2,1)} %project.3), calls=%async_computation.1 | async-start | bytes 4194304 | tf_op jit(solution)/shard_map/all_to_all | solution.py:470
  80.2 9.3 %collective-permute-start = (f32[2,8,2,256]{3,2,1,0:T(2,128)}, f32[2,8,2,256]{3,2,1,0:T(2,128)S(1)}, u32[]{:S(2)}, u32[]{:S(2)}) collective-permute-start(f32[2,8,2,256]{3,2,1,0:T(2,128)} %stats.1.refs_0_), channel_id=1, source_target_pairs={{0,16},{4,20},{8,24},{12,28},{16,0},{20,4},{24,8},{28,12},{1,17},{... | collective-permute-start | bytes 98312 | tf_op jit(solution)/shard_map/ppermute | solution.py:478
  89.5 0.6 copy-start.6
  92.4 19.0 %all-to-all-start.3 = ((bf16[8,128,256]{2,1,0:T(8,128)(2,1)}), bf16[8,128,256]{2,1,0:T(8,128)(2,1)S(1)}, u32[]{:S(2)}, u32[]{:S(2)}) async-start(bf16[8,128,256]{2,1,0:T(8,128)(2,1)} %bitcast.2), calls=%async_computation.3 | async-start | bytes 1048576 | tf_op jit(solution)/shard_map/all_to_all | solution.py:475
  111.4 12.4 %copy-start.2 = (bf16[8,128,256]{2,1,0:T(8,128)(2,1)}, bf16[8,128,256]{2,1,0:T(8,128)(2,1)S(1)}, u32[]{:S(2)}) copy-start(bf16[8,128,256]{2,1,0:T(8,128)(2,1)S(1)} %all-to-all-done.3.g_ref.refs_3_) | copy-start | bytes 1572868
  111.4 27.6 %collective-permute-start.1 = (f32[4,256,128]{2,1,0:T(8,128)}, f32[4,256,128]{2,1,0:T(8,128)S(1)}, u32[]{:S(2)}, u32[]{:S(2)}) collective-permute-start(f32[4,256,128]{2,1,0:T(8,128)} %context.2), channel_id=1, source_target_pairs={{0,16},{4,20},{8,24},{12,28},{16,0},{20,4},{24,8},{28,12},{1,17},{... | collective-permute-start | bytes 1572872 | tf_op jit(solution)/shard_map/ppermute | solution.py:478
  139.0 0.8 copy-start.5
  142.1 4.8 %collective-permute-start.2 = (f32[4,2,256]{2,1,0:T(2,128)}, f32[4,2,256]{2,1,0:T(2,128)S(1)}, u32[]{:S(2)}, u32[]{:S(2)}) collective-permute-start(f32[4,2,256]{2,1,0:T(2,128)} %get-tuple-element.41.rest_0_), channel_id=1, source_target_pairs={{0,16},{4,20},{8,24},{12,28},{16,0},{20,4},{24,8},{28,12},{1,17},{... | collective-permute-start | bytes 24584 | tf_op jit(solution)/shard_map/ppermute | solution.py:478
  146.8 9.8 %copy-start.7 = (f32[4,2,256]{2,1,0:T(2,128)}, f32[4,2,256]{2,1,0:T(2,128)S(1)}, u32[]{:S(2)}) copy-start(f32[4,2,256]{2,1,0:T(2,128)S(1)} %collective-permute-done.2.rest_1_) | copy-start | bytes 24580
  156.7 34.0 %all-to-all-start.5 = ((bf16[4,1024,256]{2,1,0:T(8,128)(2,1)}), bf16[4,1024,256]{2,1,0:T(8,128)(2,1)S(1)}, u32[]{:S(2)}, u32[]{:S(2)}) async-start(bf16[4,1024,256]{2,1,0:T(8,128)(2,1)} %bitcast.20), calls=%async_computation.6 | async-start | bytes 4194304 | tf_op jit(solution)/shard_map/all_to_all | solution.py:470
  160.3 39.1 %reduce-scatter.2.cloned.1.call-start = ((), (), s32[]{:S(2)}) async-start(), calls=%async_computation.10 | async-start | bytes 2621440 | tf_op jit(solution)/shard_map/reduce_scatter | solution.py:561
  190.7 4.6 %copy-start.3 = (f32[4,256,128]{2,1,0:T(8,128)S(1)}, f32[4,256,128]{2,1,0:T(8,128)}, u32[]{:S(2)}) copy-start(f32[4,256,128]{2,1,0:T(8,128)} %get-tuple-element.46) | copy-start | bytes 1572868
  190.7 37.7 %all-to-all-start.6 = ((bf16[4,1024,256]{2,1,0:T(8,128)(2,1)}), bf16[4,1024,256]{2,1,0:T(8,128)(2,1)}, u32[]{:S(2)}, u32[]{:S(2)}) async-start(bf16[4,1024,256]{2,1,0:T(8,128)(2,1)} %bitcast.21), calls=%async_computation.7 | async-start | bytes 4194304 | tf_op jit(solution)/shard_map/all_to_all | solution.py:470
  195.3 30.2 %collective-permute-start.3 = (f32[4,256,128]{2,1,0:T(8,128)S(1)}, f32[4,256,128]{2,1,0:T(8,128)S(1)}, u32[]{:S(2)}, u32[]{:S(2)}) collective-permute-start(f32[4,256,128]{2,1,0:T(8,128)S(1)} %copy-done.3), channel_id=1, source_target_pairs={{0,16},{4,20},{8,24},{12,28},{16,0},{20,4},{24,8},{28,12},{1,17},{... | collective-permute-start | bytes 1572872 | tf_op jit(solution)/shard_map/ppermute | solution.py:478
  225.6 0.8 copy-start.4
  228.4 10.1 %all-to-all-start.7 = ((bf16[4,128,256]{2,1,0:T(8,128)(2,1)}), bf16[4,128,256]{2,1,0:T(8,128)(2,1)S(1)}, u32[]{:S(2)}, u32[]{:S(2)}) async-start(bf16[4,128,256]{2,1,0:T(8,128)(2,1)} %combine_query.1), calls=%async_computation.8 | async-start | bytes 524288 | tf_op jit(solution)/shard_map/all_to_all | solution.py:470
Sparse Core Ops, SparseCore 0:
  9.6 19.4 all-gather.1
  167.4 31.9 reduce-scatter.1

commit v5 on v4

--- a/solution.py
+++ b/solution.py
@@ -201,11 +201,14 @@
 
     lax.fori_loop(0, n_q, question, 0)
 
-    def finish(slot, carry):
-        o_ref[slot] = acc[slot].astype(BF16)
-        return carry
-
-    lax.fori_loop(0, k_ref.shape[0], finish, 0)
+    per = k_ref.shape[0] // o_ref.shape[0]
+
+    def finish(owner, carry):
+        for place in range(per):
+            o_ref[owner, place * PLEN : (place + 1) * PLEN] = acc[owner * per + place].astype(BF16)
+        return carry
+
+    lax.fori_loop(0, o_ref.shape[0], finish, 0)
 
 
 def turn(src_ref, dst_ref):
@@ -314,16 +317,15 @@
 
 
 def combine_context_kernel(n_parts, outer_ref, *refs):
-    parts, (st_ref, g_ref, o_ref, dot_ref) = refs[:n_parts], refs[n_parts:]
+    parts, (st_ref, g_ref, _, o_ref, dot_ref, ctx_ref, sem) = refs[:n_parts], refs[n_parts:]
     width = g_ref.shape[2]
-    inner = o_ref.shape[0]
+    inner, rows = ctx_ref.shape[0], ctx_ref.shape[1]
     first = outer_ref[0] * inner
     for q in range(inner):
         mix = parts[0][q]
         for part in parts[1:]:
             mix = mix + part[q]
         grad = jnp.transpose(g_ref[first + q].astype(F32))
-        rows = mix.shape[1]
         pieces = []
         for head in range(width // HEAD_DIM):
             feats = slice(head * HEAD_DIM, (head + 1) * HEAD_DIM)
@@ -332,7 +334,10 @@
             ctx = (mix[feats] / total).astype(BF16).astype(F32)
             dot_ref[q, pair : pair + 1, lanes] = jnp.sum(grad[feats] * ctx, axis=0, keepdims=True)
             pieces.append(ctx)
-        o_ref[q] = jnp.transpose(jnp.concatenate(pieces, axis=0)).astype(BF16)
+        ctx_ref[q] = jnp.transpose(jnp.concatenate(pieces, axis=0)).astype(BF16)
+    copy = pltpu.make_async_copy(ctx_ref, o_ref.at[:, pl.ds(o_ref.shape[1] - rows, rows), :], sem)
+    copy.start()
+    copy.wait()
 
 
 def combine_query_kernel(n_parts, *refs):
@@ -388,22 +393,43 @@
         o_ref[...] += part
 
 
-def out_project(x, w):
-    blocks, rows, width = x.shape
+def out_project(x, rows, w):
+    blocks, length, width = x.shape
     cols = w.shape[1]
     return pl.pallas_call(
         out_project_kernel,
         grid=(blocks,),
         in_specs=[
-            pl.BlockSpec((1, rows, width), lambda j: (j, 0, 0)),
+            pl.BlockSpec((1, rows, width), lambda j: (j, length // rows - 1, 0)),
             pl.BlockSpec((width, cols), lambda j: (j, 0)),
         ],
         out_specs=pl.BlockSpec((rows, cols), lambda j: (0, 0)),
         out_shape=jax.ShapeDtypeStruct((rows, cols), F32),
         compiler_params=params(("arbitrary",)),
-        cost_estimate=cost_us(5),
+        cost_estimate=cost_us(1),
         name="out_project",
     )(x, w)
+
+
+def collect_kernel(x_ref, o_ref):
+    width = x_ref.shape[2]
+    for block in range(x_ref.shape[0]):
+        o_ref[:, block * width : (block + 1) * width] = x_ref[block]
+
+
+def collect(x, rows):
+    blocks, _, width = x.shape
+    tile = min(rows, 512)
+    return pl.pallas_call(
+        collect_kernel,
+        grid=(rows // tile,),
+        in_specs=[pl.BlockSpec((blocks, tile, width), lambda m: (0, m, 0))],
+        out_specs=pl.BlockSpec((tile, blocks * width), lambda m: (m, 0)),
+        out_shape=jax.ShapeDtypeStruct((rows, blocks * width), x.dtype),
+        compiler_params=params(("arbitrary",)),
+        cost_estimate=cost_us(1),
+        name="collect",
+    )(x)
 
 
 def vmem_call(kernel, scalars, arrays, out_shape, scratch, time, name):
@@ -481,9 +507,6 @@
             [(o * inner + i, ((o + r) % n_outer) * inner + i) for o in range(n_outer) for i in range(inner)],
         )
 
-    def from_block(x):
-        return jnp.transpose(x, (1, 0, 2)).reshape(x.shape[1], head_width)
-
     def partials(parts):
         return [parts[0]] + [to_outer(parts[r], r) for r in range(1, n_outer)]
 
@@ -533,7 +556,7 @@
             (keys, values, q_all, norm_then),
             mix_shape,
             [turned_pair, turned],
-            10,
+            5 if r == 0 else 14,
             "context",
         )
         norm_then = after(norm, mixes[r], g_all)
@@ -541,45 +564,53 @@
         value_grad_kernel,
         (pick, live),
         (keys, q_all, g_all, norm_then),
-        sds((n_local, PLEN, width), BF16),
+        sds((inner, tok_local + rows, width), BF16),
         [turned_pair, pair_scratch, acc_scratch],
-        15,
+        5,
         "value_grad",
     )
-    context, grad_dot = vmem_call(
+    smem, vmem = pl.BlockSpec(memory_space=pltpu.SMEM), pl.BlockSpec(memory_space=pltpu.VMEM)
+    anywhere = pl.BlockSpec(memory_space=pl.ANY)
+    packed, grad_dot = pl.pallas_call(
         functools.partial(combine_context_kernel, n_outer),
-        (outer,),
-        partials([after(mix, g_all) for mix in mixes]) + [after(norm, value_done), g_all],
-        (sds((inner, rows, width), BF16), sds((inner, n_pair, 2 * rows), F32)),
-        [],
-        2,
-        "combine_context",
-    )
+        in_specs=[smem] + [vmem] * (n_outer + 2) + [anywhere],
+        out_specs=(anywhere, vmem),
+        out_shape=(
+            sds((inner, tok_local + rows, width), BF16),
+            sds((inner, n_pair, 2 * rows), F32),
+        ),
+        scratch_shapes=[pltpu.VMEM((inner, rows, width), BF16), pltpu.SemaphoreType.DMA],
+        input_output_aliases={n_outer + 3: 0},
+        compiler_params=params(),
+        cost_estimate=cost_us(3),
+        name="combine_context",
+    )(outer, *partials([after(mix, g_all) for mix in mixes]), norm, g_all, value_done)
     dots = [grad_dot] + [to_outer(grad_dot, n_outer - r) for r in range(1, n_outer)]
-    projected = out_project(swap(after(context, *dots[1:])), out_weight)
-    value_back = swap(value_done.reshape(inner, tok_local, width))
-    output = lax.psum_scatter(projected, "head", scatter_dimension=1, tiled=True).astype(BF16)
+    packed_back = swap(after(packed, *dots[1:]))
+    value_grad = collect(packed_back, tok_local)
     done = vmem_call(
         functools.partial(score_grad_kernel, n_outer),
         (pick, live, outer),
-        [keys, values, q_all, g_all, after(norm, projected)] + dots,
+        [keys, values, q_all, g_all, norm] + dots,
         (sds((n_local, PLEN, width), BF16),) + (mix_shape,) * n_outer,
         [turned_pair, pair_scratch, turned_pair, turned, acc_scratch],
         25,
         "score_grad",
     )
-    key_back = swap(after(done[0], value_back).reshape(inner, tok_local, width))
+    projected = out_project(after(packed_back, done[0]), rows, out_weight)
+    output = lax.psum_scatter(projected, "head", scatter_dimension=1, tiled=True).astype(BF16)
+    key_back = swap(after(done[0], projected).reshape(inner, tok_local, width))
     query_done = vmem_call(
         functools.partial(combine_query_kernel, n_outer),
         (),
-        [after(done[1], output)] + partials(done[1:])[1:],
+        [after(done[1], value_grad)] + partials(done[1:])[1:],
         sds((inner, rows, width), BF16),
         [],
-        2,
+        40,
         "combine_query",
     )
-    query_grad = from_block(swap(after(query_done, key_back)))
-    key_grad, value_grad = from_block(key_back), from_block(value_back)
+    query_grad = collect(swap(after(query_done, key_back)), rows)
+    key_grad = collect(key_back, tok_local)
     return (output, query_grad, key_grad, value_grad)
 
 

time: 248 us -> 242 us (0.976)
  blocking collectives: 9.84 us -> 0 us
  Pallas kernels: 127 us -> 135 us
  local copies, waits for them, and re-layouts: 10.2 us -> 7.1 us
    all_to_all x5, waiting for transfers between devices: 2.45 us -> 25.5 us  [swap(): lax.all_to_all(x, 'pas', split_axis=0, concat_axis=0, tiled=True, axis_in...]
    ppermute x4, waiting for transfers between devices: 34.1 us -> 15.3 us  [to_outer(): lax.ppermute(x, 'pas', [(o * inner + i, (o + r) % n_outer * inner + i) fo...]
    pallas_call x0 -> x4, Pallas kernels: none -> 10.3 us  [the longest x3 7.35 us: collect(): pl.pallas_call(collect_kernel, grid=(rows // tile,), in_specs=[pl.BlockSp...]
    all_to_all x1 -> x0, blocking collectives: 9.84 us -> none  [swap(): lax.all_to_all(x, 'pas', split_axis=0, concat_axis=0, tiled=True, axis_in...]
    reshape x2 -> x0, local copies, waits for them, and re-layouts: 4.81 us -> none  [from_block(): return jnp.transpose(x, (1, 0, 2)).reshape(x.shape[1], head_width)]
    pallas_call x9 -> x8, Pallas kernels: 82.2 us -> 79.9 us  [vmem_call(): pl.pallas_call(kernel, in_specs=[smem] * len(scalars) + [vmem] * len(arra...]
    unnamed x17 -> x20, local copies, waits for them, and re-layouts: 5.21 us -> 7.1 us
  transfers between devices with their start and end apart: 13 -> 13, of which waited for: 8 -> 9; matrix products, arithmetic and copies ran while one was open for 3% -> 0% of each run, Pallas kernels for 50% -> 55%
where the time goes in v5:
time: 242 us; the launch traced here: 241 us
  Pallas kernels  135 us (56%)
  waiting for transfers between devices  43.3 us (18%)
  starting transfers between devices  40.2 us (17%)
  between operations  14.1 us (6%)
  local copies, waits for them, and re-layouts  7.1 us (3%)
    pallas_call x8, Pallas kernels, vmem_call(): pl.pallas_call(kernel, in_specs=[smem] * len(scalars) + [vmem] * len(arra...  79.9 us
    pallas_call x2, Pallas kernels, project(): pl.pallas_call(project_kernel, grid=(rows // tile,), in_specs=[pl.BlockSp...  28.7 us
    all_to_all x5, waiting for transfers between devices, swap(): lax.all_to_all(x, 'pas', split_axis=0, concat_axis=0, tiled=True, axis_in...  25.5 us
    all_to_all x5, starting transfers between devices, swap(): lax.all_to_all(x, 'pas', split_axis=0, concat_axis=0, tiled=True, axis_in...  19.3 us
    ppermute x4, waiting for transfers between devices, to_outer(): lax.ppermute(x, 'pas', [(o * inner + i, (o + r) % n_outer * inner + i) fo...  15.3 us
    all_to_all x2, starting transfers between devices, swap_all(): return lax.all_to_all(x, 'pas', split_axis=0, concat_axis=0, tiled=True)  13.3 us
    pallas_call x3, Pallas kernels, collect(): pl.pallas_call(collect_kernel, grid=(rows // tile,), in_specs=[pl.BlockSp...  7.35 us
    ppermute x4, starting transfers between devices, to_outer(): lax.ppermute(x, 'pas', [(o * inner + i, (o + r) % n_outer * inner + i) fo...  7.34 us
  transfers between devices with their start and end apart: 13, of which 9 were waited for; matrix products, arithmetic and copies ran while one was open for 0% of the time, Pallas kernels for 55%

profile of v5, /device:TPU:0, one launch (start us, length us, event | category | flops | bytes accessed | tf_op | source)
XLA Modules:
  0.0 241.2 jit_solution(633827775993448139)
XLA Ops:
  7.2 0.7 all-gather.2.cloned.1.call-update
  7.9 1.8 spread.1
  9.7 7.3 %all-to-all-start.2 = ((bf16[8,128,256]{2,1,0:T(8,128)(2,1)}), bf16[8,128,256]{2,1,0:T(8,128)(2,1)S(1)}, u32[]{:S(2)}, u32[]{:S(2)}) async-start(bf16[8,128,256]{2,1,0:T(8,128)(2,1)} %spread.1), calls=%async_computation.2 | async-start | bytes 1048576 | tf_op jit(solution)/shard_map/all_to_all | solution.py:501
  17.0 14.6 %project.2 = bf16[4,1024,256]{2,1,0:T(8,128)(2,1)} custom-call(bf16[1024,4096]{1,0:T(8,128)(2,1)} %x_ref.3, bf16[4096,1024]{1,0:T(8,128)(2,1)} %w_ref.4), custom_call_target="tpu_custom_call" | custom-call | flops 14000000000 | tf_op jit(solution)/shard_map/project/pallas_call | solution.py:55
  31.5 0.8 copy-done.3
  32.3 4.2 %all-to-all-start = ((bf16[4,1024,256]{2,1,0:T(8,128)(2,1)}), bf16[4,1024,256]{2,1,0:T(8,128)(2,1)S(1)}, u32[]{:S(2)}, u32[]{:S(2)}) async-start(bf16[4,1024,256]{2,1,0:T(8,128)(2,1)} %project.2), calls=%async_computation | async-start | bytes 4194304 | tf_op jit(solution)/shard_map/all_to_all | solution.py:496
  36.5 14.2 %project.3 = bf16[4,1024,256]{2,1,0:T(8,128)(2,1)} custom-call(bf16[1024,4096]{1,0:T(8,128)(2,1)} %x_ref.3, bf16[4096,1024]{1,0:T(8,128)(2,1)} %w_ref.5), custom_call_target="tpu_custom_call" | custom-call | flops 14000000000 | tf_op jit(solution)/shard_map/project/pallas_call | solution.py:55
  50.7 2.3 route.1
  53.0 6.8 %context_grad.1 = bf16[2,4,128,256]{3,2,1,0:T(8,128)(2,1)} custom-call(bf16[128,4096]{1,0:T(8,128)(2,1)} %all-gather.2.cloned.1.call-done.x_ref, bf16[1024,4096]{1,0:T(8,128)(2,1)} %w_ref.7), custom_call_target="tpu_custom_call" | custom-call | flops 5000000000 | tf_op jit(solution)/shard_map/context_grad/pallas_call | solution.py:368
  59.8 1.0 all-to-all-done
  60.8 1.3 copy-done.2
  62.1 4.5 %all-to-all-start.1 = ((bf16[4,1024,256]{2,1,0:T(8,128)(2,1)}), bf16[4,1024,256]{2,1,0:T(8,128)(2,1)}, u32[]{:S(2)}, u32[]{:S(2)}) async-start(bf16[4,1024,256]{2,1,0:T(8,128)(2,1)} %project.3), calls=%async_computation.1 | async-start | bytes 4194304 | tf_op jit(solution)/shard_map/all_to_all | solution.py:496
  66.6 13.6 %stats.1.refs_0_ = f32[2,8,2,256]{3,2,1,0:T(2,128)} custom-call(s32[8,24]{1,0:T(8,128)} %get-tuple-element.29.pick_ref, s32[8]{0:T(128)} %get-tuple-element.30.live_ref, bf16[16,256,256]{2,1,0:T(8,128)(2,1)} %bitcast.5, bf16[8,128,256]{2,1,0:T(8,128)(2,1)} %copy-done.3), custom_call_target="tpu_custom_call" | custom-call | flops 12999999488 | tf_op jit(solution)/shard_map/stats/pallas_call | solution.py:438
  80.2 2.6 %collective-permute-start = (f32[2,8,2,256]{3,2,1,0:T(2,128)}, f32[2,8,2,256]{3,2,1,0:T(2,128)S(1)}, u32[]{:S(2)}, u32[]{:S(2)}) collective-permute-start(f32[2,8,2,256]{3,2,1,0:T(2,128)} %stats.1.refs_0_), channel_id=1, source_target_pairs={{0,16},{4,20},{8,24},{12,28},{16,0},{20,4},{24,8},{28,12},{1,17},{... | collective-permute-start | bytes 98312 | tf_op jit(solution)/shard_map/ppermute | solution.py:504
  82.8 6.7 %collective-permute-done.refs_1_ = f32[2,8,2,256]{3,2,1,0:T(2,128)S(1)} collective-permute-done((f32[2,8,2,256]{3,2,1,0:T(2,128)}, f32[2,8,2,256]{3,2,1,0:T(2,128)S(1)}, u32[]{:S(2)}, u32[]{:S(2)}) %collective-permute-start) | collective-permute-done | bytes 32800 | tf_op jit(solution)/shard_map/ppermute | solution.py:504
  89.5 0.6 copy-done.8
  90.1 1.4 merge.1.st_ref.refs_2_
  91.5 0.8 all-to-all-done.1
  92.4 6.0 %all-to-all-start.3 = ((bf16[8,128,256]{2,1,0:T(8,128)(2,1)}), bf16[8,128,256]{2,1,0:T(8,128)(2,1)S(1)}, u32[]{:S(2)}, u32[]{:S(2)}) async-start(bf16[8,128,256]{2,1,0:T(8,128)(2,1)} %bitcast.2), calls=%async_computation.3 | async-start | bytes 1048576 | tf_op jit(solution)/shard_map/all_to_all | solution.py:501
  98.4 11.2 %context.2 = f32[4,256,128]{2,1,0:T(8,128)} custom-call(s32[8,24]{1,0:T(8,128)} %get-tuple-element.29.pick_ref, s32[8]{0:T(128)} %get-tuple-element.30.live_ref, s32[1]{0:T(128)} %bitcast.outer_ref, bf16[16,256,256]{2,1,0:T(8,128)(2,1)} %bitcast.6, bf16[16,256,256]{2,1,0:T(8,128)(2,1)} %bitcast.3.v_ref, bf16[8,128,256]{2,1,0:T(8,128)(2,1)} %copy-done.3, ...), custom_call_target="tpu_custom_call" | custom-call | flops 14000000000 | tf_op jit(solution)/shard_map/context/pallas_call | solution.py:438
  109.6 1.8 all-to-all-done.3.g_ref.refs_3_
  111.4 1.2 collective-permute-start.1
  112.6 11.2 %context.3.refs_0_ = f32[4,256,128]{2,1,0:T(8,128)} custom-call(s32[8,24]{1,0:T(8,128)} %get-tuple-element.29.pick_ref, s32[8]{0:T(128)} %get-tuple-element.30.live_ref, s32[1]{0:T(128)} %bitcast.outer_ref, bf16[16,256,256]{2,1,0:T(8,128)(2,1)} %bitcast.7, bf16[16,256,256]{2,1,0:T(8,128)(2,1)} %bitcast.3.v_ref, bf16[8,128,256]{2,1,0:T(8,128)(2,1)} %copy-done.3, ...), custom_call_target="tpu_custom_call" | custom-call | flops 5000000000 | tf_op jit(solution)/shard_map/context/pallas_call | solution.py:438
  123.7 15.3 %value_grad.1.refs_4_ = bf16[4,1152,256]{2,1,0:T(8,128)(2,1)} custom-call(s32[8,24]{1,0:T(8,128)} %get-tuple-element.29.pick_ref, s32[8]{0:T(128)} %get-tuple-element.30.live_ref, bf16[16,256,256]{2,1,0:T(8,128)(2,1)} %bitcast.8, bf16[8,128,256]{2,1,0:T(8,128)(2,1)} %copy-done.3, bf16[8,128,256]{2,1,0:T(8,128)(2,1)} %copy-done.4, ...), custom_call_target="tpu_custom_call" | custom-call | flops 5000000000 | tf_op jit(solution)/shard_map/value_grad/pallas_call | solution.py:438
  139.0 0.8 copy-done.7
  139.8 2.9 %combine_context.1 = (bf16[4,1152,256]{2,1,0:T(8,128)(2,1)}, f32[4,2,256]{2,1,0:T(2,128)}) custom-call(s32[1]{0:T(128)} %bitcast.outer_ref, f32[4,256,128]{2,1,0:T(8,128)} %context.3.refs_0_, f32[4,256,128]{2,1,0:T(8,128)} %copy-done.7, f32[3,8,2,256]{3,2,1,0:T(2,128)} %merge.1.st_ref.refs_2_, ...), custom_call_target="tpu_custom_call", output_to_operand_aliasing={{0}: (5, {})} | custom-call | flops 3000000000 | tf_op jit(solution)/shard_map/combine_context/pallas_call | solution.py:574
  142.8 1.8 collective-permute-start.2
  144.6 3.0 %collective-permute-done.2.rest_1_ = f32[4,2,256]{2,1,0:T(2,128)S(1)} collective-permute-done((f32[4,2,256]{2,1,0:T(2,128)}, f32[4,2,256]{2,1,0:T(2,128)S(1)}, u32[]{:S(2)}, u32[]{:S(2)}) %collective-permute-start.2) | collective-permute-done | bytes 8224 | tf_op jit(solution)/shard_map/ppermute | solution.py:504
  147.6 0.6 copy-done.9
  148.2 3.6 %all-to-all-start.4 = ((bf16[4,1152,256]{2,1,0:T(8,128)(2,1)}), bf16[4,1152,256]{2,1,0:T(8,128)(2,1)S(1)}, u32[]{:S(2)}, u32[]{:S(2)}) async-start(bf16[4,1152,256]{2,1,0:T(8,128)(2,1)} %get-tuple-element.40), calls=%async_computation.4 | async-start | bytes 4718592 | tf_op jit(solution)/shard_map/all_to_all | solution.py:496
  151.8 0.2 reduce-scatter.2.cloned.1.call-start
  152.0 23.4 %score_grad.1 = (bf16[16,256,256]{2,1,0:T(8,128)(2,1)}, f32[4,256,128]{2,1,0:T(8,128)}, f32[4,256,128]{2,1,0:T(8,128)}) custom-call(s32[8,24]{1,0:T(8,128)} %get-tuple-element.29.pick_ref, s32[8]{0:T(128)} %get-tuple-element.30.live_ref, s32[1]{0:T(128)} %bitcast.outer_ref, bf16[16,256,256]{2,1,0:T(8,128)(2,1)} %bitcast.9, ...), custom_call_target="tpu_custom_call" | custom-call | flops 24999999488 | tf_op jit(solution)/shard_map/score_grad/pallas_call | solution.py:438
  175.5 1.8 collective-permute-start.3
  177.2 1.0 all-to-all-done.4.x_ref
  178.2 1.4 copy-done
  179.6 6.7 %out_project.1 = f32[128,4096]{1,0:T(8,128)} custom-call(bf16[4,1152,256]{2,1,0:T(8,128)(2,1)} %copy-done, bf16[1024,4096]{1,0:T(8,128)(2,1)} %w_ref.7), custom_call_target="tpu_custom_call" | custom-call | flops 1000000000 | tf_op jit(solution)/shard_map/out_project/pallas_call | solution.py:399
  186.3 3.6 %all-to-all-start.5 = ((bf16[4,1024,256]{2,1,0:T(8,128)(2,1)}), bf16[4,1024,256]{2,1,0:T(8,128)(2,1)S(1)}, u32[]{:S(2)}, u32[]{:S(2)}) async-start(bf16[4,1024,256]{2,1,0:T(8,128)(2,1)} %bitcast.10), calls=%async_computation.6 | async-start | bytes 4194304 | tf_op jit(solution)/shard_map/all_to_all | solution.py:496
  190.0 3.0 %collect.3 = bf16[1024,1024]{1,0:T(8,128)(2,1)} custom-call(bf16[4,1152,256]{2,1,0:T(8,128)(2,1)} %copy-done), custom_call_target="tpu_custom_call" | custom-call | flops 1000000000 | tf_op jit(solution)/shard_map/collect/pallas_call | solution.py:423
  192.9 5.6 %collective-permute-done.3.refs_1_ = f32[4,256,128]{2,1,0:T(8,128)S(1)} collective-permute-done((f32[4,256,128]{2,1,0:T(8,128)}, f32[4,256,128]{2,1,0:T(8,128)S(1)}, u32[]{:S(2)}, u32[]{:S(2)}) %collective-permute-start.3) | collective-permute-done | bytes 524320 | tf_op jit(solution)/shard_map/ppermute | solution.py:504
  198.6 0.8 copy-done.6
  199.4 2.0 combine_query.1
  201.4 19.5 %all-to-all-done.5.x_ref = bf16[4,1024,256]{2,1,0:T(8,128)(2,1)S(1)} async-done(((bf16[4,1024,256]{2,1,0:T(8,128)(2,1)}), bf16[4,1024,256]{2,1,0:T(8,128)(2,1)S(1)}, u32[]{:S(2)}, u32[]{:S(2)}) %all-to-all-start.5) | async-done | bytes 2097184 | tf_op jit(solution)/shard_map/all_to_all | solution.py:496
  221.0 3.4 %all-to-all-start.6 = ((bf16[4,128,256]{2,1,0:T(8,128)(2,1)}), bf16[4,128,256]{2,1,0:T(8,128)(2,1)S(1)}, u32[]{:S(2)}, u32[]{:S(2)}) async-start(bf16[4,128,256]{2,1,0:T(8,128)(2,1)} %combine_query.1), calls=%async_computation.7 | async-start | bytes 524288 | tf_op jit(solution)/shard_map/all_to_all | solution.py:496
  224.4 2.7 %collect.5 = bf16[1024,1024]{1,0:T(8,128)(2,1)} custom-call(bf16[4,1024,256]{2,1,0:T(8,128)(2,1)} %copy-done.1), custom_call_target="tpu_custom_call" | custom-call | flops 1000000000 | tf_op jit(solution)/shard_map/collect/pallas_call | solution.py:423
  227.1 3.1 %all-to-all-done.6.x_ref = bf16[4,128,256]{2,1,0:T(8,128)(2,1)S(1)} async-done(((bf16[4,128,256]{2,1,0:T(8,128)(2,1)}), bf16[4,128,256]{2,1,0:T(8,128)(2,1)S(1)}, u32[]{:S(2)}, u32[]{:S(2)}) %all-to-all-start.6) | async-done | bytes 262176 | tf_op jit(solution)/shard_map/all_to_all | solution.py:496
  230.2 0.7 copy-done.5
  230.9 1.7 collect.4
  232.6 1.8 convert_element_type.3
  (18 shorter events, 0.1 us)
Async XLA Ops:
  7.2 29.3 %all-gather.2.cloned.1.call-start = ((), (), s32[]{:S(2)}) async-start(), calls=%async_computation.8 | async-start | bytes 1310720 | tf_op jit(solution)/shard_map/all_gather | solution.py:515
  9.7 21.8 %all-to-all-start.2 = ((bf16[8,128,256]{2,1,0:T(8,128)(2,1)}), bf16[8,128,256]{2,1,0:T(8,128)(2,1)S(1)}, u32[]{:S(2)}, u32[]{:S(2)}) async-start(bf16[8,128,256]{2,1,0:T(8,128)(2,1)} %spread.1), calls=%async_computation.2 | async-start | bytes 1048576 | tf_op jit(solution)/shard_map/all_to_all | solution.py:501
  31.5 0.8 copy-start.3
  32.3 28.5 %all-to-all-start = ((bf16[4,1024,256]{2,1,0:T(8,128)(2,1)}), bf16[4,1024,256]{2,1,0:T(8,128)(2,1)S(1)}, u32[]{:S(2)}, u32[]{:S(2)}) async-start(bf16[4,1024,256]{2,1,0:T(8,128)(2,1)} %project.2), calls=%async_computation | async-start | bytes 4194304 | tf_op jit(solution)/shard_map/all_to_all | solution.py:496
  60.8 1.3 copy-start.2
  62.1 30.2 %all-to-all-start.1 = ((bf16[4,1024,256]{2,1,0:T(8,128)(2,1)}), bf16[4,1024,256]{2,1,0:T(8,128)(2,1)}, u32[]{:S(2)}, u32[]{:S(2)}) async-start(bf16[4,1024,256]{2,1,0:T(8,128)(2,1)} %project.3), calls=%async_computation.1 | async-start | bytes 4194304 | tf_op jit(solution)/shard_map/all_to_all | solution.py:496
  80.2 9.3 %collective-permute-start = (f32[2,8,2,256]{3,2,1,0:T(2,128)}, f32[2,8,2,256]{3,2,1,0:T(2,128)S(1)}, u32[]{:S(2)}, u32[]{:S(2)}) collective-permute-start(f32[2,8,2,256]{3,2,1,0:T(2,128)} %stats.1.refs_0_), channel_id=1, source_target_pairs={{0,16},{4,20},{8,24},{12,28},{16,0},{20,4},{24,8},{28,12},{1,17},{... | collective-permute-start | bytes 98312 | tf_op jit(solution)/shard_map/ppermute | solution.py:504
  89.5 0.6 copy-start.8
  92.4 19.0 %all-to-all-start.3 = ((bf16[8,128,256]{2,1,0:T(8,128)(2,1)}), bf16[8,128,256]{2,1,0:T(8,128)(2,1)S(1)}, u32[]{:S(2)}, u32[]{:S(2)}) async-start(bf16[8,128,256]{2,1,0:T(8,128)(2,1)} %bitcast.2), calls=%async_computation.3 | async-start | bytes 1048576 | tf_op jit(solution)/shard_map/all_to_all | solution.py:501
  111.4 12.4 %copy-start.4 = (bf16[8,128,256]{2,1,0:T(8,128)(2,1)}, bf16[8,128,256]{2,1,0:T(8,128)(2,1)S(1)}, u32[]{:S(2)}) copy-start(bf16[8,128,256]{2,1,0:T(8,128)(2,1)S(1)} %all-to-all-done.3.g_ref.refs_3_) | copy-start | bytes 1572868
  111.4 27.6 %collective-permute-start.1 = (f32[4,256,128]{2,1,0:T(8,128)}, f32[4,256,128]{2,1,0:T(8,128)S(1)}, u32[]{:S(2)}, u32[]{:S(2)}) collective-permute-start(f32[4,256,128]{2,1,0:T(8,128)} %context.2), channel_id=1, source_target_pairs={{0,16},{4,20},{8,24},{12,28},{16,0},{20,4},{24,8},{28,12},{1,17},{... | collective-permute-start | bytes 1572872 | tf_op jit(solution)/shard_map/ppermute | solution.py:504
  139.0 0.8 copy-start.7
  142.8 4.8 %collective-permute-start.2 = (f32[4,2,256]{2,1,0:T(2,128)}, f32[4,2,256]{2,1,0:T(2,128)S(1)}, u32[]{:S(2)}, u32[]{:S(2)}) collective-permute-start(f32[4,2,256]{2,1,0:T(2,128)} %get-tuple-element.39.rest_0_), channel_id=1, source_target_pairs={{0,16},{4,20},{8,24},{12,28},{16,0},{20,4},{24,8},{28,12},{1,17},{... | collective-permute-start | bytes 24584 | tf_op jit(solution)/shard_map/ppermute | solution.py:504
  147.6 0.6 copy-start.9
  148.2 30.0 %all-to-all-start.4 = ((bf16[4,1152,256]{2,1,0:T(8,128)(2,1)}), bf16[4,1152,256]{2,1,0:T(8,128)(2,1)S(1)}, u32[]{:S(2)}, u32[]{:S(2)}) async-start(bf16[4,1152,256]{2,1,0:T(8,128)(2,1)} %get-tuple-element.40), calls=%async_computation.4 | async-start | bytes 4718592 | tf_op jit(solution)/shard_map/all_to_all | solution.py:496
  151.8 80.8 %reduce-scatter.2.cloned.1.call-start = ((), (), s32[]{:S(2)}) async-start(), calls=%async_computation.9 | async-start | bytes 2621440 | tf_op jit(solution)/shard_map/reduce_scatter | solution.py:601
  175.5 23.1 %collective-permute-start.3 = (f32[4,256,128]{2,1,0:T(8,128)}, f32[4,256,128]{2,1,0:T(8,128)S(1)}, u32[]{:S(2)}, u32[]{:S(2)}) collective-permute-start(f32[4,256,128]{2,1,0:T(8,128)} %get-tuple-element.45), channel_id=1, source_target_pairs={{0,16},{4,20},{8,24},{12,28},{16,0},{20,4},{24,8},{28,12},{1,17},{... | collective-permute-start | bytes 1572872 | tf_op jit(solution)/shard_map/ppermute | solution.py:504
  178.2 1.4 copy-start
  186.3 34.7 %all-to-all-start.5 = ((bf16[4,1024,256]{2,1,0:T(8,128)(2,1)}), bf16[4,1024,256]{2,1,0:T(8,128)(2,1)S(1)}, u32[]{:S(2)}, u32[]{:S(2)}) async-start(bf16[4,1024,256]{2,1,0:T(8,128)(2,1)} %bitcast.10), calls=%async_computation.6 | async-start | bytes 4194304 | tf_op jit(solution)/shard_map/all_to_all | solution.py:496
  198.6 0.8 copy-start.6
  221.0 3.4 %copy-start.1 = (bf16[4,1024,256]{2,1,0:T(8,128)(2,1)}, bf16[4,1024,256]{2,1,0:T(8,128)(2,1)S(1)}, u32[]{:S(2)}) copy-start(bf16[4,1024,256]{2,1,0:T(8,128)(2,1)S(1)} %all-to-all-done.5.x_ref) | copy-start | bytes 6291460
  221.0 9.2 %all-to-all-start.6 = ((bf16[4,128,256]{2,1,0:T(8,128)(2,1)}), bf16[4,128,256]{2,1,0:T(8,128)(2,1)S(1)}, u32[]{:S(2)}, u32[]{:S(2)}) async-start(bf16[4,128,256]{2,1,0:T(8,128)(2,1)} %combine_query.1), calls=%async_computation.7 | async-start | bytes 524288 | tf_op jit(solution)/shard_map/all_to_all | solution.py:496
  230.2 0.7 copy-start.5
Sparse Core Ops, SparseCore 0:
  9.6 19.4 all-gather.1
  186.5 30.4 reduce-scatter.1

commit v6 on v5

--- a/solution.py
+++ b/solution.py
@@ -587,7 +587,6 @@
     )(outer, *partials([after(mix, g_all) for mix in mixes]), norm, g_all, value_done)
     dots = [grad_dot] + [to_outer(grad_dot, n_outer - r) for r in range(1, n_outer)]
     packed_back = swap(after(packed, *dots[1:]))
-    value_grad = collect(packed_back, tok_local)
     done = vmem_call(
         functools.partial(score_grad_kernel, n_outer),
         (pick, live, outer),
@@ -598,8 +597,9 @@
         "score_grad",
     )
     projected = out_project(after(packed_back, done[0]), rows, out_weight)
+    value_grad = collect(after(packed_back, projected), tok_local)
     output = lax.psum_scatter(projected, "head", scatter_dimension=1, tiled=True).astype(BF16)
-    key_back = swap(after(done[0], projected).reshape(inner, tok_local, width))
+    key_back = swap(after(done[0], packed_back).reshape(inner, tok_local, width))
     query_done = vmem_call(
         functools.partial(combine_query_kernel, n_outer),
         (),

time: 242 us -> 239 us (0.988)
  waiting for transfers between devices: 43.3 us -> 39.2 us
    all_to_all x5, waiting for transfers between devices: 25.5 us -> 22 us  [swap(): lax.all_to_all(x, 'pas', split_axis=0, concat_axis=0, tiled=True, axis_in...]
    unnamed x20 -> x18, local copies, waits for them, and re-layouts: 7.1 us -> 7.05 us
where the time goes in v6:
time: 239 us; the launch traced here: 238 us
  Pallas kernels  134 us (56%)
  starting transfers between devices  41 us (17%)
  waiting for transfers between devices  39.2 us (16%)
  between operations  14.1 us (6%)
  local copies, waits for them, and re-layouts  7.05 us (3%)
    pallas_call x8, Pallas kernels, vmem_call(): pl.pallas_call(kernel, in_specs=[smem] * len(scalars) + [vmem] * len(arra...  80 us
    pallas_call x2, Pallas kernels, project(): pl.pallas_call(project_kernel, grid=(rows // tile,), in_specs=[pl.BlockSp...  28.7 us
    all_to_all x5, waiting for transfers between devices, swap(): lax.all_to_all(x, 'pas', split_axis=0, concat_axis=0, tiled=True, axis_in...  22 us
    all_to_all x5, starting transfers between devices, swap(): lax.all_to_all(x, 'pas', split_axis=0, concat_axis=0, tiled=True, axis_in...  20.3 us
    ppermute x4, waiting for transfers between devices, to_outer(): lax.ppermute(x, 'pas', [(o * inner + i, (o + r) % n_outer * inner + i) fo...  14.7 us
    all_to_all x2, starting transfers between devices, swap_all(): return lax.all_to_all(x, 'pas', split_axis=0, concat_axis=0, tiled=True)  13.3 us
    ppermute x4, starting transfers between devices, to_outer(): lax.ppermute(x, 'pas', [(o * inner + i, (o + r) % n_outer * inner + i) fo...  7.31 us
    pallas_call x3, Pallas kernels, collect(): pl.pallas_call(collect_kernel, grid=(rows // tile,), in_specs=[pl.BlockSp...  7.09 us
  transfers between devices with their start and end apart: 13, of which 9 were waited for; matrix products, arithmetic and copies ran while one was open for 0% of the time, Pallas kernels for 55%

profile of v6, /device:TPU:0, one launch (start us, length us, event | category | flops | bytes accessed | tf_op | source)
XLA Modules:
  0.0 237.6 jit_solution(3515171233258819136)
XLA Ops:
  7.2 0.7 all-gather.2.cloned.1.call-update
  7.9 1.8 spread.1
  9.7 7.3 %all-to-all-start.2 = ((bf16[8,128,256]{2,1,0:T(8,128)(2,1)}), bf16[8,128,256]{2,1,0:T(8,128)(2,1)S(1)}, u32[]{:S(2)}, u32[]{:S(2)}) async-start(bf16[8,128,256]{2,1,0:T(8,128)(2,1)} %spread.1), calls=%async_computation.2 | async-start | bytes 1048576 | tf_op jit(solution)/shard_map/all_to_all | solution.py:501
  17.0 14.6 %project.2 = bf16[4,1024,256]{2,1,0:T(8,128)(2,1)} custom-call(bf16[1024,4096]{1,0:T(8,128)(2,1)} %x_ref.3, bf16[4096,1024]{1,0:T(8,128)(2,1)} %w_ref.4), custom_call_target="tpu_custom_call" | custom-call | flops 14000000000 | tf_op jit(solution)/shard_map/project/pallas_call | solution.py:55
  31.5 0.8 copy-done.2
  32.3 4.2 %all-to-all-start = ((bf16[4,1024,256]{2,1,0:T(8,128)(2,1)}), bf16[4,1024,256]{2,1,0:T(8,128)(2,1)S(1)}, u32[]{:S(2)}, u32[]{:S(2)}) async-start(bf16[4,1024,256]{2,1,0:T(8,128)(2,1)} %project.2), calls=%async_computation | async-start | bytes 4194304 | tf_op jit(solution)/shard_map/all_to_all | solution.py:496
  36.5 14.2 %project.3 = bf16[4,1024,256]{2,1,0:T(8,128)(2,1)} custom-call(bf16[1024,4096]{1,0:T(8,128)(2,1)} %x_ref.3, bf16[4096,1024]{1,0:T(8,128)(2,1)} %w_ref.5), custom_call_target="tpu_custom_call" | custom-call | flops 14000000000 | tf_op jit(solution)/shard_map/project/pallas_call | solution.py:55
  50.7 2.3 route.1
  53.0 6.8 %context_grad.1 = bf16[2,4,128,256]{3,2,1,0:T(8,128)(2,1)} custom-call(bf16[128,4096]{1,0:T(8,128)(2,1)} %all-gather.2.cloned.1.call-done.x_ref, bf16[1024,4096]{1,0:T(8,128)(2,1)} %w_ref.7), custom_call_target="tpu_custom_call" | custom-call | flops 5000000000 | tf_op jit(solution)/shard_map/context_grad/pallas_call | solution.py:368
  59.8 1.1 all-to-all-done
  60.8 1.3 copy-done.1
  62.1 4.5 %all-to-all-start.1 = ((bf16[4,1024,256]{2,1,0:T(8,128)(2,1)}), bf16[4,1024,256]{2,1,0:T(8,128)(2,1)}, u32[]{:S(2)}, u32[]{:S(2)}) async-start(bf16[4,1024,256]{2,1,0:T(8,128)(2,1)} %project.3), calls=%async_computation.1 | async-start | bytes 4194304 | tf_op jit(solution)/shard_map/all_to_all | solution.py:496
  66.6 13.6 %stats.1.refs_0_ = f32[2,8,2,256]{3,2,1,0:T(2,128)} custom-call(s32[8,24]{1,0:T(8,128)} %get-tuple-element.30.pick_ref, s32[8]{0:T(128)} %get-tuple-element.31.live_ref, bf16[16,256,256]{2,1,0:T(8,128)(2,1)} %bitcast.5, bf16[8,128,256]{2,1,0:T(8,128)(2,1)} %copy-done.2), custom_call_target="tpu_custom_call" | custom-call | flops 12999999488 | tf_op jit(solution)/shard_map/stats/pallas_call | solution.py:438
  80.2 2.6 %collective-permute-start = (f32[2,8,2,256]{3,2,1,0:T(2,128)}, f32[2,8,2,256]{3,2,1,0:T(2,128)S(1)}, u32[]{:S(2)}, u32[]{:S(2)}) collective-permute-start(f32[2,8,2,256]{3,2,1,0:T(2,128)} %stats.1.refs_0_), channel_id=1, source_target_pairs={{0,16},{4,20},{8,24},{12,28},{16,0},{20,4},{24,8},{28,12},{1,17},{... | collective-permute-start | bytes 98312 | tf_op jit(solution)/shard_map/ppermute | solution.py:504
  82.8 6.7 %collective-permute-done.refs_1_ = f32[2,8,2,256]{3,2,1,0:T(2,128)S(1)} collective-permute-done((f32[2,8,2,256]{3,2,1,0:T(2,128)}, f32[2,8,2,256]{3,2,1,0:T(2,128)S(1)}, u32[]{:S(2)}, u32[]{:S(2)}) %collective-permute-start) | collective-permute-done | bytes 32800 | tf_op jit(solution)/shard_map/ppermute | solution.py:504
  89.5 0.6 copy-done.7
  90.1 1.4 merge.1.st_ref.refs_2_
  91.5 0.8 all-to-all-done.1
  92.4 6.0 %all-to-all-start.3 = ((bf16[8,128,256]{2,1,0:T(8,128)(2,1)}), bf16[8,128,256]{2,1,0:T(8,128)(2,1)S(1)}, u32[]{:S(2)}, u32[]{:S(2)}) async-start(bf16[8,128,256]{2,1,0:T(8,128)(2,1)} %bitcast.2), calls=%async_computation.3 | async-start | bytes 1048576 | tf_op jit(solution)/shard_map/all_to_all | solution.py:501
  98.4 11.2 %context.2 = f32[4,256,128]{2,1,0:T(8,128)} custom-call(s32[8,24]{1,0:T(8,128)} %get-tuple-element.30.pick_ref, s32[8]{0:T(128)} %get-tuple-element.31.live_ref, s32[1]{0:T(128)} %bitcast.outer_ref, bf16[16,256,256]{2,1,0:T(8,128)(2,1)} %bitcast.6, bf16[16,256,256]{2,1,0:T(8,128)(2,1)} %bitcast.3.v_ref, bf16[8,128,256]{2,1,0:T(8,128)(2,1)} %copy-done.2, ...), custom_call_target="tpu_custom_call" | custom-call | flops 14000000000 | tf_op jit(solution)/shard_map/context/pallas_call | solution.py:438
  109.6 1.8 all-to-all-done.3.g_ref.refs_3_
  111.4 1.2 collective-permute-start.1
  112.6 11.2 %context.3.refs_0_ = f32[4,256,128]{2,1,0:T(8,128)} custom-call(s32[8,24]{1,0:T(8,128)} %get-tuple-element.30.pick_ref, s32[8]{0:T(128)} %get-tuple-element.31.live_ref, s32[1]{0:T(128)} %bitcast.outer_ref, bf16[16,256,256]{2,1,0:T(8,128)(2,1)} %bitcast.7, bf16[16,256,256]{2,1,0:T(8,128)(2,1)} %bitcast.3.v_ref, bf16[8,128,256]{2,1,0:T(8,128)(2,1)} %copy-done.2, ...), custom_call_target="tpu_custom_call" | custom-call | flops 5000000000 | tf_op jit(solution)/shard_map/context/pallas_call | solution.py:438
  123.8 15.2 %value_grad.1.refs_4_ = bf16[4,1152,256]{2,1,0:T(8,128)(2,1)} custom-call(s32[8,24]{1,0:T(8,128)} %get-tuple-element.30.pick_ref, s32[8]{0:T(128)} %get-tuple-element.31.live_ref, bf16[16,256,256]{2,1,0:T(8,128)(2,1)} %bitcast.8, bf16[8,128,256]{2,1,0:T(8,128)(2,1)} %copy-done.2, bf16[8,128,256]{2,1,0:T(8,128)(2,1)} %copy-done.3, ...), custom_call_target="tpu_custom_call" | custom-call | flops 5000000000 | tf_op jit(solution)/shard_map/value_grad/pallas_call | solution.py:438
  139.0 0.8 copy-done.6
  139.8 2.9 %combine_context.1 = (bf16[4,1152,256]{2,1,0:T(8,128)(2,1)}, f32[4,2,256]{2,1,0:T(2,128)}) custom-call(s32[1]{0:T(128)} %bitcast.outer_ref, f32[4,256,128]{2,1,0:T(8,128)} %context.3.refs_0_, f32[4,256,128]{2,1,0:T(8,128)} %copy-done.6, f32[3,8,2,256]{3,2,1,0:T(2,128)} %merge.1.st_ref.refs_2_, ...), custom_call_target="tpu_custom_call", output_to_operand_aliasing={{0}: (5, {})} | custom-call | flops 3000000000 | tf_op jit(solution)/shard_map/combine_context/pallas_call | solution.py:574
  142.7 1.8 collective-permute-start.2
  144.6 3.0 %collective-permute-done.2.rest_1_ = f32[4,2,256]{2,1,0:T(2,128)S(1)} collective-permute-done((f32[4,2,256]{2,1,0:T(2,128)}, f32[4,2,256]{2,1,0:T(2,128)S(1)}, u32[]{:S(2)}, u32[]{:S(2)}) %collective-permute-start.2) | collective-permute-done | bytes 8224 | tf_op jit(solution)/shard_map/ppermute | solution.py:504
  147.6 0.6 copy-done.8
  148.1 3.8 %all-to-all-start.4 = ((bf16[4,1152,256]{2,1,0:T(8,128)(2,1)}), bf16[4,1152,256]{2,1,0:T(8,128)(2,1)S(1)}, u32[]{:S(2)}, u32[]{:S(2)}) async-start(bf16[4,1152,256]{2,1,0:T(8,128)(2,1)} %get-tuple-element.41), calls=%async_computation.4 | async-start | bytes 4718592 | tf_op jit(solution)/shard_map/all_to_all | solution.py:496
  152.0 23.4 %score_grad.1 = (bf16[16,256,256]{2,1,0:T(8,128)(2,1)}, f32[4,256,128]{2,1,0:T(8,128)}, f32[4,256,128]{2,1,0:T(8,128)}) custom-call(s32[8,24]{1,0:T(8,128)} %get-tuple-element.30.pick_ref, s32[8]{0:T(128)} %get-tuple-element.31.live_ref, s32[1]{0:T(128)} %bitcast.outer_ref, bf16[16,256,256]{2,1,0:T(8,128)(2,1)} %bitcast.9, ...), custom_call_target="tpu_custom_call" | custom-call | flops 24999999488 | tf_op jit(solution)/shard_map/score_grad/pallas_call | solution.py:438
  175.4 1.7 collective-permute-start.3
  177.1 1.0 all-to-all-done.4.x_ref
  178.2 1.4 copy-done
  179.6 4.5 %all-to-all-start.5 = ((bf16[4,1024,256]{2,1,0:T(8,128)(2,1)}), bf16[4,1024,256]{2,1,0:T(8,128)(2,1)}, u32[]{:S(2)}, u32[]{:S(2)}) async-start(bf16[4,1024,256]{2,1,0:T(8,128)(2,1)} %bitcast.10), calls=%async_computation.6 | async-start | bytes 4194304 | tf_op jit(solution)/shard_map/all_to_all | solution.py:496
  184.0 0.0 reduce-scatter.2.cloned.1.call-start
  184.1 6.7 %out_project.1 = f32[128,4096]{1,0:T(8,128)} custom-call(bf16[4,1152,256]{2,1,0:T(8,128)(2,1)} %copy-done, bf16[1024,4096]{1,0:T(8,128)(2,1)} %w_ref.7), custom_call_target="tpu_custom_call" | custom-call | flops 1000000000 | tf_op jit(solution)/shard_map/out_project/pallas_call | solution.py:399
  190.8 2.7 %collect.3 = bf16[1024,1024]{1,0:T(8,128)(2,1)} custom-call(bf16[4,1152,256]{2,1,0:T(8,128)(2,1)} %copy-done), custom_call_target="tpu_custom_call" | custom-call | flops 1000000000 | tf_op jit(solution)/shard_map/collect/pallas_call | solution.py:423
  193.5 5.0 %collective-permute-done.3.refs_1_ = f32[4,256,128]{2,1,0:T(8,128)S(1)} collective-permute-done((f32[4,256,128]{2,1,0:T(8,128)}, f32[4,256,128]{2,1,0:T(8,128)S(1)}, u32[]{:S(2)}, u32[]{:S(2)}) %collective-permute-start.3) | collective-permute-done | bytes 524320 | tf_op jit(solution)/shard_map/ppermute | solution.py:504
  198.5 0.8 copy-done.5
  199.3 2.1 combine_query.1
  201.4 16.4 %all-to-all-done.5.x_ref = bf16[4,1024,256]{2,1,0:T(8,128)(2,1)} async-done(((bf16[4,1024,256]{2,1,0:T(8,128)(2,1)}), bf16[4,1024,256]{2,1,0:T(8,128)(2,1)}, u32[]{:S(2)}, u32[]{:S(2)}) %all-to-all-start.5) | async-done | bytes 2097184 | tf_op jit(solution)/shard_map/all_to_all | solution.py:496
  217.8 3.4 %all-to-all-start.6 = ((bf16[4,128,256]{2,1,0:T(8,128)(2,1)}), bf16[4,128,256]{2,1,0:T(8,128)(2,1)S(1)}, u32[]{:S(2)}, u32[]{:S(2)}) async-start(bf16[4,128,256]{2,1,0:T(8,128)(2,1)} %combine_query.1), calls=%async_computation.7 | async-start | bytes 524288 | tf_op jit(solution)/shard_map/all_to_all | solution.py:496
  221.3 2.7 %collect.5 = bf16[1024,1024]{1,0:T(8,128)(2,1)} custom-call(bf16[4,1024,256]{2,1,0:T(8,128)(2,1)} %all-to-all-done.5.x_ref), custom_call_target="tpu_custom_call" | custom-call | flops 1000000000 | tf_op jit(solution)/shard_map/collect/pallas_call | solution.py:423
  224.0 2.6 %all-to-all-done.6.x_ref = bf16[4,128,256]{2,1,0:T(8,128)(2,1)S(1)} async-done(((bf16[4,128,256]{2,1,0:T(8,128)(2,1)}), bf16[4,128,256]{2,1,0:T(8,128)(2,1)S(1)}, u32[]{:S(2)}, u32[]{:S(2)}) %all-to-all-start.6) | async-done | bytes 262176 | tf_op jit(solution)/shard_map/all_to_all | solution.py:496
  226.6 0.7 copy-done.4
  227.3 1.7 collect.4
  229.0 1.8 convert_element_type.3
  (16 shorter events, 0.1 us)
Async XLA Ops:
  7.2 29.3 %all-gather.2.cloned.1.call-start = ((), (), s32[]{:S(2)}) async-start(), calls=%async_computation.8 | async-start | bytes 1310720 | tf_op jit(solution)/shard_map/all_gather | solution.py:515
  9.7 21.8 %all-to-all-start.2 = ((bf16[8,128,256]{2,1,0:T(8,128)(2,1)}), bf16[8,128,256]{2,1,0:T(8,128)(2,1)S(1)}, u32[]{:S(2)}, u32[]{:S(2)}) async-start(bf16[8,128,256]{2,1,0:T(8,128)(2,1)} %spread.1), calls=%async_computation.2 | async-start | bytes 1048576 | tf_op jit(solution)/shard_map/all_to_all | solution.py:501
  31.5 0.8 copy-start.2
  32.3 28.5 %all-to-all-start = ((bf16[4,1024,256]{2,1,0:T(8,128)(2,1)}), bf16[4,1024,256]{2,1,0:T(8,128)(2,1)S(1)}, u32[]{:S(2)}, u32[]{:S(2)}) async-start(bf16[4,1024,256]{2,1,0:T(8,128)(2,1)} %project.2), calls=%async_computation | async-start | bytes 4194304 | tf_op jit(solution)/shard_map/all_to_all | solution.py:496
  60.8 1.3 copy-start.1
  62.1 30.3 %all-to-all-start.1 = ((bf16[4,1024,256]{2,1,0:T(8,128)(2,1)}), bf16[4,1024,256]{2,1,0:T(8,128)(2,1)}, u32[]{:S(2)}, u32[]{:S(2)}) async-start(bf16[4,1024,256]{2,1,0:T(8,128)(2,1)} %project.3), calls=%async_computation.1 | async-start | bytes 4194304 | tf_op jit(solution)/shard_map/all_to_all | solution.py:496
  80.2 9.3 %collective-permute-start = (f32[2,8,2,256]{3,2,1,0:T(2,128)}, f32[2,8,2,256]{3,2,1,0:T(2,128)S(1)}, u32[]{:S(2)}, u32[]{:S(2)}) collective-permute-start(f32[2,8,2,256]{3,2,1,0:T(2,128)} %stats.1.refs_0_), channel_id=1, source_target_pairs={{0,16},{4,20},{8,24},{12,28},{16,0},{20,4},{24,8},{28,12},{1,17},{... | collective-permute-start | bytes 98312 | tf_op jit(solution)/shard_map/ppermute | solution.py:504
  89.5 0.6 copy-start.7
  92.4 19.0 %all-to-all-start.3 = ((bf16[8,128,256]{2,1,0:T(8,128)(2,1)}), bf16[8,128,256]{2,1,0:T(8,128)(2,1)S(1)}, u32[]{:S(2)}, u32[]{:S(2)}) async-start(bf16[8,128,256]{2,1,0:T(8,128)(2,1)} %bitcast.2), calls=%async_computation.3 | async-start | bytes 1048576 | tf_op jit(solution)/shard_map/all_to_all | solution.py:501
  111.4 12.4 %copy-start.3 = (bf16[8,128,256]{2,1,0:T(8,128)(2,1)}, bf16[8,128,256]{2,1,0:T(8,128)(2,1)S(1)}, u32[]{:S(2)}) copy-start(bf16[8,128,256]{2,1,0:T(8,128)(2,1)S(1)} %all-to-all-done.3.g_ref.refs_3_) | copy-start | bytes 1572868
  111.4 27.6 %collective-permute-start.1 = (f32[4,256,128]{2,1,0:T(8,128)}, f32[4,256,128]{2,1,0:T(8,128)S(1)}, u32[]{:S(2)}, u32[]{:S(2)}) collective-permute-start(f32[4,256,128]{2,1,0:T(8,128)} %context.2), channel_id=1, source_target_pairs={{0,16},{4,20},{8,24},{12,28},{16,0},{20,4},{24,8},{28,12},{1,17},{... | collective-permute-start | bytes 1572872 | tf_op jit(solution)/shard_map/ppermute | solution.py:504
  139.0 0.8 copy-start.6
  142.7 4.8 %collective-permute-start.2 = (f32[4,2,256]{2,1,0:T(2,128)}, f32[4,2,256]{2,1,0:T(2,128)S(1)}, u32[]{:S(2)}, u32[]{:S(2)}) collective-permute-start(f32[4,2,256]{2,1,0:T(2,128)} %get-tuple-element.40.rest_0_), channel_id=1, source_target_pairs={{0,16},{4,20},{8,24},{12,28},{16,0},{20,4},{24,8},{28,12},{1,17},{... | collective-permute-start | bytes 24584 | tf_op jit(solution)/shard_map/ppermute | solution.py:504
  147.6 0.6 copy-start.8
  148.1 30.0 %all-to-all-start.4 = ((bf16[4,1152,256]{2,1,0:T(8,128)(2,1)}), bf16[4,1152,256]{2,1,0:T(8,128)(2,1)S(1)}, u32[]{:S(2)}, u32[]{:S(2)}) async-start(bf16[4,1152,256]{2,1,0:T(8,128)(2,1)} %get-tuple-element.41), calls=%async_computation.4 | async-start | bytes 4718592 | tf_op jit(solution)/shard_map/all_to_all | solution.py:496
  175.4 23.2 %collective-permute-start.3 = (f32[4,256,128]{2,1,0:T(8,128)}, f32[4,256,128]{2,1,0:T(8,128)S(1)}, u32[]{:S(2)}, u32[]{:S(2)}) collective-permute-start(f32[4,256,128]{2,1,0:T(8,128)} %get-tuple-element.47), channel_id=1, source_target_pairs={{0,16},{4,20},{8,24},{12,28},{16,0},{20,4},{24,8},{28,12},{1,17},{... | collective-permute-start | bytes 1572872 | tf_op jit(solution)/shard_map/ppermute | solution.py:504
  178.2 1.4 copy-start
  179.6 38.3 %all-to-all-start.5 = ((bf16[4,1024,256]{2,1,0:T(8,128)(2,1)}), bf16[4,1024,256]{2,1,0:T(8,128)(2,1)}, u32[]{:S(2)}, u32[]{:S(2)}) async-start(bf16[4,1024,256]{2,1,0:T(8,128)(2,1)} %bitcast.10), calls=%async_computation.6 | async-start | bytes 4194304 | tf_op jit(solution)/shard_map/all_to_all | solution.py:496
  184.0 44.9 %reduce-scatter.2.cloned.1.call-start = ((), (), s32[]{:S(2)}) async-start(), calls=%async_computation.9 | async-start | bytes 2621440 | tf_op jit(solution)/shard_map/reduce_scatter | solution.py:601
  198.5 0.8 copy-start.5
  217.8 8.8 %all-to-all-start.6 = ((bf16[4,128,256]{2,1,0:T(8,128)(2,1)}), bf16[4,128,256]{2,1,0:T(8,128)(2,1)S(1)}, u32[]{:S(2)}, u32[]{:S(2)}) async-start(bf16[4,128,256]{2,1,0:T(8,128)(2,1)} %combine_query.1), calls=%async_computation.7 | async-start | bytes 524288 | tf_op jit(solution)/shard_map/all_to_all | solution.py:496
  226.6 0.7 copy-start.4
Sparse Core Ops, SparseCore 0:
  9.6 19.4 all-gather.1
  191.0 30.9 reduce-scatter.1

commit v7 on v6

--- a/solution.py
+++ b/solution.py
@@ -340,13 +340,22 @@
     copy.wait()
 
 
-def combine_query_kernel(n_parts, *refs):
-    parts, o_ref = refs[:n_parts], refs[n_parts]
-    for q in range(o_ref.shape[0]):
+def combine_query_kernel(n_parts, place_ref, *refs):
+    parts, o_refs = refs[:n_parts], refs[n_parts:]
+    for r, o_ref in enumerate(o_refs):
+        q = lax.rem(place_ref[0] + r, len(o_refs))
         mix = parts[0][q]
         for part in parts[1:]:
             mix = mix + part[q]
-        o_ref[q] = jnp.transpose(mix * SCALE).astype(BF16)
+        o_ref[...] = jnp.transpose(mix * SCALE).astype(BF16)
+
+
+def gather_query_kernel(place_ref, *refs):
+    blocks, o_ref = refs[:-1], refs[-1]
+    width = blocks[0].shape[1]
+    for r, block in enumerate(blocks):
+        source = lax.rem(place_ref[0] + len(blocks) - r, len(blocks))
+        o_ref[:, pl.ds(pl.multiple_of(source * width, LANES), width)] = block[...]
 
 
 def spread_kernel(x_ref, o_ref):
@@ -600,16 +609,27 @@
     value_grad = collect(after(packed_back, projected), tok_local)
     output = lax.psum_scatter(projected, "head", scatter_dimension=1, tiled=True).astype(BF16)
     key_back = swap(after(done[0], packed_back).reshape(inner, tok_local, width))
-    query_done = vmem_call(
+    place = (lax.axis_index("pas") % inner).astype(jnp.int32).reshape(1)
+    query_blocks = vmem_call(
         functools.partial(combine_query_kernel, n_outer),
-        (),
+        (place,),
         [after(done[1], value_grad)] + partials(done[1:])[1:],
-        sds((inner, rows, width), BF16),
+        (sds((rows, width), BF16),) * inner,
         [],
         40,
         "combine_query",
     )
-    query_grad = collect(swap(after(query_done, key_back)), rows)
+    arrived = [query_blocks[0]] + [
+        lax.ppermute(
+            query_blocks[r],
+            "pas",
+            [(o * inner + i, o * inner + (i + r) % inner) for o in range(n_outer) for i in range(inner)],
+        )
+        for r in range(1, inner)
+    ]
+    query_grad = vmem_call(
+        gather_query_kernel, (place,), arrived, sds((rows, head_width), BF16), [], 30, "gather_query"
+    )
     key_grad = collect(key_back, tok_local)
     return (output, query_grad, key_grad, value_grad)
 

time: 239 us -> 235 us (0.983)
  waiting for transfers between devices: 39.2 us -> 35.6 us
    all_to_all x5 -> x4, waiting for transfers between devices: 22 us -> 2.88 us  [swap(): lax.all_to_all(x, 'pas', split_axis=0, concat_axis=0, tiled=True, axis_in...]
    ppermute x0 -> x3, waiting for transfers between devices: none -> 15.4 us  [body(): lax.ppermute(query_blocks[r], 'pas', [(o * inner + i, o * inner + (i + r)...]
    all_to_all x5 -> x4, starting transfers between devices: 20.3 us -> 16.9 us  [swap(): lax.all_to_all(x, 'pas', split_axis=0, concat_axis=0, tiled=True, axis_in...]
    ppermute x0 -> x3, starting transfers between devices: none -> 3.22 us  [body(): lax.ppermute(query_blocks[r], 'pas', [(o * inner + i, o * inner + (i + r)...]
    pallas_call x3 -> x2, Pallas kernels: 7.09 us -> 5.38 us  [collect(): pl.pallas_call(collect_kernel, grid=(rows // tile,), in_specs=[pl.BlockSp...]
    pallas_call x8 -> x9, Pallas kernels: 80 us -> 81.6 us  [vmem_call(): pl.pallas_call(kernel, in_specs=[smem] * len(scalars) + [vmem] * len(arra...]
    unnamed x18 -> x22, local copies, waits for them, and re-layouts: 7.05 us -> 6.95 us
  transfers between devices with their start and end apart: 13 -> 15, of which waited for: 9 -> 8; matrix products, arithmetic and copies ran while one was open for 0% -> 0% of each run, Pallas kernels for 55% -> 56%
where the time goes in v7:
time: 235 us; the launch traced here: 234 us
  Pallas kernels  134 us (57%)
  starting transfers between devices  40.8 us (17%)
  waiting for transfers between devices  35.6 us (15%)
  between operations  14.1 us (6%)
  local copies, waits for them, and re-layouts  6.95 us (3%)
    pallas_call x9, Pallas kernels, vmem_call(): pl.pallas_call(kernel, in_specs=[smem] * len(scalars) + [vmem] * len(arra...  81.6 us
    pallas_call x2, Pallas kernels, project(): pl.pallas_call(project_kernel, grid=(rows // tile,), in_specs=[pl.BlockSp...  28.7 us
    all_to_all x4, starting transfers between devices, swap(): lax.all_to_all(x, 'pas', split_axis=0, concat_axis=0, tiled=True, axis_in...  16.9 us
    ppermute x3, waiting for transfers between devices, body(): lax.ppermute(query_blocks[r], 'pas', [(o * inner + i, o * inner + (i + r)...  15.4 us
    ppermute x4, waiting for transfers between devices, to_outer(): lax.ppermute(x, 'pas', [(o * inner + i, (o + r) % n_outer * inner + i) fo...  14.7 us
    all_to_all x2, starting transfers between devices, swap_all(): return lax.all_to_all(x, 'pas', split_axis=0, concat_axis=0, tiled=True)  13.3 us
    ppermute x4, starting transfers between devices, to_outer(): lax.ppermute(x, 'pas', [(o * inner + i, (o + r) % n_outer * inner + i) fo...  7.33 us
    unnamed x22, local copies, waits for them, and re-layouts  6.95 us
  transfers between devices with their start and end apart: 15, of which 8 were waited for; matrix products, arithmetic and copies ran while one was open for 0% of the time, Pallas kernels for 56%

profile of v7, /device:TPU:0, one launch (start us, length us, event | category | flops | bytes accessed | tf_op | source)
XLA Modules:
  0.0 233.6 jit_solution(17865823345416568320)
XLA Ops:
  7.2 0.7 all-gather.2.cloned.1.call-update
  7.9 1.8 spread.1
  9.7 7.3 %all-to-all-start.2 = ((bf16[8,128,256]{2,1,0:T(8,128)(2,1)}), bf16[8,128,256]{2,1,0:T(8,128)(2,1)S(1)}, u32[]{:S(2)}, u32[]{:S(2)}) async-start(bf16[8,128,256]{2,1,0:T(8,128)(2,1)} %spread.1), calls=%async_computation.2 | async-start | bytes 1048576 | tf_op jit(solution)/shard_map/all_to_all | solution.py:510
  17.0 14.6 %project.2 = bf16[4,1024,256]{2,1,0:T(8,128)(2,1)} custom-call(bf16[1024,4096]{1,0:T(8,128)(2,1)} %x_ref.3, bf16[4096,1024]{1,0:T(8,128)(2,1)} %w_ref.4), custom_call_target="tpu_custom_call" | custom-call | flops 14000000000 | tf_op jit(solution)/shard_map/project/pallas_call | solution.py:55
  31.5 0.8 copy-done.2
  32.3 4.2 %all-to-all-start = ((bf16[4,1024,256]{2,1,0:T(8,128)(2,1)}), bf16[4,1024,256]{2,1,0:T(8,128)(2,1)S(1)}, u32[]{:S(2)}, u32[]{:S(2)}) async-start(bf16[4,1024,256]{2,1,0:T(8,128)(2,1)} %project.2), calls=%async_computation | async-start | bytes 4194304 | tf_op jit(solution)/shard_map/all_to_all | solution.py:505
  36.5 14.2 %project.3 = bf16[4,1024,256]{2,1,0:T(8,128)(2,1)} custom-call(bf16[1024,4096]{1,0:T(8,128)(2,1)} %x_ref.3, bf16[4096,1024]{1,0:T(8,128)(2,1)} %w_ref.5), custom_call_target="tpu_custom_call" | custom-call | flops 14000000000 | tf_op jit(solution)/shard_map/project/pallas_call | solution.py:55
  50.7 2.3 route.1
  52.9 6.8 %context_grad.1 = bf16[2,4,128,256]{3,2,1,0:T(8,128)(2,1)} custom-call(bf16[128,4096]{1,0:T(8,128)(2,1)} %all-gather.2.cloned.1.call-done.x_ref, bf16[1024,4096]{1,0:T(8,128)(2,1)} %w_ref.7), custom_call_target="tpu_custom_call" | custom-call | flops 5000000000 | tf_op jit(solution)/shard_map/context_grad/pallas_call | solution.py:377
  59.7 1.1 all-to-all-done
  60.8 1.3 copy-done.1
  62.1 4.4 %all-to-all-start.1 = ((bf16[4,1024,256]{2,1,0:T(8,128)(2,1)}), bf16[4,1024,256]{2,1,0:T(8,128)(2,1)}, u32[]{:S(2)}, u32[]{:S(2)}) async-start(bf16[4,1024,256]{2,1,0:T(8,128)(2,1)} %project.3), calls=%async_computation.1 | async-start | bytes 4194304 | tf_op jit(solution)/shard_map/all_to_all | solution.py:505
  66.6 13.6 %stats.1.refs_0_ = f32[2,8,2,256]{3,2,1,0:T(2,128)} custom-call(s32[8,24]{1,0:T(8,128)} %get-tuple-element.33.pick_ref, s32[8]{0:T(128)} %get-tuple-element.34.live_ref, bf16[16,256,256]{2,1,0:T(8,128)(2,1)} %bitcast.6, bf16[8,128,256]{2,1,0:T(8,128)(2,1)} %copy-done.2), custom_call_target="tpu_custom_call" | custom-call | flops 12999999488 | tf_op jit(solution)/shard_map/stats/pallas_call | solution.py:447
  80.2 2.6 %collective-permute-start = (f32[2,8,2,256]{3,2,1,0:T(2,128)}, f32[2,8,2,256]{3,2,1,0:T(2,128)S(1)}, u32[]{:S(2)}, u32[]{:S(2)}) collective-permute-start(f32[2,8,2,256]{3,2,1,0:T(2,128)} %stats.1.refs_0_), channel_id=1, source_target_pairs={{0,16},{4,20},{8,24},{12,28},{16,0},{20,4},{24,8},{28,12},{1,17},{... | collective-permute-start | bytes 98312 | tf_op jit(solution)/shard_map/ppermute | solution.py:513
  82.8 6.7 %collective-permute-done.refs_1_ = f32[2,8,2,256]{3,2,1,0:T(2,128)S(1)} collective-permute-done((f32[2,8,2,256]{3,2,1,0:T(2,128)}, f32[2,8,2,256]{3,2,1,0:T(2,128)S(1)}, u32[]{:S(2)}, u32[]{:S(2)}) %collective-permute-start) | collective-permute-done | bytes 32800 | tf_op jit(solution)/shard_map/ppermute | solution.py:513
  89.5 0.6 copy-done.9
  90.1 1.4 merge.1.st_ref.refs_2_
  91.5 0.8 all-to-all-done.1
  92.3 6.0 %all-to-all-start.3 = ((bf16[8,128,256]{2,1,0:T(8,128)(2,1)}), bf16[8,128,256]{2,1,0:T(8,128)(2,1)S(1)}, u32[]{:S(2)}, u32[]{:S(2)}) async-start(bf16[8,128,256]{2,1,0:T(8,128)(2,1)} %bitcast.2), calls=%async_computation.3 | async-start | bytes 1048576 | tf_op jit(solution)/shard_map/all_to_all | solution.py:510
  98.3 11.2 %context.2 = f32[4,256,128]{2,1,0:T(8,128)} custom-call(s32[8,24]{1,0:T(8,128)} %get-tuple-element.33.pick_ref, s32[8]{0:T(128)} %get-tuple-element.34.live_ref, s32[1]{0:T(128)} %bitcast.outer_ref, bf16[16,256,256]{2,1,0:T(8,128)(2,1)} %bitcast.7, bf16[16,256,256]{2,1,0:T(8,128)(2,1)} %bitcast.3.v_ref, bf16[8,128,256]{2,1,0:T(8,128)(2,1)} %copy-done.2, ...), custom_call_target="tpu_custom_call" | custom-call | flops 14000000000 | tf_op jit(solution)/shard_map/context/pallas_call | solution.py:447
  109.5 1.8 all-to-all-done.3.g_ref.refs_3_
  111.3 1.2 collective-permute-start.1
  112.5 11.2 %context.3.refs_0_ = f32[4,256,128]{2,1,0:T(8,128)} custom-call(s32[8,24]{1,0:T(8,128)} %get-tuple-element.33.pick_ref, s32[8]{0:T(128)} %get-tuple-element.34.live_ref, s32[1]{0:T(128)} %bitcast.outer_ref, bf16[16,256,256]{2,1,0:T(8,128)(2,1)} %bitcast.8, bf16[16,256,256]{2,1,0:T(8,128)(2,1)} %bitcast.3.v_ref, bf16[8,128,256]{2,1,0:T(8,128)(2,1)} %copy-done.2, ...), custom_call_target="tpu_custom_call" | custom-call | flops 5000000000 | tf_op jit(solution)/shard_map/context/pallas_call | solution.py:447
  123.7 15.2 %value_grad.1.refs_4_ = bf16[4,1152,256]{2,1,0:T(8,128)(2,1)} custom-call(s32[8,24]{1,0:T(8,128)} %get-tuple-element.33.pick_ref, s32[8]{0:T(128)} %get-tuple-element.34.live_ref, bf16[16,256,256]{2,1,0:T(8,128)(2,1)} %bitcast.9, bf16[8,128,256]{2,1,0:T(8,128)(2,1)} %copy-done.2, bf16[8,128,256]{2,1,0:T(8,128)(2,1)} %copy-done.3, ...), custom_call_target="tpu_custom_call" | custom-call | flops 5000000000 | tf_op jit(solution)/shard_map/value_grad/pallas_call | solution.py:447
  139.0 0.8 copy-done.5
  139.8 2.9 %combine_context.1 = (bf16[4,1152,256]{2,1,0:T(8,128)(2,1)}, f32[4,2,256]{2,1,0:T(2,128)}) custom-call(s32[1]{0:T(128)} %bitcast.outer_ref, f32[4,256,128]{2,1,0:T(8,128)} %context.3.refs_0_, f32[4,256,128]{2,1,0:T(8,128)} %copy-done.5, f32[3,8,2,256]{3,2,1,0:T(2,128)} %merge.1.st_ref.refs_2_, ...), custom_call_target="tpu_custom_call", output_to_operand_aliasing={{0}: (5, {})} | custom-call | flops 3000000000 | tf_op jit(solution)/shard_map/combine_context/pallas_call | solution.py:583
  142.7 1.8 collective-permute-start.2
  144.5 3.0 %collective-permute-done.2.rest_1_ = f32[4,2,256]{2,1,0:T(2,128)S(1)} collective-permute-done((f32[4,2,256]{2,1,0:T(2,128)}, f32[4,2,256]{2,1,0:T(2,128)S(1)}, u32[]{:S(2)}, u32[]{:S(2)}) %collective-permute-start.2) | collective-permute-done | bytes 8224 | tf_op jit(solution)/shard_map/ppermute | solution.py:513
  147.5 0.6 copy-done.10
  148.1 3.8 %all-to-all-start.4 = ((bf16[4,1152,256]{2,1,0:T(8,128)(2,1)}), bf16[4,1152,256]{2,1,0:T(8,128)(2,1)S(1)}, u32[]{:S(2)}, u32[]{:S(2)}) async-start(bf16[4,1152,256]{2,1,0:T(8,128)(2,1)} %get-tuple-element.44), calls=%async_computation.4 | async-start | bytes 4718592 | tf_op jit(solution)/shard_map/all_to_all | solution.py:505
  151.9 23.5 %score_grad.1 = (bf16[16,256,256]{2,1,0:T(8,128)(2,1)}, f32[4,256,128]{2,1,0:T(8,128)}, f32[4,256,128]{2,1,0:T(8,128)}) custom-call(s32[8,24]{1,0:T(8,128)} %get-tuple-element.33.pick_ref, s32[8]{0:T(128)} %get-tuple-element.34.live_ref, s32[1]{0:T(128)} %bitcast.outer_ref, bf16[16,256,256]{2,1,0:T(8,128)(2,1)} %bitcast.10, ...), custom_call_target="tpu_custom_call" | custom-call | flops 24999999488 | tf_op jit(solution)/shard_map/score_grad/pallas_call | solution.py:447
  175.4 1.7 collective-permute-start.3
  177.1 1.0 all-to-all-done.4.x_ref
  178.1 1.4 copy-done
  179.5 4.4 %all-to-all-start.5 = ((bf16[4,1024,256]{2,1,0:T(8,128)(2,1)}), bf16[4,1024,256]{2,1,0:T(8,128)(2,1)}, u32[]{:S(2)}, u32[]{:S(2)}) async-start(bf16[4,1024,256]{2,1,0:T(8,128)(2,1)} %bitcast.11), calls=%async_computation.6 | async-start | bytes 4194304 | tf_op jit(solution)/shard_map/all_to_all | solution.py:505
  184.0 0.0 reduce-scatter.2.cloned.1.call-start
  184.0 6.7 %out_project.1 = f32[128,4096]{1,0:T(8,128)} custom-call(bf16[4,1152,256]{2,1,0:T(8,128)(2,1)} %copy-done, bf16[1024,4096]{1,0:T(8,128)(2,1)} %w_ref.7), custom_call_target="tpu_custom_call" | custom-call | flops 1000000000 | tf_op jit(solution)/shard_map/out_project/pallas_call | solution.py:408
  190.8 2.7 %collect.2 = bf16[1024,1024]{1,0:T(8,128)(2,1)} custom-call(bf16[4,1152,256]{2,1,0:T(8,128)(2,1)} %copy-done), custom_call_target="tpu_custom_call" | custom-call | flops 1000000000 | tf_op jit(solution)/shard_map/collect/pallas_call | solution.py:432
  193.5 5.0 %collective-permute-done.3.refs_1_ = f32[4,256,128]{2,1,0:T(8,128)S(1)} collective-permute-done((f32[4,256,128]{2,1,0:T(8,128)}, f32[4,256,128]{2,1,0:T(8,128)S(1)}, u32[]{:S(2)}, u32[]{:S(2)}) %collective-permute-start.3) | collective-permute-done | bytes 524320 | tf_op jit(solution)/shard_map/ppermute | solution.py:513
  198.5 0.8 copy-done.4
  199.3 2.0 combine_query.1
  201.3 1.8 collective-permute-start.4
  203.1 1.5 collective-permute-start.6
  204.6 15.4 %collective-permute-done.4.refs_1_ = bf16[128,256]{1,0:T(8,128)(2,1)S(1)} collective-permute-done((bf16[128,256]{1,0:T(8,128)(2,1)}, bf16[128,256]{1,0:T(8,128)(2,1)S(1)}, u32[]{:S(2)}, u32[]{:S(2)}) %collective-permute-start.4) | collective-permute-done | bytes 65568 | tf_op jit(solution)/shard_map/ppermute | solution.py:623
  220.0 0.6 copy-done.6
  220.6 1.7 gather_query.1
  222.3 2.7 %collect.3 = bf16[1024,1024]{1,0:T(8,128)(2,1)} custom-call(bf16[4,1024,256]{2,1,0:T(8,128)(2,1)} %all-to-all-done.5.x_ref), custom_call_target="tpu_custom_call" | custom-call | flops 1000000000 | tf_op jit(solution)/shard_map/collect/pallas_call | solution.py:432
  225.0 1.8 convert_element_type.3
  (24 shorter events, 0.1 us)
Async XLA Ops:
  7.2 29.3 %all-gather.2.cloned.1.call-start = ((), (), s32[]{:S(2)}) async-start(), calls=%async_computation.7 | async-start | bytes 1310720 | tf_op jit(solution)/shard_map/all_gather | solution.py:524
  9.7 21.8 %all-to-all-start.2 = ((bf16[8,128,256]{2,1,0:T(8,128)(2,1)}), bf16[8,128,256]{2,1,0:T(8,128)(2,1)S(1)}, u32[]{:S(2)}, u32[]{:S(2)}) async-start(bf16[8,128,256]{2,1,0:T(8,128)(2,1)} %spread.1), calls=%async_computation.2 | async-start | bytes 1048576 | tf_op jit(solution)/shard_map/all_to_all | solution.py:510
  31.5 0.8 copy-start.2
  32.3 28.5 %all-to-all-start = ((bf16[4,1024,256]{2,1,0:T(8,128)(2,1)}), bf16[4,1024,256]{2,1,0:T(8,128)(2,1)S(1)}, u32[]{:S(2)}, u32[]{:S(2)}) async-start(bf16[4,1024,256]{2,1,0:T(8,128)(2,1)} %project.2), calls=%async_computation | async-start | bytes 4194304 | tf_op jit(solution)/shard_map/all_to_all | solution.py:505
  60.8 1.3 copy-start.1
  62.1 30.2 %all-to-all-start.1 = ((bf16[4,1024,256]{2,1,0:T(8,128)(2,1)}), bf16[4,1024,256]{2,1,0:T(8,128)(2,1)}, u32[]{:S(2)}, u32[]{:S(2)}) async-start(bf16[4,1024,256]{2,1,0:T(8,128)(2,1)} %project.3), calls=%async_computation.1 | async-start | bytes 4194304 | tf_op jit(solution)/shard_map/all_to_all | solution.py:505
  80.2 9.3 %collective-permute-start = (f32[2,8,2,256]{3,2,1,0:T(2,128)}, f32[2,8,2,256]{3,2,1,0:T(2,128)S(1)}, u32[]{:S(2)}, u32[]{:S(2)}) collective-permute-start(f32[2,8,2,256]{3,2,1,0:T(2,128)} %stats.1.refs_0_), channel_id=1, source_target_pairs={{0,16},{4,20},{8,24},{12,28},{16,0},{20,4},{24,8},{28,12},{1,17},{... | collective-permute-start | bytes 98312 | tf_op jit(solution)/shard_map/ppermute | solution.py:513
  89.5 0.6 copy-start.9
  92.3 19.0 %all-to-all-start.3 = ((bf16[8,128,256]{2,1,0:T(8,128)(2,1)}), bf16[8,128,256]{2,1,0:T(8,128)(2,1)S(1)}, u32[]{:S(2)}, u32[]{:S(2)}) async-start(bf16[8,128,256]{2,1,0:T(8,128)(2,1)} %bitcast.2), calls=%async_computation.3 | async-start | bytes 1048576 | tf_op jit(solution)/shard_map/all_to_all | solution.py:510
  111.3 12.4 %copy-start.3 = (bf16[8,128,256]{2,1,0:T(8,128)(2,1)}, bf16[8,128,256]{2,1,0:T(8,128)(2,1)S(1)}, u32[]{:S(2)}) copy-start(bf16[8,128,256]{2,1,0:T(8,128)(2,1)S(1)} %all-to-all-done.3.g_ref.refs_3_) | copy-start | bytes 1572868
  111.3 27.6 %collective-permute-start.1 = (f32[4,256,128]{2,1,0:T(8,128)}, f32[4,256,128]{2,1,0:T(8,128)S(1)}, u32[]{:S(2)}, u32[]{:S(2)}) collective-permute-start(f32[4,256,128]{2,1,0:T(8,128)} %context.2), channel_id=1, source_target_pairs={{0,16},{4,20},{8,24},{12,28},{16,0},{20,4},{24,8},{28,12},{1,17},{... | collective-permute-start | bytes 1572872 | tf_op jit(solution)/shard_map/ppermute | solution.py:513
  139.0 0.8 copy-start.5
  142.7 4.8 %collective-permute-start.2 = (f32[4,2,256]{2,1,0:T(2,128)}, f32[4,2,256]{2,1,0:T(2,128)S(1)}, u32[]{:S(2)}, u32[]{:S(2)}) collective-permute-start(f32[4,2,256]{2,1,0:T(2,128)} %get-tuple-element.43.rest_0_), channel_id=1, source_target_pairs={{0,16},{4,20},{8,24},{12,28},{16,0},{20,4},{24,8},{28,12},{1,17},{... | collective-permute-start | bytes 24584 | tf_op jit(solution)/shard_map/ppermute | solution.py:513
  147.5 0.6 copy-start.10
  148.1 30.0 %all-to-all-start.4 = ((bf16[4,1152,256]{2,1,0:T(8,128)(2,1)}), bf16[4,1152,256]{2,1,0:T(8,128)(2,1)S(1)}, u32[]{:S(2)}, u32[]{:S(2)}) async-start(bf16[4,1152,256]{2,1,0:T(8,128)(2,1)} %get-tuple-element.44), calls=%async_computation.4 | async-start | bytes 4718592 | tf_op jit(solution)/shard_map/all_to_all | solution.py:505
  175.4 23.1 %collective-permute-start.3 = (f32[4,256,128]{2,1,0:T(8,128)}, f32[4,256,128]{2,1,0:T(8,128)S(1)}, u32[]{:S(2)}, u32[]{:S(2)}) collective-permute-start(f32[4,256,128]{2,1,0:T(8,128)} %get-tuple-element.50), channel_id=1, source_target_pairs={{0,16},{4,20},{8,24},{12,28},{16,0},{20,4},{24,8},{28,12},{1,17},{... | collective-permute-start | bytes 1572872 | tf_op jit(solution)/shard_map/ppermute | solution.py:513
  178.1 1.4 copy-start
  179.5 42.8 %all-to-all-start.5 = ((bf16[4,1024,256]{2,1,0:T(8,128)(2,1)}), bf16[4,1024,256]{2,1,0:T(8,128)(2,1)}, u32[]{:S(2)}, u32[]{:S(2)}) async-start(bf16[4,1024,256]{2,1,0:T(8,128)(2,1)} %bitcast.11), calls=%async_computation.6 | async-start | bytes 4194304 | tf_op jit(solution)/shard_map/all_to_all | solution.py:505
  184.0 41.0 %reduce-scatter.2.cloned.1.call-start = ((), (), s32[]{:S(2)}) async-start(), calls=%async_computation.8 | async-start | bytes 2621440 | tf_op jit(solution)/shard_map/reduce_scatter | solution.py:610
  198.5 0.8 copy-start.4
  201.3 18.6 %collective-permute-start.4 = (bf16[128,256]{1,0:T(8,128)(2,1)}, bf16[128,256]{1,0:T(8,128)(2,1)S(1)}, u32[]{:S(2)}, u32[]{:S(2)}) collective-permute-start(bf16[128,256]{1,0:T(8,128)(2,1)} %get-tuple-element.52), channel_id=1, source_target_pairs={{0,4},{4,8},{8,12},{12,0},{16,20},{20,24},{24,28},{28,16},{1,5},{5... | collective-permute-start | bytes 196616 | tf_op jit(solution)/shard_map/ppermute | solution.py:623
  203.1 16.9 %collective-permute-start.5 = (bf16[128,256]{1,0:T(8,128)(2,1)}, bf16[128,256]{1,0:T(8,128)(2,1)S(1)}, u32[]{:S(2)}, u32[]{:S(2)}) collective-permute-start(bf16[128,256]{1,0:T(8,128)(2,1)} %get-tuple-element.53), channel_id=1, source_target_pairs={{0,8},{4,12},{8,0},{12,4},{16,24},{20,28},{24,16},{28,20},{1,9},{5... | collective-permute-start | bytes 196616 | tf_op jit(solution)/shard_map/ppermute | solution.py:623
  203.1 16.9 %collective-permute-start.6 = (bf16[128,256]{1,0:T(8,128)(2,1)}, bf16[128,256]{1,0:T(8,128)(2,1)S(1)}, u32[]{:S(2)}, u32[]{:S(2)}) collective-permute-start(bf16[128,256]{1,0:T(8,128)(2,1)} %get-tuple-element.54), channel_id=1, source_target_pairs={{0,12},{4,0},{8,4},{12,8},{16,28},{20,16},{24,20},{28,24},{1,13},{... | collective-permute-start | bytes 196616 | tf_op jit(solution)/shard_map/ppermute | solution.py:623
  220.0 0.6 copy-start.6
  220.0 0.6 copy-start.7
  220.0 0.7 copy-start.8
Sparse Core Ops, SparseCore 0:
  9.6 19.4 all-gather.1
  190.9 30.9 reduce-scatter.1

commit v8 on v7

--- a/solution.py
+++ b/solution.py
@@ -11,6 +11,7 @@
 PLEN = 256
 INNER = 4
 GROUP = 8
+SIZES = (6, 7)
 LANES = 128
 NEG_LARGE = -1e30
 SCALE = HEAD_DIM ** (-0.5)
@@ -111,12 +112,20 @@
 def each_group(pick_ref, live_ref, ident, entries, start):
     live = live_ref[ident]
 
-    def group(step, carry):
-        first = step * GROUP
-        slots = [pick_ref[ident, first + j] for j in range(GROUP)]
-        return entries(carry, slots, [first + j < live for j in range(GROUP)])
-
-    return lax.fori_loop(0, lax.div(live + (GROUP - 1), GROUP), group, start)
+    def group(first, size, carry):
+        slots = [pick_ref[ident, first + j] for j in range(size)]
+        return entries(carry, slots, [first + j < live for j in range(size)])
+
+    def in_groups():
+        steps = lax.div(live + (GROUP - 1), GROUP)
+        return lax.fori_loop(0, steps, lambda step, carry: group(step * GROUP, GROUP, carry), start)
+
+    def by_size(sizes):
+        if not sizes:
+            return in_groups()
+        return lax.cond(live <= sizes[0], lambda: group(0, sizes[0], start), lambda: by_size(sizes[1:]))
+
+    return by_size(SIZES)
 
 
 def pair_lanes(pair):
@@ -132,7 +141,7 @@
 
 
 def shifted(scores, lives, top):
-    keys = scores.shape[0] // GROUP
+    keys = scores.shape[0] // len(lives)
     return [
         jnp.exp(scores[j * keys : (j + 1) * keys] - jnp.where(live, top, -NEG_LARGE))
         for j, live in enumerate(lives)

time: 235 us -> 233 us (level)
  waiting for transfers between devices: 35.6 us -> 39 us
  Pallas kernels: 134 us -> 131 us
    all_to_all x4, waiting for transfers between devices: 2.88 us -> 7.11 us  [swap(): lax.all_to_all(x, 'pas', split_axis=0, concat_axis=0, tiled=True, axis_in...]
    pallas_call x9, Pallas kernels: 81.6 us -> 77.7 us  [vmem_call(): pl.pallas_call(kernel, in_specs=[smem] * len(scalars) + [vmem] * len(arra...]
  transfers between devices with their start and end apart: 15 -> 15, of which waited for: 8 -> 8; matrix products, arithmetic and copies ran while one was open for 0% -> 0% of each run, Pallas kernels for 56% -> 55%
where the time goes in v8:
time: 233 us; the launch traced here: 231 us
  Pallas kernels  131 us (56%)
  waiting for transfers between devices  39 us (17%)
  starting transfers between devices  38.8 us (17%)
  between operations  14.1 us (6%)
  local copies, waits for them, and re-layouts  6.95 us (3%)
    pallas_call x9, Pallas kernels, vmem_call(): pl.pallas_call(kernel, in_specs=[smem] * len(scalars) + [vmem] * len(arra...  77.7 us
    pallas_call x2, Pallas kernels, project(): pl.pallas_call(project_kernel, grid=(rows // tile,), in_specs=[pl.BlockSp...  28.7 us
    all_to_all x4, starting transfers between devices, swap(): lax.all_to_all(x, 'pas', split_axis=0, concat_axis=0, tiled=True, axis_in...  16.9 us
    ppermute x3, waiting for transfers between devices, body(): lax.ppermute(query_blocks[r], 'pas', [(o * inner + i, o * inner + (i + r)...  15.9 us
    ppermute x4, waiting for transfers between devices, to_outer(): lax.ppermute(x, 'pas', [(o * inner + i, (o + r) % n_outer * inner + i) fo...  13.4 us
    all_to_all x2, starting transfers between devices, swap_all(): return lax.all_to_all(x, 'pas', split_axis=0, concat_axis=0, tiled=True)  13.3 us
    all_to_all x4, waiting for transfers between devices, swap(): lax.all_to_all(x, 'pas', split_axis=0, concat_axis=0, tiled=True, axis_in...  7.11 us
    unnamed x22, local copies, waits for them, and re-layouts  6.95 us
  transfers between devices with their start and end apart: 15, of which 8 were waited for; matrix products, arithmetic and copies ran while one was open for 0% of the time, Pallas kernels for 55%

profile of v8, /device:TPU:0, one launch (start us, length us, event | category | flops | bytes accessed | tf_op | source)
XLA Modules:
  0.0 231.2 jit_solution(17768664222133262578)
XLA Ops:
  7.2 0.7 all-gather.2.cloned.1.call-update
  7.9 1.8 spread.1
  9.7 7.3 %all-to-all-start.2 = ((bf16[8,128,256]{2,1,0:T(8,128)(2,1)}), bf16[8,128,256]{2,1,0:T(8,128)(2,1)S(1)}, u32[]{:S(2)}, u32[]{:S(2)}) async-start(bf16[8,128,256]{2,1,0:T(8,128)(2,1)} %spread.1), calls=%async_computation.2 | async-start | bytes 1048576 | tf_op jit(solution)/shard_map/all_to_all | solution.py:519
  17.0 14.6 %project.2 = bf16[4,1024,256]{2,1,0:T(8,128)(2,1)} custom-call(bf16[1024,4096]{1,0:T(8,128)(2,1)} %x_ref.3, bf16[4096,1024]{1,0:T(8,128)(2,1)} %w_ref.4), custom_call_target="tpu_custom_call" | custom-call | flops 14000000000 | tf_op jit(solution)/shard_map/project/pallas_call | solution.py:56
  31.5 0.8 copy-done.2
  32.3 4.2 %all-to-all-start = ((bf16[4,1024,256]{2,1,0:T(8,128)(2,1)}), bf16[4,1024,256]{2,1,0:T(8,128)(2,1)S(1)}, u32[]{:S(2)}, u32[]{:S(2)}) async-start(bf16[4,1024,256]{2,1,0:T(8,128)(2,1)} %project.2), calls=%async_computation | async-start | bytes 4194304 | tf_op jit(solution)/shard_map/all_to_all | solution.py:514
  36.5 14.2 %project.3 = bf16[4,1024,256]{2,1,0:T(8,128)(2,1)} custom-call(bf16[1024,4096]{1,0:T(8,128)(2,1)} %x_ref.3, bf16[4096,1024]{1,0:T(8,128)(2,1)} %w_ref.5), custom_call_target="tpu_custom_call" | custom-call | flops 14000000000 | tf_op jit(solution)/shard_map/project/pallas_call | solution.py:56
  50.7 2.3 route.1
  52.9 6.8 %context_grad.1 = bf16[2,4,128,256]{3,2,1,0:T(8,128)(2,1)} custom-call(bf16[128,4096]{1,0:T(8,128)(2,1)} %all-gather.2.cloned.1.call-done.x_ref, bf16[1024,4096]{1,0:T(8,128)(2,1)} %w_ref.7), custom_call_target="tpu_custom_call" | custom-call | flops 5000000000 | tf_op jit(solution)/shard_map/context_grad/pallas_call | solution.py:386
  59.7 1.1 all-to-all-done
  60.8 1.3 copy-done.1
  62.1 4.4 %all-to-all-start.1 = ((bf16[4,1024,256]{2,1,0:T(8,128)(2,1)}), bf16[4,1024,256]{2,1,0:T(8,128)(2,1)}, u32[]{:S(2)}, u32[]{:S(2)}) async-start(bf16[4,1024,256]{2,1,0:T(8,128)(2,1)} %project.3), calls=%async_computation.1 | async-start | bytes 4194304 | tf_op jit(solution)/shard_map/all_to_all | solution.py:514
  66.6 12.7 %stats.1.refs_0_ = f32[2,8,2,256]{3,2,1,0:T(2,128)} custom-call(s32[8,24]{1,0:T(8,128)} %get-tuple-element.33.pick_ref, s32[8]{0:T(128)} %get-tuple-element.34.live_ref, bf16[16,256,256]{2,1,0:T(8,128)(2,1)} %bitcast.6, bf16[8,128,256]{2,1,0:T(8,128)(2,1)} %copy-done.2), custom_call_target="tpu_custom_call" | custom-call | flops 12999999488 | tf_op jit(solution)/shard_map/stats/pallas_call | solution.py:456
  79.3 2.1 collective-permute-start
  81.4 8.1 %collective-permute-done.refs_1_ = f32[2,8,2,256]{3,2,1,0:T(2,128)S(1)} collective-permute-done((f32[2,8,2,256]{3,2,1,0:T(2,128)}, f32[2,8,2,256]{3,2,1,0:T(2,128)S(1)}, u32[]{:S(2)}, u32[]{:S(2)}) %collective-permute-start) | collective-permute-done | bytes 32800 | tf_op jit(solution)/shard_map/ppermute | solution.py:522
  89.5 0.6 copy-done.9
  90.1 1.4 merge.1.st_ref.refs_2_
  91.5 0.8 all-to-all-done.1
  92.3 6.0 %all-to-all-start.3 = ((bf16[8,128,256]{2,1,0:T(8,128)(2,1)}), bf16[8,128,256]{2,1,0:T(8,128)(2,1)S(1)}, u32[]{:S(2)}, u32[]{:S(2)}) async-start(bf16[8,128,256]{2,1,0:T(8,128)(2,1)} %bitcast.2), calls=%async_computation.3 | async-start | bytes 1048576 | tf_op jit(solution)/shard_map/all_to_all | solution.py:519
  98.3 11.1 %context.2 = f32[4,256,128]{2,1,0:T(8,128)} custom-call(s32[8,24]{1,0:T(8,128)} %get-tuple-element.33.pick_ref, s32[8]{0:T(128)} %get-tuple-element.34.live_ref, s32[1]{0:T(128)} %bitcast.outer_ref, bf16[16,256,256]{2,1,0:T(8,128)(2,1)} %bitcast.7, bf16[16,256,256]{2,1,0:T(8,128)(2,1)} %bitcast.3.v_ref, bf16[8,128,256]{2,1,0:T(8,128)(2,1)} %copy-done.2, ...), custom_call_target="tpu_custom_call" | custom-call | flops 14000000000 | tf_op jit(solution)/shard_map/context/pallas_call | solution.py:456
  109.4 1.9 all-to-all-done.3.g_ref.refs_3_
  111.3 0.8 collective-permute-start.1
  112.1 10.5 %context.3.refs_0_ = f32[4,256,128]{2,1,0:T(8,128)} custom-call(s32[8,24]{1,0:T(8,128)} %get-tuple-element.33.pick_ref, s32[8]{0:T(128)} %get-tuple-element.34.live_ref, s32[1]{0:T(128)} %bitcast.outer_ref, bf16[16,256,256]{2,1,0:T(8,128)(2,1)} %bitcast.8, bf16[16,256,256]{2,1,0:T(8,128)(2,1)} %bitcast.3.v_ref, bf16[8,128,256]{2,1,0:T(8,128)(2,1)} %copy-done.2, ...), custom_call_target="tpu_custom_call" | custom-call | flops 5000000000 | tf_op jit(solution)/shard_map/context/pallas_call | solution.py:456
  122.6 14.5 %value_grad.1.refs_4_ = bf16[4,1152,256]{2,1,0:T(8,128)(2,1)} custom-call(s32[8,24]{1,0:T(8,128)} %get-tuple-element.33.pick_ref, s32[8]{0:T(128)} %get-tuple-element.34.live_ref, bf16[16,256,256]{2,1,0:T(8,128)(2,1)} %bitcast.9, bf16[8,128,256]{2,1,0:T(8,128)(2,1)} %copy-done.2, bf16[8,128,256]{2,1,0:T(8,128)(2,1)} %copy-done.3, ...), custom_call_target="tpu_custom_call" | custom-call | flops 5000000000 | tf_op jit(solution)/shard_map/value_grad/pallas_call | solution.py:456
  137.1 0.8 copy-done.5
  137.9 2.9 %combine_context.1 = (bf16[4,1152,256]{2,1,0:T(8,128)(2,1)}, f32[4,2,256]{2,1,0:T(2,128)}) custom-call(s32[1]{0:T(128)} %bitcast.outer_ref, f32[4,256,128]{2,1,0:T(8,128)} %context.3.refs_0_, f32[4,256,128]{2,1,0:T(8,128)} %copy-done.5, f32[3,8,2,256]{3,2,1,0:T(2,128)} %merge.1.st_ref.refs_2_, ...), custom_call_target="tpu_custom_call", output_to_operand_aliasing={{0}: (5, {})} | custom-call | flops 3000000000 | tf_op jit(solution)/shard_map/combine_context/pallas_call | solution.py:592
  140.8 1.6 collective-permute-start.2
  142.4 3.2 %collective-permute-done.2.rest_1_ = f32[4,2,256]{2,1,0:T(2,128)S(1)} collective-permute-done((f32[4,2,256]{2,1,0:T(2,128)}, f32[4,2,256]{2,1,0:T(2,128)S(1)}, u32[]{:S(2)}, u32[]{:S(2)}) %collective-permute-start.2) | collective-permute-done | bytes 8224 | tf_op jit(solution)/shard_map/ppermute | solution.py:522
  145.6 0.6 copy-done.10
  146.2 3.9 %all-to-all-start.4 = ((bf16[4,1152,256]{2,1,0:T(8,128)(2,1)}), bf16[4,1152,256]{2,1,0:T(8,128)(2,1)S(1)}, u32[]{:S(2)}, u32[]{:S(2)}) async-start(bf16[4,1152,256]{2,1,0:T(8,128)(2,1)} %get-tuple-element.44), calls=%async_computation.4 | async-start | bytes 4718592 | tf_op jit(solution)/shard_map/all_to_all | solution.py:514
  150.1 22.1 %score_grad.1 = (bf16[16,256,256]{2,1,0:T(8,128)(2,1)}, f32[4,256,128]{2,1,0:T(8,128)}, f32[4,256,128]{2,1,0:T(8,128)}) custom-call(s32[8,24]{1,0:T(8,128)} %get-tuple-element.33.pick_ref, s32[8]{0:T(128)} %get-tuple-element.34.live_ref, s32[1]{0:T(128)} %bitcast.outer_ref, bf16[16,256,256]{2,1,0:T(8,128)(2,1)} %bitcast.10, ...), custom_call_target="tpu_custom_call" | custom-call | flops 24999999488 | tf_op jit(solution)/shard_map/score_grad/pallas_call | solution.py:456
  172.1 0.8 collective-permute-start.3
  172.9 5.2 %all-to-all-done.4.x_ref = bf16[4,1152,256]{2,1,0:T(8,128)(2,1)S(1)} async-done(((bf16[4,1152,256]{2,1,0:T(8,128)(2,1)}), bf16[4,1152,256]{2,1,0:T(8,128)(2,1)S(1)}, u32[]{:S(2)}, u32[]{:S(2)}) %all-to-all-start.4) | async-done | bytes 2359328 | tf_op jit(solution)/shard_map/all_to_all | solution.py:514
  178.2 1.4 copy-done
  179.6 4.4 %all-to-all-start.5 = ((bf16[4,1024,256]{2,1,0:T(8,128)(2,1)}), bf16[4,1024,256]{2,1,0:T(8,128)(2,1)}, u32[]{:S(2)}, u32[]{:S(2)}) async-start(bf16[4,1024,256]{2,1,0:T(8,128)(2,1)} %bitcast.11), calls=%async_computation.6 | async-start | bytes 4194304 | tf_op jit(solution)/shard_map/all_to_all | solution.py:514
  184.0 0.0 reduce-scatter.2.cloned.1.call-start
  184.1 6.7 %out_project.1 = f32[128,4096]{1,0:T(8,128)} custom-call(bf16[4,1152,256]{2,1,0:T(8,128)(2,1)} %copy-done, bf16[1024,4096]{1,0:T(8,128)(2,1)} %w_ref.7), custom_call_target="tpu_custom_call" | custom-call | flops 1000000000 | tf_op jit(solution)/shard_map/out_project/pallas_call | solution.py:417
  190.8 2.7 %collect.2 = bf16[1024,1024]{1,0:T(8,128)(2,1)} custom-call(bf16[4,1152,256]{2,1,0:T(8,128)(2,1)} %copy-done), custom_call_target="tpu_custom_call" | custom-call | flops 1000000000 | tf_op jit(solution)/shard_map/collect/pallas_call | solution.py:441
  193.5 2.1 collective-permute-done.3.refs_1_
  195.6 0.8 copy-done.4
  196.4 2.0 combine_query.1
  198.4 1.8 collective-permute-start.4
  200.2 1.5 collective-permute-start.6
  201.7 15.9 %collective-permute-done.4.refs_1_ = bf16[128,256]{1,0:T(8,128)(2,1)S(1)} collective-permute-done((bf16[128,256]{1,0:T(8,128)(2,1)}, bf16[128,256]{1,0:T(8,128)(2,1)S(1)}, u32[]{:S(2)}, u32[]{:S(2)}) %collective-permute-start.4) | collective-permute-done | bytes 65568 | tf_op jit(solution)/shard_map/ppermute | solution.py:632
  217.6 0.6 copy-done.6
  218.2 1.7 gather_query.1
  219.9 2.7 %collect.3 = bf16[1024,1024]{1,0:T(8,128)(2,1)} custom-call(bf16[4,1024,256]{2,1,0:T(8,128)(2,1)} %all-to-all-done.5.x_ref), custom_call_target="tpu_custom_call" | custom-call | flops 1000000000 | tf_op jit(solution)/shard_map/collect/pallas_call | solution.py:441
  222.6 1.8 convert_element_type.3
  (24 shorter events, 0.1 us)
Async XLA Ops:
  7.2 29.3 %all-gather.2.cloned.1.call-start = ((), (), s32[]{:S(2)}) async-start(), calls=%async_computation.7 | async-start | bytes 1310720 | tf_op jit(solution)/shard_map/all_gather | solution.py:533
  9.7 21.8 %all-to-all-start.2 = ((bf16[8,128,256]{2,1,0:T(8,128)(2,1)}), bf16[8,128,256]{2,1,0:T(8,128)(2,1)S(1)}, u32[]{:S(2)}, u32[]{:S(2)}) async-start(bf16[8,128,256]{2,1,0:T(8,128)(2,1)} %spread.1), calls=%async_computation.2 | async-start | bytes 1048576 | tf_op jit(solution)/shard_map/all_to_all | solution.py:519
  31.5 0.8 copy-start.2
  32.3 28.5 %all-to-all-start = ((bf16[4,1024,256]{2,1,0:T(8,128)(2,1)}), bf16[4,1024,256]{2,1,0:T(8,128)(2,1)S(1)}, u32[]{:S(2)}, u32[]{:S(2)}) async-start(bf16[4,1024,256]{2,1,0:T(8,128)(2,1)} %project.2), calls=%async_computation | async-start | bytes 4194304 | tf_op jit(solution)/shard_map/all_to_all | solution.py:514
  60.8 1.3 copy-start.1
  62.1 30.2 %all-to-all-start.1 = ((bf16[4,1024,256]{2,1,0:T(8,128)(2,1)}), bf16[4,1024,256]{2,1,0:T(8,128)(2,1)}, u32[]{:S(2)}, u32[]{:S(2)}) async-start(bf16[4,1024,256]{2,1,0:T(8,128)(2,1)} %project.3), calls=%async_computation.1 | async-start | bytes 4194304 | tf_op jit(solution)/shard_map/all_to_all | solution.py:514
  79.3 10.2 %collective-permute-start = (f32[2,8,2,256]{3,2,1,0:T(2,128)}, f32[2,8,2,256]{3,2,1,0:T(2,128)S(1)}, u32[]{:S(2)}, u32[]{:S(2)}) collective-permute-start(f32[2,8,2,256]{3,2,1,0:T(2,128)} %stats.1.refs_0_), channel_id=1, source_target_pairs={{0,16},{4,20},{8,24},{12,28},{16,0},{20,4},{24,8},{28,12},{1,17},{... | collective-permute-start | bytes 98312 | tf_op jit(solution)/shard_map/ppermute | solution.py:522
  89.5 0.6 copy-start.9
  92.3 19.0 %all-to-all-start.3 = ((bf16[8,128,256]{2,1,0:T(8,128)(2,1)}), bf16[8,128,256]{2,1,0:T(8,128)(2,1)S(1)}, u32[]{:S(2)}, u32[]{:S(2)}) async-start(bf16[8,128,256]{2,1,0:T(8,128)(2,1)} %bitcast.2), calls=%async_computation.3 | async-start | bytes 1048576 | tf_op jit(solution)/shard_map/all_to_all | solution.py:519
  111.3 11.3 %copy-start.3 = (bf16[8,128,256]{2,1,0:T(8,128)(2,1)}, bf16[8,128,256]{2,1,0:T(8,128)(2,1)S(1)}, u32[]{:S(2)}) copy-start(bf16[8,128,256]{2,1,0:T(8,128)(2,1)S(1)} %all-to-all-done.3.g_ref.refs_3_) | copy-start | bytes 1572868
  111.3 25.7 %collective-permute-start.1 = (f32[4,256,128]{2,1,0:T(8,128)}, f32[4,256,128]{2,1,0:T(8,128)S(1)}, u32[]{:S(2)}, u32[]{:S(2)}) collective-permute-start(f32[4,256,128]{2,1,0:T(8,128)} %context.2), channel_id=1, source_target_pairs={{0,16},{4,20},{8,24},{12,28},{16,0},{20,4},{24,8},{28,12},{1,17},{... | collective-permute-start | bytes 1572872 | tf_op jit(solution)/shard_map/ppermute | solution.py:522
  137.1 0.8 copy-start.5
  140.8 4.8 %collective-permute-start.2 = (f32[4,2,256]{2,1,0:T(2,128)}, f32[4,2,256]{2,1,0:T(2,128)S(1)}, u32[]{:S(2)}, u32[]{:S(2)}) collective-permute-start(f32[4,2,256]{2,1,0:T(2,128)} %get-tuple-element.43.rest_0_), channel_id=1, source_target_pairs={{0,16},{4,20},{8,24},{12,28},{16,0},{20,4},{24,8},{28,12},{1,17},{... | collective-permute-start | bytes 24584 | tf_op jit(solution)/shard_map/ppermute | solution.py:522
  145.6 0.6 copy-start.10
  146.2 31.9 %all-to-all-start.4 = ((bf16[4,1152,256]{2,1,0:T(8,128)(2,1)}), bf16[4,1152,256]{2,1,0:T(8,128)(2,1)S(1)}, u32[]{:S(2)}, u32[]{:S(2)}) async-start(bf16[4,1152,256]{2,1,0:T(8,128)(2,1)} %get-tuple-element.44), calls=%async_computation.4 | async-start | bytes 4718592 | tf_op jit(solution)/shard_map/all_to_all | solution.py:514
  172.1 23.5 %collective-permute-start.3 = (f32[4,256,128]{2,1,0:T(8,128)}, f32[4,256,128]{2,1,0:T(8,128)S(1)}, u32[]{:S(2)}, u32[]{:S(2)}) collective-permute-start(f32[4,256,128]{2,1,0:T(8,128)} %get-tuple-element.50), channel_id=1, source_target_pairs={{0,16},{4,20},{8,24},{12,28},{16,0},{20,4},{24,8},{28,12},{1,17},{... | collective-permute-start | bytes 1572872 | tf_op jit(solution)/shard_map/ppermute | solution.py:522
  178.2 1.4 copy-start
  179.6 40.3 %all-to-all-start.5 = ((bf16[4,1024,256]{2,1,0:T(8,128)(2,1)}), bf16[4,1024,256]{2,1,0:T(8,128)(2,1)}, u32[]{:S(2)}, u32[]{:S(2)}) async-start(bf16[4,1024,256]{2,1,0:T(8,128)(2,1)} %bitcast.11), calls=%async_computation.6 | async-start | bytes 4194304 | tf_op jit(solution)/shard_map/all_to_all | solution.py:514
  184.0 38.6 %reduce-scatter.2.cloned.1.call-start = ((), (), s32[]{:S(2)}) async-start(), calls=%async_computation.8 | async-start | bytes 2621440 | tf_op jit(solution)/shard_map/reduce_scatter | solution.py:619
  195.6 0.8 copy-start.4
  198.4 19.1 %collective-permute-start.4 = (bf16[128,256]{1,0:T(8,128)(2,1)}, bf16[128,256]{1,0:T(8,128)(2,1)S(1)}, u32[]{:S(2)}, u32[]{:S(2)}) collective-permute-start(bf16[128,256]{1,0:T(8,128)(2,1)} %get-tuple-element.52), channel_id=1, source_target_pairs={{0,4},{4,8},{8,12},{12,0},{16,20},{20,24},{24,28},{28,16},{1,5},{5... | collective-permute-start | bytes 196616 | tf_op jit(solution)/shard_map/ppermute | solution.py:632
  200.2 17.4 %collective-permute-start.5 = (bf16[128,256]{1,0:T(8,128)(2,1)}, bf16[128,256]{1,0:T(8,128)(2,1)S(1)}, u32[]{:S(2)}, u32[]{:S(2)}) collective-permute-start(bf16[128,256]{1,0:T(8,128)(2,1)} %get-tuple-element.53), channel_id=1, source_target_pairs={{0,8},{4,12},{8,0},{12,4},{16,24},{20,28},{24,16},{28,20},{1,9},{5... | collective-permute-start | bytes 196616 | tf_op jit(solution)/shard_map/ppermute | solution.py:632
  200.2 17.4 %collective-permute-start.6 = (bf16[128,256]{1,0:T(8,128)(2,1)}, bf16[128,256]{1,0:T(8,128)(2,1)S(1)}, u32[]{:S(2)}, u32[]{:S(2)}) collective-permute-start(bf16[128,256]{1,0:T(8,128)(2,1)} %get-tuple-element.54), channel_id=1, source_target_pairs={{0,12},{4,0},{8,4},{12,8},{16,28},{20,16},{24,20},{28,24},{1,13},{... | collective-permute-start | bytes 196616 | tf_op jit(solution)/shard_map/ppermute | solution.py:632
  217.6 0.6 copy-start.6
  217.6 0.6 copy-start.7
  217.6 0.7 copy-start.8
Sparse Core Ops, SparseCore 0:
  9.6 19.4 all-gather.1
  190.9 30.9 reduce-scatter.1
